TPU v7x, 32 devices: a whole 2x2x4 slice. The times are simulated.
32 devices in a mesh: band: 8 (over z, x), mem: 4 (over y, core).
Axes of the slice: x: 2, y: 2, z: 4, core: 2. Of those that a mesh axis runs over, the one named last changes fastest.
Arguments:
- coef: float32 [2, 512, 128, 2, 512], P(None, 'band', 'mem'), may hold values from -6 to 6
- perturb: bfloat16 [768, 128, 2, 1536], P('band', 'mem'), may hold values from -6 to 6
- weight: float32 [768, 2, 1536], P('band'), may hold values from 1 to 10
- table: bfloat16 [512, 512, 768], P('band'), may hold values from -0.0078125 to 0.0078125
- wave_map: int32 [512], replicated, may hold values from 0 to 511, each once
- lat_map: int32 [768], replicated, may hold values from 0 to 767, each once
Outputs:
- increment: float32 [768, 2, 1536], P('band')
- product: float32 [2, 512, 128, 2, 512], P(None, 'band', 'mem')
Inputs may be any that keep to these rules, and one draw needn't show every extreme that they name: A permutation: spectral row r holds zonal wavenumber wave_map[r]. A permutation: grid row s holds Gaussian latitude lat_map[s]; the last dimension of table stands in natural latitude order.
All inputs are finite; a program needn't handle non-finite values.
Results may differ from a plain program's by a relative error of at most 0.0048.
Values may be sent and summed in bfloat16 or wider, within the bound.
No kernel may reach another device: no remote copies, remote signals or barrier semaphores. Data moves between devices by JAX's collectives and lax.ppermute only.
A program may use at most 320 MiB of HBM per device.

v0:
```python
import math

import jax
import jax.numpy as jnp
from jax import lax
from jax.sharding import PartitionSpec as P


def body(coef, perturb, weight, table, wave_map, lat_map):
    parts, wave_rows, local_members, vertical_levels, nwave = coef.shape
    lat_rows = perturb.shape[0]
    lon = perturb.shape[3]
    batch = local_members * vertical_levels
    ensemble_members = local_members * lax.axis_size("mem")
    scale = 1.0 / math.sqrt(ensemble_members - 1)
    start = lax.axis_index("band") * wave_rows
    own_waves = lax.dynamic_slice_in_dim(wave_map, start, wave_rows)
    start_offsets = jnp.arange(nwave, dtype=jnp.int32)
    valid = (start_offsets[None, :] < (nwave - own_waves)[:, None]).astype(jnp.float32)
    loc_table = (jnp.take(table, lat_map, axis=2).astype(jnp.float32) * valid[:, :, None]).astype(
        jnp.bfloat16
    )
    columns = jnp.arange(lon, dtype=jnp.int32)
    phase = wave_map[:, None] * columns[None, :] % lon
    angle = phase.astype(jnp.float32) * (2.0 * math.pi / lon)
    scale_multiplier = jnp.where(wave_map == 0, 1.0, 2.0).astype(jnp.float32)[:, None]
    fourier_table = jnp.stack(
        [scale_multiplier * jnp.cos(angle), -scale_multiplier * jnp.sin(angle)], axis=0
    ).astype(jnp.bfloat16)
    masked = coef * valid[None, :, None, None, :]
    spec = masked.astype(jnp.bfloat16).reshape(parts, wave_rows, batch, nwave)
    fields = jnp.stack(
        [
            jnp.einsum("mjl,mqj->mlq", loc_table, spec[part], preferred_element_type=jnp.float32)
            for part in range(2)
        ],
        axis=0,
    )
    fields = fields.astype(jnp.bfloat16)
    received_parts = lax.all_to_all(fields, "band", split_axis=2, concat_axis=1, tiled=True)
    grand_total = jnp.einsum(
        "cke,cg->keg", received_parts[0], fourier_table[0], preferred_element_type=jnp.float32
    )
    grid = grand_total + jnp.einsum(
        "cke,cg->keg", received_parts[1], fourier_table[1], preferred_element_type=jnp.float32
    )
    grid = grid.reshape(lat_rows, local_members, vertical_levels, lon)
    partial_value = jnp.sum(perturb.astype(jnp.float32) * grid, axis=1) * scale
    increment = lax.psum(partial_value, "mem")
    gradient = weight * increment
    adjoint_grid = (perturb.astype(jnp.float32) * gradient[:, None] * scale).astype(jnp.bfloat16)
    adjoint_grid = adjoint_grid.reshape(lat_rows, batch, lon)
    adjoint_fields = jnp.einsum(
        "crx,sqx->crsq", fourier_table, adjoint_grid, preferred_element_type=jnp.float32
    )
    adjoint_fields = adjoint_fields.astype(jnp.bfloat16)
    returned = lax.all_to_all(adjoint_fields, "band", split_axis=1, concat_axis=2, tiled=True)
    back = jnp.stack(
        [
            jnp.einsum(
                "msq,mjs->mqj", returned[part], loc_table, preferred_element_type=jnp.float32
            )
            for part in range(2)
        ],
        axis=0,
    )
    product = masked + back.reshape(parts, wave_rows, local_members, vertical_levels, nwave)
    return (increment, product)


def solution(mesh):
    in_specs = (
        P(None, "band", "mem", None, None),
        P("band", "mem", None, None),
        P("band", None, None),
        P("band", None, None),
        P(),
        P(),
    )
    out_specs = (P("band", None, None), P(None, "band", "mem", None, None))
    return jax.shard_map(body, mesh=mesh, in_specs=in_specs, out_specs=out_specs, check_vma=False)
```

profile of v0, /device:TPU:8, one launch (start us, length us, event | category | flops | bytes accessed | tf_op | source)
XLA Modules:
  0.0 1523.4 jit_solution(15214544979070194078)
XLA Ops:
  7.2 0.7 compare_select_fusion
  7.9 0.7 compare_and_fusion
  8.6 0.8 dynamic-slice_subtract_fusion
  9.3 0.1 fusion.14
  9.4 0.0 copy-start.2
  9.4 63.6 %copy.25 = bf16[64,512,768]{1,0,2:T(8,128)(2,1)} copy(bf16[64,512,768]{2,1,0:T(8,128)(2,1)} %param.9) | data formatting | bytes 100663296 | tf_op args[3]
  73.0 33.6 %gather_fusion = bf16[768,64,512]{2,1,0:T(8,128)(2,1)} fusion(bf16[64,512,768]{1,0,2:T(8,128)(2,1)} %copy.25, s32[1024]{0:T(1024)S(1)} %pad_clamp_fusion), kind=kCustom, calls=%fused_computation | custom fusion | bytes 100666368 | tf_op jit(solution)/shard_map/jit(_take)/gather | solution.py:20
  106.6 33.4 %fusion = bf16[64,512,768]{1,0,2:T(8,128)(2,1)} fusion(f32[64,512]{1,0:T(8,128)S(1)} %fusion.14, bf16[768,64,512]{2,1,0:T(8,128)(2,1)} %gather_fusion, pred[768]{0:T(1024)(128)(4,1)S(1)} %compare_and_fusion), kind=kLoop, calls=%fused_computation.2 | loop fusion | flops 100663296 | bytes 100795136 | tf_op jit(solution)/shard_map/convert_element_type | solution.py:20
  140.0 62.4 %copy.26 = bf16[64,512,768]{2,1,0:T(8,128)(2,1)} copy(bf16[64,512,768]{1,0,2:T(8,128)(2,1)} %fusion) | data formatting | bytes 100663296 | tf_op jit(solution)/shard_map/convert_element_type | solution.py:20
  202.4 0.0 copy-done.2
  202.4 8.7 multiply_convert_fusion.1
  211.1 7.3 fusion.25
  218.5 7.2 squeeze.24
  225.7 7.2 squeeze.25
  232.8 22.5 %convert_bitcast_fusion.1 = bf16[1,64,768,64]{2,3,1,0:T(8,128)(2,1)} fusion(bf16[64,64,512]{2,1,0:T(8,128)(2,1)} %squeeze.24, bf16[64,512,768]{2,1,0:T(8,128)(2,1)} %copy.26), kind=kOutput, calls=%fused_computation.14 | convolution fusion | flops 3224371200 | bytes 60817408 | tf_op jit(solution)/shard_map/mjl,mqj->mlq/dot_general | solution.py:34
  255.3 22.4 %convert_bitcast_fusion = bf16[1,64,768,64]{2,3,1,0:T(8,128)(2,1)} fusion(bf16[64,64,512]{2,1,0:T(8,128)(2,1)} %squeeze.25, bf16[64,512,768]{2,1,0:T(8,128)(2,1)} %copy.26), kind=kOutput, calls=%fused_computation.13 | convolution fusion | flops 3224371200 | bytes 60817408 | tf_op jit(solution)/shard_map/mjl,mqj->mlq/dot_general | solution.py:34
  277.8 10.5 pad_maximum_fusion
  288.3 35.0 %copy.28 = bf16[2,64,768,64]{3,1,0,2:T(8,128)(2,1)} copy(bf16[2,64,768,64]{2,3,1,0:T(8,128)(2,1)} %pad_maximum_fusion) | data formatting | bytes 25165824 | tf_op jit(solution)/shard_map/stack | solution.py:32
  323.3 23.1 %reshape.209 = bf16[8,2,393216]{2,1,0:T(2,128)(2,1)} reshape(bf16[768,2,64,64]{3,2,1,0:T(8,128)(2,1)} %bitcast.50) | data formatting | bytes 25165824
  346.4 0.0 copy-start.4
  346.4 6.4 all-to-all-start
  352.7 0.0 all-reduce.2.cloned.1.call-start
  352.8 0.0 copy-done.4
  352.8 270.5 %all-to-all-done = bf16[8,2,393216]{2,1,0:T(2,128)(2,1)} async-done(((bf16[8,2,393216]{2,1,0:T(2,128)(2,1)}), bf16[8,2,393216]{2,1,0:T(2,128)(2,1)}, u32[]{:S(2)}, u32[]{:S(2)}) %all-to-all-start) | async-done | bytes 12582944 | tf_op jit(solution)/shard_map/all_to_all | solution.py:40
  623.2 22.5 %reshape.210 = bf16[768,2,64,64]{3,2,1,0:T(8,128)(2,1)} reshape(bf16[8,2,393216]{2,1,0:T(2,128)(2,1)} %all-to-all-done) | data formatting | bytes 25165824
  645.7 36.0 %copy.29 = bf16[2,64,8,96,64]{3,4,1,2,0:T(8,128)(2,1)} copy(bf16[2,64,8,96,64]{4,1,0,3,2:T(8,128)(2,1)} %bitcast.51) | data formatting | bytes 25165824 | tf_op jit(solution)/shard_map/all_to_all | solution.py:40
  681.7 12.7 fusion.24
  694.4 12.9 copy.30
  707.3 13.0 copy.31
  720.2 0.0 copy-start
  720.2 25.3 %fusion.12 = f32[96,64,1536]{2,1,0:T(8,128)} fusion(bf16[512,96,64]{0,2,1:T(8,128)(2,1)} %copy.30, s32[512]{0:T(512)S(1)} %copy-done.4, f32[512]{0:T(512)S(1)} %get-tuple-element.11), kind=kOutput, calls=%fused_computation.28 | convolution fusion | flops 9672327168 | bytes 44044288 | tf_op jit(solution)/shard_map/cke,cg->keg/dot_general | solution.py:41
  745.6 0.0 copy-done
  745.6 32.6 %convolution_add_fusion = f32[96,64,1536]{2,1,0:T(8,128)} fusion(f32[96,64,1536]{2,1,0:T(8,128)} %fusion.12, bf16[512,96,64]{0,2,1:T(8,128)(2,1)S(1)} %copy-done, f32[512]{0:T(512)S(1)} %get-tuple-element.10, s32[512]{0:T(512)S(1)} %copy-done.4), kind=kOutput, calls=%fused_computation.11 | convolution fusion | flops 9681764352 | bytes 81793024 | tf_op jit(solution)/shard_map/cke,cg->keg/dot_general | solution.py:44
  778.2 42.9 %reshape.194 = f32[96,32,2,1536]{3,2,1,0:T(2,128)} reshape(f32[96,64,1536]{2,1,0:T(8,128)} %convolution_add_fusion) | data formatting | bytes 75497472 | tf_op jit(solution)/shard_map/reshape | solution.py:47
  821.1 22.7 %fusion.1 = f32[96,2,1536]{2,1,0:T(2,128)S(1)} fusion(f32[96,32,2,1536]{3,2,1,0:T(2,128)} %reshape.194, bf16[96,32,2,1536]{3,2,1,0:T(2,128)(2,1)} %param.7), kind=kLoop, calls=%fused_computation.5 | loop fusion | flops 28016640 | bytes 57802752 | tf_op jit(solution)/shard_map/reduce_sum | solution.py:48
  843.8 1.6 broadcast_multiply_fusion
  845.4 0.0 all-reduce.2.cloned.1.call-update
  845.4 13.8 multiply_convert_fusion.3
  859.3 24.7 %all-reduce.2.cloned.1.call-done = f32[96,2,1536]{2,1,0:T(2,128)} async-done(((f32[96,2,1536]{2,1,0:T(2,128)}), f32[96,2,1536]{2,1,0:T(2,128)}) %all-reduce.2.cloned.1.call-update) | async-done | bytes 1179664 | tf_op jit(solution)/shard_map/psum | solution.py:49
  884.0 2.2 mul.133
  886.2 22.0 %fusion.3 = bf16[96,32,2,1536]{3,2,1,0:T(2,128)(2,1)S(1)} fusion(bf16[96,32,2,1536]{3,2,1,0:T(2,128)(2,1)} %param.7, f32[96,2,1536]{2,1,0:T(2,128)S(1)} %mul.133), kind=kLoop, calls=%fused_computation.7 | loop fusion | flops 37748736 | bytes 38928384 | tf_op jit(solution)/shard_map/convert_element_type | solution.py:51
  908.3 17.4 %copy.40 = bf16[96,32,2,1536]{3,0,2,1:T(8,128)(2,1)} copy(bf16[96,32,2,1536]{3,2,1,0:T(2,128)(2,1)S(1)} %fusion.3) | data formatting | bytes 37748736 | tf_op jit(solution)/shard_map/reshape | solution.py:52
  925.7 25.0 %convolution_convert_fusion = bf16[2,512,96,64]{1,2,3,0:T(8,128)(2,1)} fusion(bf16[96,64,1536,1]{2,0,1,3:T(8,128)(2,1)} %bitcast.56, bf16[1,512,1536]{2,1,0:T(8,128)(2,1)S(1)} %get-tuple-element.9, bf16[1,512,1536]{2,1,0:T(8,128)(2,1)S(1)} %get-tuple-element.8), kind=kOutput, calls=%fused_computation.12 | convolution fusion | flops 19339935744 | bytes 34603008 | tf_op jit(solution)/shard_map/crx,sqx->crsq/dot_general | solution.py:53
  950.7 21.7 %copy.33 = bf16[2,512,96,64]{2,3,0,1:T(8,128)(2,1)} copy(bf16[2,512,96,64]{1,2,3,0:T(8,128)(2,1)} %convolution_convert_fusion) | data formatting | bytes 25165824 | tf_op jit(solution)/shard_map/convert_element_type | solution.py:56
  972.4 367.8 %all_to_all.30 = bf16[2,512,96,64]{2,3,0,1:T(8,128)(2,1)S(1)} all-to-all(bf16[2,512,96,64]{2,3,0,1:T(8,128)(2,1)} %copy.33), channel_id=1, replica_groups=mesh['band'=8,'mem'=4] {'band'}, dimensions={1} | all-to-all | bytes 25165824 | tf_op jit(solution)/shard_map/all_to_all | solution.py:57
  1340.2 2.2 copy.34
  1342.4 7.8 fusion.23
  1350.1 23.6 %copy.35 = bf16[1,64,8,96,64]{3,2,4,1,0:T(8,128)(2,1)} copy(bf16[1,64,8,96,64]{3,4,1,2,0:T(8,128)(2,1)} %get-tuple-element.2) | data formatting | bytes 12582912 | tf_op jit(solution)/shard_map/slice | solution.py:61
  1373.7 13.7 squeeze.30
  1387.4 25.6 %fusion.26 = f32[64,64,512]{2,1,0:T(8,128)} fusion(bf16[64,768,64]{1,2,0:T(8,128)(2,1)} %squeeze.30, bf16[64,512,768]{2,1,0:T(8,128)(2,1)} %copy.26), kind=kOutput, calls=%fused_computation.49 | convolution fusion | flops 3221225472 | bytes 65011712 | tf_op jit(solution)/shard_map/msq,mjs->mqj/dot_general | solution.py:60
  1413.0 10.8 stack.31
  1423.8 23.8 %copy.37 = bf16[1,64,8,96,64]{3,2,4,1,0:T(8,128)(2,1)} copy(bf16[1,64,8,96,64]{3,4,1,2,0:T(8,128)(2,1)} %get-tuple-element.3) | data formatting | bytes 12582912 | tf_op jit(solution)/shard_map/slice | solution.py:61
  1447.6 13.7 squeeze.31
  1461.3 25.6 %fusion.27 = f32[64,64,512]{2,1,0:T(8,128)} fusion(bf16[64,768,64]{1,2,0:T(8,128)(2,1)} %squeeze.31, bf16[64,512,768]{2,1,0:T(8,128)(2,1)} %copy.26), kind=kOutput, calls=%fused_computation.50 | convolution fusion | flops 3221225472 | bytes 65011712 | tf_op jit(solution)/shard_map/msq,mjs->mqj/dot_general | solution.py:60
  1486.9 0.0 copy-start.3
  1486.9 10.6 stack.32
  1497.5 0.0 copy-done.3
  1497.5 0.0 copy-start.1
  1497.5 17.5 %maximum_add_fusion = f32[2,64,32,2,512]{4,3,2,1,0:T(2,128)} fusion(f32[1,64,32,2,512]{4,3,2,1,0:T(2,128)} %stack.32, f32[1,64,32,2,512]{4,3,2,1,0:T(2,128)} %stack.31, f32[2,64,32,2,512]{4,3,2,1,0:T(2,128)} %param.6, f32[64,512]{1,0:T(8,128)S(1)} %copy-done.3), kind=kLoop, calls=%fused_computation.8 | loop fusion | flops 12582912 | bytes 50462720 | tf_op jit(solution)/shard_map/add | solution.py:67
  1515.0 0.0 copy-done.1
  1515.1 1.0 copy.42
  (2 shorter events, 0.0 us)
Async XLA Ops:
  9.4 193.0 %copy-start.2 = (f32[64,512]{1,0:T(8,128)}, f32[64,512]{1,0:T(8,128)S(1)}, u32[]{:S(2)}) copy-start(f32[64,512]{1,0:T(8,128)S(1)} %fusion.14) | copy-start | bytes 393220
  346.4 6.4 copy-start.4
  346.4 276.9 %all-to-all-start = ((bf16[8,2,393216]{2,1,0:T(2,128)(2,1)}), bf16[8,2,393216]{2,1,0:T(2,128)(2,1)}, u32[]{:S(2)}, u32[]{:S(2)}) async-start(bf16[8,2,393216]{2,1,0:T(2,128)(2,1)} %reshape.209), calls=%async_computation | async-start | bytes 25165824 | tf_op jit(solution)/shard_map/all_to_all | solution.py:40
  352.7 531.3 %all-reduce.2.cloned.1.call-start = ((), (), s32[]{:S(2)}) async-start(), calls=%async_computation.2 | async-start | bytes 2359296 | tf_op jit(solution)/shard_map/psum | solution.py:49
  720.2 25.3 %copy-start = (bf16[512,96,64]{0,2,1:T(8,128)(2,1)S(1)}, bf16[512,96,64]{0,2,1:T(8,128)(2,1)}, u32[]{:S(2)}) copy-start(bf16[512,96,64]{0,2,1:T(8,128)(2,1)} %copy.31) | copy-start | bytes 18874372
  1486.9 10.6 copy-start.3
  1497.5 17.5 %copy-start.1 = (f32[96,2,1536]{2,1,0:T(2,128)S(1)}, f32[96,2,1536]{2,1,0:T(2,128)}, u32[]{:S(2)}) copy-start(f32[96,2,1536]{2,1,0:T(2,128)} %all-reduce.2.cloned.1.call-done) | copy-start | bytes 3538948
Sparse Core Ops, SparseCore 0:
  845.6 38.3 all-reduce.1
where the time goes:
time: 1540 us; the launch traced here: 1520 us
  local copies, waits for them, and re-layouts  526 us (34%)
  blocking collectives  368 us (24%)
  waiting for transfers between devices  295 us (19%)
  matrix products  179 us (12%)
  other arithmetic  135 us (9%)
    all_to_all x1, blocking collectives, body(): lax.all_to_all(adjoint_fields, 'band', split_axis=1, concat_axis=2, tiled...  368 us
    all_to_all x1, waiting for transfers between devices, body(): lax.all_to_all(fields, 'band', split_axis=2, concat_axis=1, tiled=True)  270 us
    unnamed x14, local copies, waits for them, and re-layouts  110 us
    convert_element_type x1, local copies, waits for them, and re-layouts, body(): (jnp.take(table, lat_map, axis=2).astype(jnp.float32) * valid[:, :, None]...  62.4 us
    slice x3, local copies, waits for them, and re-layouts, body(): returned[part]  55.1 us
    dot_general x2, matrix products, body(): jnp.einsum('msq,mjs->mqj', returned[part], loc_table, preferred_element_t...  51.1 us
    dot_general x2, matrix products, body(): jnp.einsum('mjl,mqj->mlq', loc_table, spec[part], preferred_element_type=...  44.9 us
    reshape x1, local copies, waits for them, and re-layouts, body(): grid = grid.reshape(lat_rows, local_members, vertical_levels, lon)  42.9 us
  transfers between devices with their start and end apart: 2, of which 2 were waited for; matrix products, arithmetic and copies ran while one was open for 1% of the time, Pallas kernels for 0%

commit v1 on v0

v1 whole, which is shorter than its diff:
```python
import functools
import math

import jax
import jax.numpy as jnp
from jax import lax
from jax.experimental import pallas as pl
from jax.experimental.pallas import tpu as pltpu
from jax.sharding import PartitionSpec as P

F32 = jnp.float32
BF16 = jnp.bfloat16
VMEM_LIMIT = 56 * 2**20


def dot(a, b, ca, cb):
    return lax.dot_general(a, b, (((ca,), (cb,)), ((), ())), preferred_element_type=F32)


def divisor(n, most):
    return next(d for d in range(min(n, most), 0, -1) if n % d == 0)


def level_rows(ref, i):
    parts, _, _, levels, _ = ref.shape
    return jnp.concatenate(
        [ref[c, i, :, l, :] for c in range(parts) for l in range(levels)], axis=0
    )


def masked(full, wave):
    offset = lax.broadcasted_iota(jnp.int32, full.shape, 1)
    return jnp.where(offset < full.shape[1] - wave, full, 0.0)


def synth_kernel(first, rb, pair, waves, coef, table, spread, out, work):
    block, inner = pl.program_id(0), pl.program_id(1)
    ns = spread.shape[0]
    fields = []
    for i in range(pair):
        wave = waves[first + block * rb + inner * pair + i]
        spec = masked(level_rows(coef, i), wave).astype(BF16)
        fields.append(dot(spec, table[i], 1, 0).astype(BF16))
    lanes = fields[0].shape[0]
    placed = dot(spread[...], jnp.concatenate(fields, axis=0), 1, 1)
    for i in range(pair):
        work[pl.ds(inner * pair + i, ns, stride=rb), :] = placed[:, i * lanes : (i + 1) * lanes]

    @pl.when(inner == pl.num_programs(1) - 1)
    def _():
        out[...] = work[...].reshape(ns, rb, lanes).astype(BF16)


def synth(own_waves, coef, table, spread, first, count):
    parts, rows, members, levels, nwave = coef.shape
    lat = table.shape[2]
    ns = spread.shape[0]
    lanes = parts * members * levels
    rb = 16 if count % 16 == 0 else count
    pair = 2 if rb % 2 == 0 else 1
    inner = rb // pair
    base = first // pair
    return pl.pallas_call(
        functools.partial(synth_kernel, first, rb, pair),
        grid_spec=pltpu.PrefetchScalarGridSpec(
            num_scalar_prefetch=1,
            grid=(count // rb, inner),
            in_specs=[
                pl.BlockSpec(
                    (parts, pair, members, levels, nwave),
                    lambda b, i, w: (0, base + b * inner + i, 0, 0, 0),
                ),
                pl.BlockSpec((pair, nwave, lat), lambda b, i, w: (base + b * inner + i, 0, 0)),
                pl.BlockSpec((ns, lat), lambda b, i, w: (0, 0)),
            ],
            out_specs=pl.BlockSpec((ns, rb, lanes), lambda b, i, w: (0, b, 0)),
            scratch_shapes=[pltpu.VMEM((ns * rb, lanes), F32)],
        ),
        out_shape=jax.ShapeDtypeStruct((ns, count, lanes), BF16),
        compiler_params=pltpu.CompilerParams(vmem_limit_bytes=VMEM_LIMIT),
        cost_estimate=pl.CostEstimate(
            flops=2 * count * lanes * lat * (nwave + ns),
            bytes_accessed=count * (nwave * lat * 2 + lanes * nwave * 4 + lanes * ns * 2),
            transcendentals=0,
        ),
    )(own_waves, coef, table, spread)


def analyse_kernel(count, first, rb, pair, *refs):
    waves, parts_in, (coef, table, spread), (out, work) = (
        refs[0],
        refs[1 : 1 + count],
        refs[1 + count : 4 + count],
        refs[-2:],
    )
    block, inner = pl.program_id(0), pl.program_id(1)
    ns = spread.shape[0]
    parts, _, members, levels, _ = coef.shape
    lanes = work.shape[1]

    @pl.when(inner == 0)
    def _():
        at = 0
        for ref in parts_in:
            m, sq = ref.shape[0], ref.shape[1]
            size = m * sq * rb
            work[at : at + size, :] = ref[...].astype(F32).reshape(size, lanes)
            at += size

    rows = jnp.concatenate(
        [work[pl.ds(inner * pair + i, ns, stride=rb), :] for i in range(pair)], axis=1
    )
    rows = rows.T.astype(BF16)
    natural = dot(rows, spread[...], 1, 0).astype(BF16)
    for i in range(pair):
        wave = waves[first + block * rb + inner * pair + i]
        back = dot(natural[i * lanes : (i + 1) * lanes], table[i], 1, 1)
        total = masked(level_rows(coef, i) + back, wave)
        at = 0
        for c in range(parts):
            for l in range(levels):
                out[c, i, :, l, :] = total[at : at + members]
                at += members


def analyse(own_waves, received, coef, table, spread, first, count, product):
    parts, rows, members, levels, nwave = coef.shape
    lat = table.shape[2]
    ns = spread.shape[0]
    lanes = parts * members * levels
    rb = 16 if count % 16 == 0 else count
    pair = 2 if rb % 2 == 0 else 1
    inner = rb // pair
    base = first // pair
    n = len(received)
    into = [] if product is None else [product]
    return pl.pallas_call(
        functools.partial(analyse_kernel, n, first, rb, pair),
        grid_spec=pltpu.PrefetchScalarGridSpec(
            num_scalar_prefetch=1,
            grid=(count // rb, inner),
            in_specs=[
                pl.BlockSpec((r.shape[0], r.shape[1], rb, lanes), lambda b, i, w: (0, 0, b, 0))
                for r in received
            ]
            + [
                pl.BlockSpec(
                    (parts, pair, members, levels, nwave),
                    lambda b, i, w: (0, base + b * inner + i, 0, 0, 0),
                ),
                pl.BlockSpec((pair, nwave, lat), lambda b, i, w: (base + b * inner + i, 0, 0)),
                pl.BlockSpec((ns, lat), lambda b, i, w: (0, 0)),
            ]
            + [pl.BlockSpec(memory_space=pl.ANY)] * len(into),
            out_specs=pl.BlockSpec(
                (parts, pair, members, levels, nwave),
                lambda b, i, w: (0, base + b * inner + i, 0, 0, 0),
            ),
            scratch_shapes=[pltpu.VMEM((ns * rb, lanes), F32)],
        ),
        out_shape=jax.ShapeDtypeStruct(coef.shape, F32),
        input_output_aliases={n + 4: 0} if into else {},
        compiler_params=pltpu.CompilerParams(vmem_limit_bytes=VMEM_LIMIT),
        cost_estimate=pl.CostEstimate(
            flops=2 * count * lanes * lat * (nwave + ns),
            bytes_accessed=count * (nwave * lat * 2 + lanes * nwave * 8 + lanes * ns * 2),
            transcendentals=0,
        ),
    )(own_waves, *received, coef, table, spread, *into)


def grid_kernel(count, scale, *refs):
    pieces, (perturb, fourier), (out, left) = refs[:count], refs[count : count + 2], refs[count + 2 :]
    sb, levels, members, lon = perturb.shape
    lanes = pieces[0].shape[-1]
    half = lanes // 2
    waves = left.shape[1] // 2
    for s in range(sb):
        rows = [p[m, s] for p in pieces for m in range(p.shape[0])]
        turned = (jnp.concatenate(rows, axis=0) if len(rows) > 1 else rows[0]).T
        left[s * half : (s + 1) * half, :waves] = turned[:half]
        left[s * half : (s + 1) * half, waves:] = turned[half:]
    step = divisor(lon, 512)
    for x in range(0, lon, step):
        grid = dot(left[...], fourier[:, x : x + step], 1, 0)
        grid = grid.reshape(sb, levels, members, step) * perturb[:, :, :, x : x + step].astype(F32)
        out[:, :, x : x + step] = jnp.sum(grid, axis=2) * scale


def to_grid(received, perturb, fourier, first, sq, scale):
    lat_rows, levels, members, lon = perturb.shape
    lanes = received[0].shape[-1]
    sb = divisor(sq, 8)
    base = first // sb
    kdim = fourier.shape[0]
    return pl.pallas_call(
        functools.partial(grid_kernel, len(received), scale),
        grid=(sq // sb,),
        in_specs=[
            pl.BlockSpec((r.shape[0], sb, r.shape[2], lanes), lambda s: (0, s, 0, 0)) for r in received
        ]
        + [
            pl.BlockSpec((sb, levels, members, lon), lambda s: (base + s, 0, 0, 0)),
            pl.BlockSpec((kdim, lon), lambda s: (0, 0)),
        ],
        out_specs=pl.BlockSpec((sb, levels, lon), lambda s: (s, 0, 0)),
        out_shape=jax.ShapeDtypeStruct((sq, levels, lon), F32),
        scratch_shapes=[pltpu.VMEM((sb * levels * members, kdim), BF16)],
        compiler_params=pltpu.CompilerParams(vmem_limit_bytes=VMEM_LIMIT),
        cost_estimate=pl.CostEstimate(
            flops=2 * sq * levels * members * kdim * lon,
            bytes_accessed=sq * levels * members * (lon + kdim) * 2 + kdim * lon * 2,
            transcendentals=0,
        ),
    )(*received, perturb, fourier)


def adjoint_kernel(count, scale, perturb, gradient, fourier, *outs):
    sb, levels, members, lon = perturb.shape
    lanes = outs[0].shape[-1]
    half = lanes // 2
    waves = fourier.shape[0] // 2
    force = gradient[...] * scale
    adjoint = perturb[...].astype(F32) * force[:, :, None, :]
    adjoint = adjoint.astype(BF16).reshape(sb * levels * members, lon)
    result = [dot(fourier[c * waves : (c + 1) * waves], adjoint, 1, 1) for c in range(2)]
    for s in range(sb):
        rows = jnp.concatenate([r[:, s * half : (s + 1) * half] for r in result], axis=1).astype(BF16)
        at = 0
        for out in outs:
            for m in range(out.shape[0]):
                out[m, s] = rows[at : at + out.shape[2]]
                at += out.shape[2]


def from_grid(perturb, gradient, fourier, first, sq, shapes, scale):
    lat_rows, levels, members, lon = perturb.shape
    lanes = 2 * levels * members
    sb = divisor(sq, 8)
    base = first // sb
    kdim = fourier.shape[0]
    return pl.pallas_call(
        functools.partial(adjoint_kernel, len(shapes), scale),
        grid=(sq // sb,),
        in_specs=[
            pl.BlockSpec((sb, levels, members, lon), lambda s: (base + s, 0, 0, 0)),
            pl.BlockSpec((sb, levels, lon), lambda s: (s, 0, 0)),
            pl.BlockSpec((kdim, lon), lambda s: (0, 0)),
        ],
        out_specs=[pl.BlockSpec((m, sb, rows, lanes), lambda s: (0, s, 0, 0)) for m, rows in shapes],
        out_shape=[jax.ShapeDtypeStruct((m, sq, rows, lanes), BF16) for m, rows in shapes],
        compiler_params=pltpu.CompilerParams(vmem_limit_bytes=VMEM_LIMIT),
        cost_estimate=pl.CostEstimate(
            flops=2 * sq * levels * members * kdim * lon,
            bytes_accessed=sq * levels * members * (lon + kdim) * 2 + kdim * lon * 2,
            transcendentals=0,
        ),
    )(perturb, gradient, fourier)


def body(coef, perturb, weight, table, wave_map, lat_map):
    parts, rows, members, levels, nwave = coef.shape
    lat_rows, _, _, lon = perturb.shape
    bands = lax.axis_size("band")
    me = lax.axis_index("band")
    scale = 1.0 / math.sqrt(members * lax.axis_size("mem") - 1)
    pairwise = bands <= 8 and bands & (bands - 1) == 0
    chunks = 2 if pairwise and lat_rows % 16 == 0 else 1
    halves = 2 if pairwise and rows % 32 == 0 else 1
    sq, rh = lat_rows // chunks, rows // halves

    count = jnp.arange(bands, dtype=jnp.int32)
    order = me ^ count if pairwise else count
    chosen = (order[:, None] == count[None, :]).astype(jnp.int32)
    waves_in_order = jnp.sum(chosen[:, :, None] * wave_map.reshape(1, bands, rows), axis=1)
    lats_in_order = jnp.sum(chosen[:, :, None] * lat_map.reshape(1, bands, lat_rows), axis=1)
    own_waves = lax.dynamic_slice_in_dim(wave_map, me * rows, rows)

    natural = jnp.arange(bands * lat_rows, dtype=jnp.int32)
    spread = (lats_in_order.reshape(-1)[:, None] == natural[None, :]).astype(BF16)
    by_chunk = lats_in_order.reshape(bands, chunks, sq).transpose(1, 0, 2).reshape(-1)
    gather = (by_chunk[:, None] == natural[None, :]).astype(BF16)

    wave_order = waves_in_order.reshape(-1)
    columns = jnp.arange(lon, dtype=jnp.int32)
    phase = wave_order[:, None] * columns[None, :] % lon
    angle = phase.astype(F32) * (2.0 * math.pi / lon)
    factor = jnp.where(wave_order == 0, 1.0, 2.0).astype(F32)[:, None]
    fourier = jnp.concatenate([factor * jnp.cos(angle), -factor * jnp.sin(angle)], axis=0).astype(BF16)

    perturb = perturb.transpose(0, 2, 1, 3)

    def send(block, hop):
        return lax.ppermute(block, "band", [(d, d ^ hop) for d in range(bands)])

    hops = sorted(range(bands), reverse=True)

    sent = [synth(own_waves, coef, table, spread, h * rh, rh) for h in range(halves)]
    arrived = []
    for q in range(chunks):
        got = {}
        for h in range(halves):
            blocks = sent[h].reshape(bands, lat_rows, rh, -1)[:, q * sq : (q + 1) * sq]
            if pairwise:
                for hop in hops:
                    block = blocks[hop : hop + 1]
                    got[hop, h] = send(block, hop) if hop else block
            else:
                got[0, h] = lax.all_to_all(blocks, "band", split_axis=0, concat_axis=0, tiled=True)
        arrived.append([got[key] for key in sorted(got)])

    increments, returned = [], []
    for q in range(chunks):
        part = to_grid(arrived[q], perturb, fourier, q * sq, sq, scale)
        if increments:
            part, increments[-1] = lax.optimization_barrier((part, increments[-1]))
        increment = lax.psum(part, "mem")
        increments.append(increment)
        gradient = weight[q * sq : (q + 1) * sq] * increment
        shapes = [(a.shape[0], a.shape[2]) for a in arrived[q]]
        outs = from_grid(perturb, gradient, fourier, q * sq, sq, shapes, scale)
        got = {}
        for h in range(halves):
            if pairwise:
                for hop in hops:
                    block = outs[hop * halves + h]
                    got[h, hop] = send(block, hop) if hop else block
            else:
                got[h, 0] = lax.all_to_all(outs[h], "band", split_axis=0, concat_axis=0, tiled=True)
        returned.append(got)

    product = None
    for h in range(halves):
        received = [
            returned[q][h, hop]
            for q in range(chunks)
            for hop in range(bands if pairwise else 1)
        ]
        product = analyse(own_waves, received, coef, table, gather, h * rh, rh, product)
    increment = jnp.concatenate(increments, axis=0) if chunks > 1 else increments[0]
    return (increment, product)


def solution(mesh):
    in_specs = (
        P(None, "band", "mem", None, None),
        P("band", "mem", None, None),
        P("band", None, None),
        P("band", None, None),
        P(),
        P(),
    )
    out_specs = (P("band", None, None), P(None, "band", "mem", None, None))
    return jax.shard_map(body, mesh=mesh, in_specs=in_specs, out_specs=out_specs, check_vma=False)
```

time: 1540 us -> 742 us (0.48)
  local copies, waits for them, and re-layouts: 526 us -> 36.3 us
  blocking collectives: 368 us -> 0 us
  matrix products: 179 us -> 0 us
  Pallas kernels: 0 us -> 175 us
  other arithmetic: 135 us -> 22.9 us
  waiting for transfers between devices: 295 us -> 397 us
  starting transfers between devices: 6.38 us -> 94.2 us
    all_to_all x1 -> x0, blocking collectives: 368 us -> none  [body(): lax.all_to_all(adjoint_fields, 'band', split_axis=1, concat_axis=2, tiled...]
    ppermute x0 -> x56, waiting for transfers between devices: none -> 344 us  [send(): return lax.ppermute(block, 'band', [(d, d ^ hop) for d in range(bands)])]
    all_to_all x1 -> x0, waiting for transfers between devices: 270 us -> none  [body(): lax.all_to_all(fields, 'band', split_axis=2, concat_axis=1, tiled=True)]
    dot_general x7 -> x0, matrix products: 179 us -> none  [the longest x2 51.1 us: body(): jnp.einsum('msq,mjs->mqj', returned[part], loc_table, preferred_element_t...]
    pallas_call x0 -> x8, Pallas kernels: none -> 175 us  [the longest x2 62 us: analyse(): pl.pallas_call(functools.partial(analyse_kernel, n, first, rb, pair), gri...]
    ppermute x0 -> x56, starting transfers between devices: none -> 94 us  [send(): return lax.ppermute(block, 'band', [(d, d ^ hop) for d in range(bands)])]
    unnamed x14 -> x105, local copies, waits for them, and re-layouts: 110 us -> 23.3 us
    convert_element_type x2 -> x0, local copies, waits for them, and re-layouts: 84.1 us -> none  [the longest x1 62.4 us: body(): (jnp.take(table, lat_map, axis=2).astype(jnp.float32) * valid[:, :, None]...]
  transfers between devices with their start and end apart: 2 -> 58, of which waited for: 2 -> 28; matrix products, arithmetic and copies ran while one was open for 1% -> 6% of each run, Pallas kernels for 0% -> 14%
where the time goes in v1:
time: 742 us; the launch traced here: 740 us
  waiting for transfers between devices  397 us (54%)
  Pallas kernels  175 us (24%)
  starting transfers between devices  94.2 us (13%)
  local copies, waits for them, and re-layouts  36.3 us (5%)
  other arithmetic  22.9 us (3%)
  between operations  14.5 us (2%)
    ppermute x56, waiting for transfers between devices, send(): return lax.ppermute(block, 'band', [(d, d ^ hop) for d in range(bands)])  344 us
    ppermute x56, starting transfers between devices, send(): return lax.ppermute(block, 'band', [(d, d ^ hop) for d in range(bands)])  94 us
    pallas_call x2, Pallas kernels, analyse(): pl.pallas_call(functools.partial(analyse_kernel, n, first, rb, pair), gri...  62 us
    psum x2, waiting for transfers between devices, body(): increment = lax.psum(part, 'mem')  53.2 us
    pallas_call x2, Pallas kernels, synth(): pl.pallas_call(functools.partial(synth_kernel, first, rb, pair), grid_spe...  52.2 us
    pallas_call x2, Pallas kernels, to_grid(): pl.pallas_call(functools.partial(grid_kernel, len(received), scale), grid...  30.6 us
    pallas_call x2, Pallas kernels, from_grid(): pl.pallas_call(functools.partial(adjoint_kernel, len(shapes), scale), gri...  30.5 us
    unnamed x105, local copies, waits for them, and re-layouts  23.3 us
  transfers between devices with their start and end apart: 58, of which 28 were waited for; matrix products, arithmetic and copies ran while one was open for 6% of the time, Pallas kernels for 14%

profile of v1, /device:TPU:8, one launch (start us, length us, event | category | flops | bytes accessed | tf_op | source)
XLA Modules:
  0.0 740.1 jit_solution(5591557688195168671)
XLA Ops:
  10.8 26.1 %shard_map.78 = bf16[768,32,128]{2,1,0:T(8,128)(2,1)} custom-call(s32[64]{0:T(128)} %dynamic_slice.3.waves.refs_0_, f32[2,64,32,2,512]{4,3,2,1,0:T(2,128)} %refs_17_.3, bf16[64,512,768]{2,1,0:T(8,128)(2,1)} %refs_18_.3, bf16[768,768]{1,0:T(8,128)(2,1)} %fusion.5.spread), custom_call_target="tpu_custom_call" | custom-call | flops 8053063680 | bytes 39845888 | tf_op jit(solution)/shard_map/pallas_call | solution.py:63
  36.8 5.2 fusion.9
  42.1 2.5 collective-permute-start.27
  45.0 4.4 collective-permute-start.23
  49.4 1.7 collective-permute-start.19
  51.1 42.7 %collective-permute-done.27.refs_15_ = bf16[1,48,32,128]{3,2,1,0:T(8,128)(2,1)S(1)} collective-permute-done((bf16[1,48,32,128]{3,2,1,0:T(8,128)(2,1)S(1)}, bf16[1,48,32,128]{3,2,1,0:T(8,128)(2,1)S(1)}, u32[]{:S(2)}, u32[]{:S(2)}) %collective-permute-start.27) | collective-permute-done | bytes 393248 | tf_op jit(solution)/shard_map/ppermute | solution.py:294
  93.7 7.3 collective-permute-done.25.refs_13_
  101.8 6.8 collective-permute-done.23.refs_11_
  109.2 26.1 %shard_map.77 = bf16[768,32,128]{2,1,0:T(8,128)(2,1)} custom-call(s32[64]{0:T(128)} %dynamic_slice.3.waves.refs_0_, f32[2,64,32,2,512]{4,3,2,1,0:T(2,128)} %refs_17_.3, bf16[64,512,768]{2,1,0:T(8,128)(2,1)} %refs_18_.3, bf16[768,768]{1,0:T(8,128)(2,1)} %fusion.5.spread), custom_call_target="tpu_custom_call" | custom-call | flops 8053063680 | bytes 39845888 | tf_op jit(solution)/shard_map/pallas_call | solution.py:63
  136.7 6.1 collective-permute-start.9
  143.0 2.8 collective-permute-start.5
  146.6 5.4 fusion.10
  152.0 20.8 %collective-permute-done.11.refs_13_ = bf16[1,48,32,128]{3,2,1,0:T(8,128)(2,1)S(1)} collective-permute-done((bf16[1,48,32,128]{3,2,1,0:T(8,128)(2,1)S(1)}, bf16[1,48,32,128]{3,2,1,0:T(8,128)(2,1)S(1)}, u32[]{:S(2)}, u32[]{:S(2)}) %collective-permute-start.11) | collective-permute-done | bytes 393248 | tf_op jit(solution)/shard_map/ppermute | solution.py:294
  174.1 5.7 collective-permute-done.9.refs_11_
  179.8 1.6 collective-permute-start.26
  181.4 27.8 %collective-permute-done.7.refs_9_ = bf16[1,48,32,128]{3,2,1,0:T(8,128)(2,1)S(1)} collective-permute-done((bf16[1,48,32,128]{3,2,1,0:T(8,128)(2,1)S(1)}, bf16[1,48,32,128]{3,2,1,0:T(8,128)(2,1)S(1)}, u32[]{:S(2)}, u32[]{:S(2)}) %collective-permute-start.7) | collective-permute-done | bytes 393248 | tf_op jit(solution)/shard_map/ppermute | solution.py:294
  210.2 5.0 collective-permute-start.22
  216.3 2.7 collective-permute-start.18
  219.0 15.6 %collective-permute-done.26.refs_14_ = bf16[1,48,32,128]{3,2,1,0:T(8,128)(2,1)} collective-permute-done((bf16[1,48,32,128]{3,2,1,0:T(8,128)(2,1)}, bf16[1,48,32,128]{3,2,1,0:T(8,128)(2,1)}, u32[]{:S(2)}, u32[]{:S(2)}) %collective-permute-start.26) | collective-permute-done | bytes 393248 | tf_op jit(solution)/shard_map/ppermute | solution.py:294
  234.5 6.6 collective-permute-done.24.refs_12_
  241.1 2.2 collective-permute-start.14
  243.3 8.9 %collective-permute-done.22.refs_10_ = bf16[1,48,32,128]{3,2,1,0:T(8,128)(2,1)} collective-permute-done((bf16[1,48,32,128]{3,2,1,0:T(8,128)(2,1)}, bf16[1,48,32,128]{3,2,1,0:T(8,128)(2,1)}, u32[]{:S(2)}, u32[]{:S(2)}) %collective-permute-start.22) | collective-permute-done | bytes 393248 | tf_op jit(solution)/shard_map/ppermute | solution.py:294
  252.3 2.5 collective-permute-start.12
  254.8 14.5 %collective-permute-done.20.refs_8_ = bf16[1,48,32,128]{3,2,1,0:T(8,128)(2,1)} collective-permute-done((bf16[1,48,32,128]{3,2,1,0:T(8,128)(2,1)}, bf16[1,48,32,128]{3,2,1,0:T(8,128)(2,1)}, u32[]{:S(2)}, u32[]{:S(2)}) %collective-permute-start.20) | collective-permute-done | bytes 393248 | tf_op jit(solution)/shard_map/ppermute | solution.py:294
  270.2 13.8 %multiply_convert_fusion.1 = (bf16[512,1536]{1,0:T(8,128)(2,1)S(1)}, bf16[512,1536]{1,0:T(8,128)(2,1)S(1)}) fusion(s32[512]{0:T(512)S(1)} %reshape.63, f32[512]{0:T(512)S(1)} %get-tuple-element.106, f32[512]{0:T(512)S(1)} %get-tuple-element.107), kind=kLoop, calls=%fused_computation.6 | loop fusion | flops 10223616 | bytes 3151872 | tf_op jit(solution)/shard_map/convert
  284.0 18.9 %copy.16 = bf16[96,32,2,1536]{3,1,2,0:T(8,128)(2,1)} copy(bf16[96,32,2,1536]{3,2,1,0:T(2,128)(2,1)} %param.7) | data formatting | bytes 37748736 | tf_op args[1]
  302.9 1.9 pad_maximum_fusion.refs_17_.fourier
  304.8 5.9 collective-permute-start.8
  310.7 1.8 collective-permute-start.4
  314.3 15.2 %shard_map.80 = f32[48,2,1536]{2,1,0:T(2,128)} custom-call(bf16[1,48,32,128]{3,2,1,0:T(8,128)(2,1)} %get-tuple-element.93.refs_0_, bf16[1,48,32,128]{3,2,1,0:T(8,128)(2,1)} %get-tuple-element.77.refs_1_, bf16[1,48,32,128]{3,2,1,0:T(8,128)(2,1)} %copy-done.48, bf16[1,48,32,128]{3,2,1,0:T(8,128)(2,1)} %copy-done.39, bf16[1,48,32,128]{3,2,1,0:T(8,128)(2,1)} %copy-done.47, ...), custom_call_target="tpu_custom_call" | custom-call | flops 9663676416 | bytes 18874368 | tf_op jit(solution)/shard_map/pallas_call | solution.py:196
  331.8 15.4 %shard_map.79 = f32[48,2,1536]{2,1,0:T(2,128)} custom-call(bf16[1,48,32,128]{3,2,1,0:T(8,128)(2,1)} %get-tuple-element.101.refs_0_, bf16[1,48,32,128]{3,2,1,0:T(8,128)(2,1)} %get-tuple-element.85.refs_1_, bf16[1,48,32,128]{3,2,1,0:T(8,128)(2,1)} %copy-done.51, bf16[1,48,32,128]{3,2,1,0:T(8,128)(2,1)} %collective-permute-done.1.refs_3_, ...), custom_call_target="tpu_custom_call" | custom-call | flops 9663676416 | bytes 18874368 | tf_op jit(solution)/shard_map/pallas_call | solution.py:196
  347.1 16.7 %all-reduce.3.cloned.1.call-done = f32[48,2,1536]{2,1,0:T(2,128)} async-done(((f32[48,2,1536]{2,1,0:T(2,128)}), f32[48,2,1536]{2,1,0:T(2,128)}) %all-reduce.3.cloned.1.call-update) | async-done | bytes 589840 | tf_op jit(solution)/shard_map/psum | solution.py:317
  363.9 36.4 %all-reduce.5.cloned.1.call-done = f32[48,2,1536]{2,1,0:T(2,128)} async-done(((f32[48,2,1536]{2,1,0:T(2,128)}), f32[48,2,1536]{2,1,0:T(2,128)}) %all-reduce.5.cloned.1.call-update) | async-done | bytes 589840 | tf_op jit(solution)/shard_map/psum | solution.py:317
  400.3 2.9 slice_multiply_fusion
  403.2 15.3 %shard_map.82 = (bf16[1,48,32,128]{3,2,1,0:T(8,128)(2,1)}, bf16[1,48,32,128]{3,2,1,0:T(8,128)(2,1)}, bf16[1,48,32,128]{3,2,1,0:T(8,128)(2,1)}, bf16[1,48,32,128]...) custom-call(bf16[96,2,32,1536]{3,2,1,0:T(8,128)(2,1)} %bitcast.10, ...), custom_call_target="tpu_custom_call" | custom-call | flops 9663676416 | bytes 18874368 | tf_op jit(solution)/shard_map/pallas_call | solution.py:242
  422.0 2.4 collective-permute-start.38
  425.8 4.0 collective-permute-done.35.refs_10_
  431.4 14.1 %collective-permute-done.36.refs_11_ = bf16[1,48,32,128]{3,2,1,0:T(8,128)(2,1)S(1)} collective-permute-done((bf16[1,48,32,128]{3,2,1,0:T(8,128)(2,1)}, bf16[1,48,32,128]{3,2,1,0:T(8,128)(2,1)S(1)}, u32[]{:S(2)}, u32[]{:S(2)}) %collective-permute-start.36) | collective-permute-done | bytes 393248 | tf_op jit(solution)/shard_map/ppermute | solution.py:294
  446.4 5.1 collective-permute-done.37.refs_12_
  451.6 3.8 collective-permute-start.50
  455.4 21.1 %collective-permute-done.39.refs_14_ = bf16[1,48,32,128]{3,2,1,0:T(8,128)(2,1)S(1)} collective-permute-done((bf16[1,48,32,128]{3,2,1,0:T(8,128)(2,1)}, bf16[1,48,32,128]{3,2,1,0:T(8,128)(2,1)S(1)}, u32[]{:S(2)}, u32[]{:S(2)}) %collective-permute-start.39) | collective-permute-done | bytes 393248 | tf_op jit(solution)/shard_map/ppermute | solution.py:294
  476.5 2.3 collective-permute-start.51
  478.8 6.1 collective-permute-done.40.refs_15_
  484.9 27.7 %collective-permute-done.41.refs_16_ = bf16[1,48,32,128]{3,2,1,0:T(8,128)(2,1)S(1)} collective-permute-done((bf16[1,48,32,128]{3,2,1,0:T(8,128)(2,1)}, bf16[1,48,32,128]{3,2,1,0:T(8,128)(2,1)S(1)}, u32[]{:S(2)}, u32[]{:S(2)}) %collective-permute-start.41) | collective-permute-done | bytes 393248 | tf_op jit(solution)/shard_map/ppermute | solution.py:294
  512.6 1.7 collective-permute-start.54
  514.3 15.2 %shard_map.81 = (bf16[1,48,32,128]{3,2,1,0:T(8,128)(2,1)}, bf16[1,48,32,128]{3,2,1,0:T(8,128)(2,1)}, bf16[1,48,32,128]{3,2,1,0:T(8,128)(2,1)}, bf16[1,48,32,128]...) custom-call(bf16[96,2,32,1536]{3,2,1,0:T(8,128)(2,1)} %bitcast.11, ...), custom_call_target="tpu_custom_call" | custom-call | flops 9663676416 | bytes 18874368 | tf_op jit(solution)/shard_map/pallas_call | solution.py:242
  532.6 4.9 collective-permute-start.29
  537.6 7.6 %collective-permute-done.53.refs_14_ = bf16[1,48,32,128]{3,2,1,0:T(8,128)(2,1)} collective-permute-done((bf16[1,48,32,128]{3,2,1,0:T(8,128)(2,1)}, bf16[1,48,32,128]{3,2,1,0:T(8,128)(2,1)}, u32[]{:S(2)}, u32[]{:S(2)}) %collective-permute-start.53) | collective-permute-done | bytes 393248 | tf_op jit(solution)/shard_map/ppermute | solution.py:294
  546.1 8.0 %collective-permute-done.54.refs_15_ = bf16[1,48,32,128]{3,2,1,0:T(8,128)(2,1)} collective-permute-done((bf16[1,48,32,128]{3,2,1,0:T(8,128)(2,1)}, bf16[1,48,32,128]{3,2,1,0:T(8,128)(2,1)}, u32[]{:S(2)}, u32[]{:S(2)}) %collective-permute-start.54) | collective-permute-done | bytes 393248 | tf_op jit(solution)/shard_map/ppermute | solution.py:294
  554.3 6.1 collective-permute-done.55.refs_16_
  560.4 3.5 collective-permute-start.45
  565.4 4.8 collective-permute-done.43.refs_3_
  573.4 5.5 collective-permute-done.44.refs_4_
  579.0 3.3 collective-permute-start.30
  582.2 25.3 %collective-permute-done.45.refs_5_ = bf16[1,48,32,128]{3,2,1,0:T(8,128)(2,1)S(1)} collective-permute-done((bf16[1,48,32,128]{3,2,1,0:T(8,128)(2,1)}, bf16[1,48,32,128]{3,2,1,0:T(8,128)(2,1)S(1)}, u32[]{:S(2)}, u32[]{:S(2)}) %collective-permute-start.45) | collective-permute-done | bytes 393248 | tf_op jit(solution)/shard_map/ppermute | solution.py:294
  607.5 3.3 collective-permute-start.31
  610.8 26.2 %collective-permute-done.46.refs_6_ = bf16[1,48,32,128]{3,2,1,0:T(8,128)(2,1)S(1)} collective-permute-done((bf16[1,48,32,128]{3,2,1,0:T(8,128)(2,1)}, bf16[1,48,32,128]{3,2,1,0:T(8,128)(2,1)S(1)}, u32[]{:S(2)}, u32[]{:S(2)}) %collective-permute-start.46) | collective-permute-done | bytes 393248 | tf_op jit(solution)/shard_map/ppermute | solution.py:294
  637.0 4.2 collective-permute-start.32
  641.2 17.1 %collective-permute-done.47.refs_7_ = bf16[1,48,32,128]{3,2,1,0:T(8,128)(2,1)S(1)} collective-permute-done((bf16[1,48,32,128]{3,2,1,0:T(8,128)(2,1)}, bf16[1,48,32,128]{3,2,1,0:T(8,128)(2,1)S(1)}, u32[]{:S(2)}, u32[]{:S(2)}) %collective-permute-start.47) | collective-permute-done | bytes 393248 | tf_op jit(solution)/shard_map/ppermute | solution.py:294
  658.3 2.1 collective-permute-start.33
  660.4 7.3 collective-permute-done.48.refs_8_
  667.7 2.1 collective-permute-start.34
  669.8 31.0 %shard_map.83.refs_20_ = f32[2,64,32,2,512]{4,3,2,1,0:T(2,128)} custom-call(s32[64]{0:T(128)} %dynamic_slice.3.waves.refs_0_, bf16[1,48,32,128]{3,2,1,0:T(8,128)(2,1)} %get-tuple-element.54.refs_1_, bf16[1,48,32,128]{3,2,1,0:T(8,128)(2,1)} %copy-done.15, bf16[1,48,32,128]{3,2,1,0:T(8,128)(2,1)} %copy-done.16, bf16[1,48,32,128]{3,2,1,0:T(8,128)(2,1)} %copy-done.17, ...), custom_call_target="tpu_custom_call" | custom-call | flops 8053063680 | bytes 48234496 | tf_op jit(solution)/shard_map/pallas_call | solution.py:137
  702.2 31.0 %shard_map.84 = f32[2,64,32,2,512]{4,3,2,1,0:T(2,128)} custom-call(s32[64]{0:T(128)} %dynamic_slice.3.waves.refs_0_, bf16[1,48,32,128]{3,2,1,0:T(8,128)(2,1)} %get-tuple-element.38.refs_1_, bf16[1,48,32,128]{3,2,1,0:T(8,128)(2,1)} %copy-done.12, bf16[1,48,32,128]{3,2,1,0:T(8,128)(2,1)} %copy-done.13, ...), custom_call_target="tpu_custom_call", output_to_operand_aliasing={{}: (20, {})} | custom-call | flops 8053063680 | bytes 48234496 | tf_op jit(solution)/shard_map/pallas_call | solution.py:137
  (188 shorter events, 33.8 us)
Async XLA Ops:
  7.2 356.7 %all-reduce.3.cloned.1.call-start = ((), (), s32[]{:S(2)}) async-start(), calls=%async_computation | async-start | bytes 1179648 | tf_op jit(solution)/shard_map/psum | solution.py:317
  42.1 51.7 %collective-permute-start.27 = (bf16[1,48,32,128]{3,2,1,0:T(8,128)(2,1)S(1)}, bf16[1,48,32,128]{3,2,1,0:T(8,128)(2,1)S(1)}, u32[]{:S(2)}, u32[]{:S(2)}) collective-permute-start(bf16[1,48,32,128]{3,2,1,0:T(8,128)(2,1)S(1)} %get-tuple-element.70), channel_id=1, source_target_pairs={{0,28},{4,24},{8,20},{12,16},{16,12},{20,8},{24,4},{28,0},{1,29},{... | collective-permute-start | bytes 1179656 | tf_op jit(solution)/shard_map/ppermute | solution.py:294
  44.6 56.5 %collective-permute-start.25 = (bf16[1,48,32,128]{3,2,1,0:T(8,128)(2,1)S(1)}, bf16[1,48,32,128]{3,2,1,0:T(8,128)(2,1)S(1)}, u32[]{:S(2)}, u32[]{:S(2)}) collective-permute-start(bf16[1,48,32,128]{3,2,1,0:T(8,128)(2,1)S(1)} %get-tuple-element.71), channel_id=1, source_target_pairs={{0,24},{4,28},{8,16},{12,20},{16,8},{20,12},{24,0},{28,4},{1,25},{... | collective-permute-start | bytes 1179656 | tf_op jit(solution)/shard_map/ppermute | solution.py:294
  45.0 63.5 %collective-permute-start.23 = (bf16[1,48,32,128]{3,2,1,0:T(8,128)(2,1)S(1)}, bf16[1,48,32,128]{3,2,1,0:T(8,128)(2,1)S(1)}, u32[]{:S(2)}, u32[]{:S(2)}) collective-permute-start(bf16[1,48,32,128]{3,2,1,0:T(8,128)(2,1)S(1)} %get-tuple-element.72), channel_id=1, source_target_pairs={{0,20},{4,16},{8,28},{12,24},{16,4},{20,0},{24,12},{28,8},{1,21},{... | collective-permute-start | bytes 1179656 | tf_op jit(solution)/shard_map/ppermute | solution.py:294
  49.4 85.9 %collective-permute-start.21 = (bf16[1,48,32,128]{3,2,1,0:T(8,128)(2,1)S(1)}, bf16[1,48,32,128]{3,2,1,0:T(8,128)(2,1)S(1)}, u32[]{:S(2)}, u32[]{:S(2)}) collective-permute-start(bf16[1,48,32,128]{3,2,1,0:T(8,128)(2,1)S(1)} %get-tuple-element.73), channel_id=1, source_target_pairs={{0,16},{4,20},{8,24},{12,28},{16,0},{20,4},{24,8},{28,12},{1,17},{... | collective-permute-start | bytes 1179656 | tf_op jit(solution)/shard_map/ppermute | solution.py:294
  49.4 87.3 %collective-permute-start.19 = (bf16[1,48,32,128]{3,2,1,0:T(8,128)(2,1)S(1)}, bf16[1,48,32,128]{3,2,1,0:T(8,128)(2,1)S(1)}, u32[]{:S(2)}, u32[]{:S(2)}) collective-permute-start(bf16[1,48,32,128]{3,2,1,0:T(8,128)(2,1)S(1)} %get-tuple-element.74), channel_id=1, source_target_pairs={{0,12},{4,8},{8,4},{12,0},{16,28},{20,24},{24,20},{28,16},{1,13},{... | collective-permute-start | bytes 1179656 | tf_op jit(solution)/shard_map/ppermute | solution.py:294
  93.7 49.1 %collective-permute-start.17 = (bf16[1,48,32,128]{3,2,1,0:T(8,128)(2,1)S(1)}, bf16[1,48,32,128]{3,2,1,0:T(8,128)(2,1)S(1)}, u32[]{:S(2)}, u32[]{:S(2)}) collective-permute-start(bf16[1,48,32,128]{3,2,1,0:T(8,128)(2,1)S(1)} %get-tuple-element.75), channel_id=1, source_target_pairs={{0,8},{4,12},{8,0},{12,4},{16,24},{20,28},{24,16},{28,20},{1,9},{5... | collective-permute-start | bytes 1179656 | tf_op jit(solution)/shard_map/ppermute | solution.py:294
  101.1 41.9 %collective-permute-start.15 = (bf16[1,48,32,128]{3,2,1,0:T(8,128)(2,1)S(1)}, bf16[1,48,32,128]{3,2,1,0:T(8,128)(2,1)S(1)}, u32[]{:S(2)}, u32[]{:S(2)}) collective-permute-start(bf16[1,48,32,128]{3,2,1,0:T(8,128)(2,1)S(1)} %get-tuple-element.76), channel_id=1, source_target_pairs={{0,4},{4,0},{8,12},{12,8},{16,20},{20,16},{24,28},{28,24},{1,5},{5... | collective-permute-start | bytes 1179656 | tf_op jit(solution)/shard_map/ppermute | solution.py:294
  108.6 37.2 %collective-permute-start.13 = (bf16[1,48,32,128]{3,2,1,0:T(8,128)(2,1)S(1)}, bf16[1,48,32,128]{3,2,1,0:T(8,128)(2,1)S(1)}, u32[]{:S(2)}, u32[]{:S(2)}) collective-permute-start(bf16[1,48,32,128]{3,2,1,0:T(8,128)(2,1)S(1)} %get-tuple-element.78), channel_id=1, source_target_pairs={{0,28},{4,24},{8,20},{12,16},{16,12},{20,8},{24,4},{28,0},{1,29},{... | collective-permute-start | bytes 1179656 | tf_op jit(solution)/shard_map/ppermute | solution.py:294
  135.3 37.4 %collective-permute-start.11 = (bf16[1,48,32,128]{3,2,1,0:T(8,128)(2,1)S(1)}, bf16[1,48,32,128]{3,2,1,0:T(8,128)(2,1)S(1)}, u32[]{:S(2)}, u32[]{:S(2)}) collective-permute-start(bf16[1,48,32,128]{3,2,1,0:T(8,128)(2,1)S(1)} %get-tuple-element.79), channel_id=1, source_target_pairs={{0,24},{4,28},{8,16},{12,20},{16,8},{20,12},{24,0},{28,4},{1,25},{... | collective-permute-start | bytes 1179656 | tf_op jit(solution)/shard_map/ppermute | solution.py:294
  136.7 43.0 %collective-permute-start.9 = (bf16[1,48,32,128]{3,2,1,0:T(8,128)(2,1)S(1)}, bf16[1,48,32,128]{3,2,1,0:T(8,128)(2,1)S(1)}, u32[]{:S(2)}, u32[]{:S(2)}) collective-permute-start(bf16[1,48,32,128]{3,2,1,0:T(8,128)(2,1)S(1)} %get-tuple-element.80), channel_id=1, source_target_pairs={{0,20},{4,16},{8,28},{12,24},{16,4},{20,0},{24,12},{28,8},{1,21},{... | collective-permute-start | bytes 1179656 | tf_op jit(solution)/shard_map/ppermute | solution.py:294
  142.9 66.3 %collective-permute-start.7 = (bf16[1,48,32,128]{3,2,1,0:T(8,128)(2,1)S(1)}, bf16[1,48,32,128]{3,2,1,0:T(8,128)(2,1)S(1)}, u32[]{:S(2)}, u32[]{:S(2)}) collective-permute-start(bf16[1,48,32,128]{3,2,1,0:T(8,128)(2,1)S(1)} %get-tuple-element.81), channel_id=1, source_target_pairs={{0,16},{4,20},{8,24},{12,28},{16,0},{20,4},{24,8},{28,12},{1,17},{... | collective-permute-start | bytes 1179656 | tf_op jit(solution)/shard_map/ppermute | solution.py:294
  143.0 67.2 %collective-permute-start.5 = (bf16[1,48,32,128]{3,2,1,0:T(8,128)(2,1)S(1)}, bf16[1,48,32,128]{3,2,1,0:T(8,128)(2,1)S(1)}, u32[]{:S(2)}, u32[]{:S(2)}) collective-permute-start(bf16[1,48,32,128]{3,2,1,0:T(8,128)(2,1)S(1)} %get-tuple-element.82), channel_id=1, source_target_pairs={{0,12},{4,8},{8,4},{12,0},{16,28},{20,24},{24,20},{28,16},{1,13},{... | collective-permute-start | bytes 1179656 | tf_op jit(solution)/shard_map/ppermute | solution.py:294
  145.8 69.4 %collective-permute-start.3 = (bf16[1,48,32,128]{3,2,1,0:T(8,128)(2,1)S(1)}, bf16[1,48,32,128]{3,2,1,0:T(8,128)(2,1)S(1)}, u32[]{:S(2)}, u32[]{:S(2)}) collective-permute-start(bf16[1,48,32,128]{3,2,1,0:T(8,128)(2,1)S(1)} %get-tuple-element.83), channel_id=1, source_target_pairs={{0,8},{4,12},{8,0},{12,4},{16,24},{20,28},{24,16},{28,20},{1,9},{5... | collective-permute-start | bytes 1179656 | tf_op jit(solution)/shard_map/ppermute | solution.py:294
  172.7 43.6 %collective-permute-start.1 = (bf16[1,48,32,128]{3,2,1,0:T(8,128)(2,1)S(1)}, bf16[1,48,32,128]{3,2,1,0:T(8,128)(2,1)}, u32[]{:S(2)}, u32[]{:S(2)}) collective-permute-start(bf16[1,48,32,128]{3,2,1,0:T(8,128)(2,1)S(1)} %get-tuple-element.84), channel_id=1, source_target_pairs={{0,4},{4,0},{8,12},{12,8},{16,20},{20,16},{24,28},{28,24},{1,5},{5... | collective-permute-start | bytes 1179656 | tf_op jit(solution)/shard_map/ppermute | solution.py:294
  179.8 54.8 %collective-permute-start.26 = (bf16[1,48,32,128]{3,2,1,0:T(8,128)(2,1)}, bf16[1,48,32,128]{3,2,1,0:T(8,128)(2,1)}, u32[]{:S(2)}, u32[]{:S(2)}) collective-permute-start(bf16[1,48,32,128]{3,2,1,0:T(8,128)(2,1)} %get-tuple-element.86), channel_id=1, source_target_pairs={{0,28},{4,24},{8,20},{12,16},{16,12},{20,8},{24,4},{28,0},{1,29},{... | collective-permute-start | bytes 1179656 | tf_op jit(solution)/shard_map/ppermute | solution.py:294
  209.2 32.0 %collective-permute-start.24 = (bf16[1,48,32,128]{3,2,1,0:T(8,128)(2,1)}, bf16[1,48,32,128]{3,2,1,0:T(8,128)(2,1)}, u32[]{:S(2)}, u32[]{:S(2)}) collective-permute-start(bf16[1,48,32,128]{3,2,1,0:T(8,128)(2,1)} %get-tuple-element.87), channel_id=1, source_target_pairs={{0,24},{4,28},{8,16},{12,20},{16,8},{20,12},{24,0},{28,4},{1,25},{... | collective-permute-start | bytes 1179656 | tf_op jit(solution)/shard_map/ppermute | solution.py:294
  210.2 42.1 %collective-permute-start.22 = (bf16[1,48,32,128]{3,2,1,0:T(8,128)(2,1)}, bf16[1,48,32,128]{3,2,1,0:T(8,128)(2,1)}, u32[]{:S(2)}, u32[]{:S(2)}) collective-permute-start(bf16[1,48,32,128]{3,2,1,0:T(8,128)(2,1)} %get-tuple-element.88), channel_id=1, source_target_pairs={{0,20},{4,16},{8,28},{12,24},{16,4},{20,0},{24,12},{28,8},{1,21},{... | collective-permute-start | bytes 1179656 | tf_op jit(solution)/shard_map/ppermute | solution.py:294
  216.0 53.2 %collective-permute-start.20 = (bf16[1,48,32,128]{3,2,1,0:T(8,128)(2,1)}, bf16[1,48,32,128]{3,2,1,0:T(8,128)(2,1)}, u32[]{:S(2)}, u32[]{:S(2)}) collective-permute-start(bf16[1,48,32,128]{3,2,1,0:T(8,128)(2,1)} %get-tuple-element.89), channel_id=1, source_target_pairs={{0,16},{4,20},{8,24},{12,28},{16,0},{20,4},{24,8},{28,12},{1,17},{... | collective-permute-start | bytes 1179656 | tf_op jit(solution)/shard_map/ppermute | solution.py:294
  216.3 88.5 %collective-permute-start.18 = (bf16[1,48,32,128]{3,2,1,0:T(8,128)(2,1)}, bf16[1,48,32,128]{3,2,1,0:T(8,128)(2,1)S(1)}, u32[]{:S(2)}, u32[]{:S(2)}) collective-permute-start(bf16[1,48,32,128]{3,2,1,0:T(8,128)(2,1)} %get-tuple-element.90), channel_id=1, source_target_pairs={{0,12},{4,8},{8,4},{12,0},{16,28},{20,24},{24,20},{28,16},{1,13},{... | collective-permute-start | bytes 1179656 | tf_op jit(solution)/shard_map/ppermute | solution.py:294
  234.5 76.1 %collective-permute-start.16 = (bf16[1,48,32,128]{3,2,1,0:T(8,128)(2,1)}, bf16[1,48,32,128]{3,2,1,0:T(8,128)(2,1)S(1)}, u32[]{:S(2)}, u32[]{:S(2)}) collective-permute-start(bf16[1,48,32,128]{3,2,1,0:T(8,128)(2,1)} %get-tuple-element.91), channel_id=1, source_target_pairs={{0,8},{4,12},{8,0},{12,4},{16,24},{20,28},{24,16},{28,20},{1,9},{5... | collective-permute-start | bytes 1179656 | tf_op jit(solution)/shard_map/ppermute | solution.py:294
  241.1 69.5 %collective-permute-start.14 = (bf16[1,48,32,128]{3,2,1,0:T(8,128)(2,1)S(1)}, bf16[1,48,32,128]{3,2,1,0:T(8,128)(2,1)S(1)}, u32[]{:S(2)}, u32[]{:S(2)}) collective-permute-start(bf16[1,48,32,128]{3,2,1,0:T(8,128)(2,1)S(1)} %get-tuple-element.92), channel_id=1, source_target_pairs={{0,4},{4,0},{8,12},{12,8},{16,20},{20,16},{24,28},{28,24},{1,5},{5... | collective-permute-start | bytes 1179656 | tf_op jit(solution)/shard_map/ppermute | solution.py:294
  252.3 60.2 %collective-permute-start.12 = (bf16[1,48,32,128]{3,2,1,0:T(8,128)(2,1)S(1)}, bf16[1,48,32,128]{3,2,1,0:T(8,128)(2,1)S(1)}, u32[]{:S(2)}, u32[]{:S(2)}) collective-permute-start(bf16[1,48,32,128]{3,2,1,0:T(8,128)(2,1)S(1)} %get-tuple-element.94), channel_id=1, source_target_pairs={{0,28},{4,24},{8,20},{12,16},{16,12},{20,8},{24,4},{28,0},{1,29},{... | collective-permute-start | bytes 1179656 | tf_op jit(solution)/shard_map/ppermute | solution.py:294
  269.3 43.5 %collective-permute-start.10 = (bf16[1,48,32,128]{3,2,1,0:T(8,128)(2,1)S(1)}, bf16[1,48,32,128]{3,2,1,0:T(8,128)(2,1)S(1)}, u32[]{:S(2)}, u32[]{:S(2)}) collective-permute-start(bf16[1,48,32,128]{3,2,1,0:T(8,128)(2,1)S(1)} %get-tuple-element.95), channel_id=1, source_target_pairs={{0,24},{4,28},{8,16},{12,20},{16,8},{20,12},{24,0},{28,4},{1,25},{... | collective-permute-start | bytes 1179656 | tf_op jit(solution)/shard_map/ppermute | solution.py:294
  304.8 25.0 %collective-permute-start.8 = (bf16[1,48,32,128]{3,2,1,0:T(8,128)(2,1)S(1)}, bf16[1,48,32,128]{3,2,1,0:T(8,128)(2,1)}, u32[]{:S(2)}, u32[]{:S(2)}) collective-permute-start(bf16[1,48,32,128]{3,2,1,0:T(8,128)(2,1)S(1)} %get-tuple-element.96), channel_id=1, source_target_pairs={{0,20},{4,16},{8,28},{12,24},{16,4},{20,0},{24,12},{28,8},{1,21},{... | collective-permute-start | bytes 1179656 | tf_op jit(solution)/shard_map/ppermute | solution.py:294
  310.7 19.1 %collective-permute-start.6 = (bf16[1,48,32,128]{3,2,1,0:T(8,128)(2,1)S(1)}, bf16[1,48,32,128]{3,2,1,0:T(8,128)(2,1)}, u32[]{:S(2)}, u32[]{:S(2)}) collective-permute-start(bf16[1,48,32,128]{3,2,1,0:T(8,128)(2,1)S(1)} %get-tuple-element.97), channel_id=1, source_target_pairs={{0,16},{4,20},{8,24},{12,28},{16,0},{20,4},{24,8},{28,12},{1,17},{... | collective-permute-start | bytes 1179656 | tf_op jit(solution)/shard_map/ppermute | solution.py:294
  310.7 19.1 %collective-permute-start.4 = (bf16[1,48,32,128]{3,2,1,0:T(8,128)(2,1)S(1)}, bf16[1,48,32,128]{3,2,1,0:T(8,128)(2,1)S(1)}, u32[]{:S(2)}, u32[]{:S(2)}) collective-permute-start(bf16[1,48,32,128]{3,2,1,0:T(8,128)(2,1)S(1)} %get-tuple-element.98), channel_id=1, source_target_pairs={{0,12},{4,8},{8,4},{12,0},{16,28},{20,24},{24,20},{28,16},{1,13},{... | collective-permute-start | bytes 1179656 | tf_op jit(solution)/shard_map/ppermute | solution.py:294
  312.5 18.4 %collective-permute-start.2 = (bf16[1,48,32,128]{3,2,1,0:T(8,128)(2,1)S(1)}, bf16[1,48,32,128]{3,2,1,0:T(8,128)(2,1)S(1)}, u32[]{:S(2)}, u32[]{:S(2)}) collective-permute-start(bf16[1,48,32,128]{3,2,1,0:T(8,128)(2,1)S(1)} %get-tuple-element.99), channel_id=1, source_target_pairs={{0,8},{4,12},{8,0},{12,4},{16,24},{20,28},{24,16},{28,20},{1,9},{5... | collective-permute-start | bytes 1179656 | tf_op jit(solution)/shard_map/ppermute | solution.py:294
  312.8 18.1 %collective-permute-start = (bf16[1,48,32,128]{3,2,1,0:T(8,128)(2,1)S(1)}, bf16[1,48,32,128]{3,2,1,0:T(8,128)(2,1)S(1)}, u32[]{:S(2)}, u32[]{:S(2)}) collective-permute-start(bf16[1,48,32,128]{3,2,1,0:T(8,128)(2,1)S(1)} %get-tuple-element.100), channel_id=1, source_target_pairs={{0,4},{4,0},{8,12},{12,8},{16,20},{20,16},{24,28},{28,24},{1,5},{5... | collective-permute-start | bytes 1179656 | tf_op jit(solution)/shard_map/ppermute | solution.py:294
  329.5 70.8 %all-reduce.5.cloned.1.call-start = ((), (), s32[]{:S(2)}) async-start(), calls=%async_computation.1 | async-start | bytes 1179648 | tf_op jit(solution)/shard_map/psum | solution.py:317
  418.5 11.4 %collective-permute-start.35 = (bf16[1,48,32,128]{3,2,1,0:T(8,128)(2,1)}, bf16[1,48,32,128]{3,2,1,0:T(8,128)(2,1)S(1)}, u32[]{:S(2)}, u32[]{:S(2)}) collective-permute-start(bf16[1,48,32,128]{3,2,1,0:T(8,128)(2,1)} %get-tuple-element.47), channel_id=1, source_target_pairs={{0,4},{4,0},{8,12},{12,8},{16,20},{20,16},{24,28},{28,24},{1,5},{5... | collective-permute-start | bytes 1179656 | tf_op jit(solution)/shard_map/ppermute | solution.py:294
  420.0 25.5 %collective-permute-start.36 = (bf16[1,48,32,128]{3,2,1,0:T(8,128)(2,1)}, bf16[1,48,32,128]{3,2,1,0:T(8,128)(2,1)S(1)}, u32[]{:S(2)}, u32[]{:S(2)}) collective-permute-start(bf16[1,48,32,128]{3,2,1,0:T(8,128)(2,1)} %get-tuple-element.48), channel_id=1, source_target_pairs={{0,8},{4,12},{8,0},{12,4},{16,24},{20,28},{24,16},{28,20},{1,9},{5... | collective-permute-start | bytes 1179656 | tf_op jit(solution)/shard_map/ppermute | solution.py:294
  420.5 31.0 %collective-permute-start.37 = (bf16[1,48,32,128]{3,2,1,0:T(8,128)(2,1)}, bf16[1,48,32,128]{3,2,1,0:T(8,128)(2,1)S(1)}, u32[]{:S(2)}, u32[]{:S(2)}) collective-permute-start(bf16[1,48,32,128]{3,2,1,0:T(8,128)(2,1)} %get-tuple-element.49), channel_id=1, source_target_pairs={{0,12},{4,8},{8,4},{12,0},{16,28},{20,24},{24,20},{28,16},{1,13},{... | collective-permute-start | bytes 1179656 | tf_op jit(solution)/shard_map/ppermute | solution.py:294
  422.0 29.6 %collective-permute-start.38 = (bf16[1,48,32,128]{3,2,1,0:T(8,128)(2,1)}, bf16[1,48,32,128]{3,2,1,0:T(8,128)(2,1)S(1)}, u32[]{:S(2)}, u32[]{:S(2)}) collective-permute-start(bf16[1,48,32,128]{3,2,1,0:T(8,128)(2,1)} %get-tuple-element.50), channel_id=1, source_target_pairs={{0,16},{4,20},{8,24},{12,28},{16,0},{20,4},{24,8},{28,12},{1,17},{... | collective-permute-start | bytes 1179656 | tf_op jit(solution)/shard_map/ppermute | solution.py:294
  424.4 52.1 %collective-permute-start.39 = (bf16[1,48,32,128]{3,2,1,0:T(8,128)(2,1)}, bf16[1,48,32,128]{3,2,1,0:T(8,128)(2,1)S(1)}, u32[]{:S(2)}, u32[]{:S(2)}) collective-permute-start(bf16[1,48,32,128]{3,2,1,0:T(8,128)(2,1)} %get-tuple-element.51), channel_id=1, source_target_pairs={{0,20},{4,16},{8,28},{12,24},{16,4},{20,0},{24,12},{28,8},{1,21},{... | collective-permute-start | bytes 1179656 | tf_op jit(solution)/shard_map/ppermute | solution.py:294
  429.9 55.0 %collective-permute-start.40 = (bf16[1,48,32,128]{3,2,1,0:T(8,128)(2,1)}, bf16[1,48,32,128]{3,2,1,0:T(8,128)(2,1)S(1)}, u32[]{:S(2)}, u32[]{:S(2)}) collective-permute-start(bf16[1,48,32,128]{3,2,1,0:T(8,128)(2,1)} %get-tuple-element.52), channel_id=1, source_target_pairs={{0,24},{4,28},{8,16},{12,20},{16,8},{20,12},{24,0},{28,4},{1,25},{... | collective-permute-start | bytes 1179656 | tf_op jit(solution)/shard_map/ppermute | solution.py:294
  445.5 67.1 %collective-permute-start.41 = (bf16[1,48,32,128]{3,2,1,0:T(8,128)(2,1)}, bf16[1,48,32,128]{3,2,1,0:T(8,128)(2,1)S(1)}, u32[]{:S(2)}, u32[]{:S(2)}) collective-permute-start(bf16[1,48,32,128]{3,2,1,0:T(8,128)(2,1)} %get-tuple-element.53), channel_id=1, source_target_pairs={{0,28},{4,24},{8,20},{12,16},{16,12},{20,8},{24,4},{28,0},{1,29},{... | collective-permute-start | bytes 1179656 | tf_op jit(solution)/shard_map/ppermute | solution.py:294
  451.6 61.0 %collective-permute-start.49 = (bf16[1,48,32,128]{3,2,1,0:T(8,128)(2,1)}, bf16[1,48,32,128]{3,2,1,0:T(8,128)(2,1)S(1)}, u32[]{:S(2)}, u32[]{:S(2)}) collective-permute-start(bf16[1,48,32,128]{3,2,1,0:T(8,128)(2,1)} %get-tuple-element.63), channel_id=1, source_target_pairs={{0,4},{4,0},{8,12},{12,8},{16,20},{20,16},{24,28},{28,24},{1,5},{5... | collective-permute-start | bytes 1179656 | tf_op jit(solution)/shard_map/ppermute | solution.py:294
  451.6 78.0 %collective-permute-start.50 = (bf16[1,48,32,128]{3,2,1,0:T(8,128)(2,1)}, bf16[1,48,32,128]{3,2,1,0:T(8,128)(2,1)S(1)}, u32[]{:S(2)}, u32[]{:S(2)}) collective-permute-start(bf16[1,48,32,128]{3,2,1,0:T(8,128)(2,1)} %get-tuple-element.64), channel_id=1, source_target_pairs={{0,8},{4,12},{8,0},{12,4},{16,24},{20,28},{24,16},{28,20},{1,9},{5... | collective-permute-start | bytes 1179656 | tf_op jit(solution)/shard_map/ppermute | solution.py:294
  476.5 55.2 %collective-permute-start.51 = (bf16[1,48,32,128]{3,2,1,0:T(8,128)(2,1)}, bf16[1,48,32,128]{3,2,1,0:T(8,128)(2,1)}, u32[]{:S(2)}, u32[]{:S(2)}) collective-permute-start(bf16[1,48,32,128]{3,2,1,0:T(8,128)(2,1)} %get-tuple-element.65), channel_id=1, source_target_pairs={{0,12},{4,8},{8,4},{12,0},{16,28},{20,24},{24,20},{28,16},{1,13},{... | collective-permute-start | bytes 1179656 | tf_op jit(solution)/shard_map/ppermute | solution.py:294
  484.9 47.7 %collective-permute-start.52 = (bf16[1,48,32,128]{3,2,1,0:T(8,128)(2,1)}, bf16[1,48,32,128]{3,2,1,0:T(8,128)(2,1)}, u32[]{:S(2)}, u32[]{:S(2)}) collective-permute-start(bf16[1,48,32,128]{3,2,1,0:T(8,128)(2,1)} %get-tuple-element.66), channel_id=1, source_target_pairs={{0,16},{4,20},{8,24},{12,28},{16,0},{20,4},{24,8},{28,12},{1,17},{... | collective-permute-start | bytes 1179656 | tf_op jit(solution)/shard_map/ppermute | solution.py:294
  512.6 32.6 %collective-permute-start.53 = (bf16[1,48,32,128]{3,2,1,0:T(8,128)(2,1)}, bf16[1,48,32,128]{3,2,1,0:T(8,128)(2,1)}, u32[]{:S(2)}, u32[]{:S(2)}) collective-permute-start(bf16[1,48,32,128]{3,2,1,0:T(8,128)(2,1)} %get-tuple-element.67), channel_id=1, source_target_pairs={{0,20},{4,16},{8,28},{12,24},{16,4},{20,0},{24,12},{28,8},{1,21},{... | collective-permute-start | bytes 1179656 | tf_op jit(solution)/shard_map/ppermute | solution.py:294
  512.6 41.5 %collective-permute-start.54 = (bf16[1,48,32,128]{3,2,1,0:T(8,128)(2,1)}, bf16[1,48,32,128]{3,2,1,0:T(8,128)(2,1)}, u32[]{:S(2)}, u32[]{:S(2)}) collective-permute-start(bf16[1,48,32,128]{3,2,1,0:T(8,128)(2,1)} %get-tuple-element.68), channel_id=1, source_target_pairs={{0,24},{4,28},{8,16},{12,20},{16,8},{20,12},{24,0},{28,4},{1,25},{... | collective-permute-start | bytes 1179656 | tf_op jit(solution)/shard_map/ppermute | solution.py:294
  530.3 30.0 %collective-permute-start.55 = (bf16[1,48,32,128]{3,2,1,0:T(8,128)(2,1)}, bf16[1,48,32,128]{3,2,1,0:T(8,128)(2,1)S(1)}, u32[]{:S(2)}, u32[]{:S(2)}) collective-permute-start(bf16[1,48,32,128]{3,2,1,0:T(8,128)(2,1)} %get-tuple-element.69), channel_id=1, source_target_pairs={{0,28},{4,24},{8,20},{12,16},{16,12},{20,8},{24,4},{28,0},{1,29},{... | collective-permute-start | bytes 1179656 | tf_op jit(solution)/shard_map/ppermute | solution.py:294
  531.7 28.6 %collective-permute-start.28 = (bf16[1,48,32,128]{3,2,1,0:T(8,128)(2,1)}, bf16[1,48,32,128]{3,2,1,0:T(8,128)(2,1)S(1)}, u32[]{:S(2)}, u32[]{:S(2)}) collective-permute-start(bf16[1,48,32,128]{3,2,1,0:T(8,128)(2,1)} %get-tuple-element.39), channel_id=1, source_target_pairs={{0,4},{4,0},{8,12},{12,8},{16,20},{20,16},{24,28},{28,24},{1,5},{5... | collective-permute-start | bytes 1179656 | tf_op jit(solution)/shard_map/ppermute | solution.py:294
  532.6 31.2 %collective-permute-start.29 = (bf16[1,48,32,128]{3,2,1,0:T(8,128)(2,1)}, bf16[1,48,32,128]{3,2,1,0:T(8,128)(2,1)S(1)}, u32[]{:S(2)}, u32[]{:S(2)}) collective-permute-start(bf16[1,48,32,128]{3,2,1,0:T(8,128)(2,1)} %get-tuple-element.40), channel_id=1, source_target_pairs={{0,8},{4,12},{8,0},{12,4},{16,24},{20,28},{24,16},{28,20},{1,9},{5... | collective-permute-start | bytes 1179656 | tf_op jit(solution)/shard_map/ppermute | solution.py:294
  545.2 19.1 %collective-permute-start.42 = (bf16[1,48,32,128]{3,2,1,0:T(8,128)(2,1)}, bf16[1,48,32,128]{3,2,1,0:T(8,128)(2,1)S(1)}, u32[]{:S(2)}, u32[]{:S(2)}) collective-permute-start(bf16[1,48,32,128]{3,2,1,0:T(8,128)(2,1)} %get-tuple-element.55), channel_id=1, source_target_pairs={{0,4},{4,0},{8,12},{12,8},{16,20},{20,16},{24,28},{28,24},{1,5},{5... | collective-permute-start | bytes 1179656 | tf_op jit(solution)/shard_map/ppermute | solution.py:294
  554.1 16.1 %collective-permute-start.43 = (bf16[1,48,32,128]{3,2,1,0:T(8,128)(2,1)}, bf16[1,48,32,128]{3,2,1,0:T(8,128)(2,1)S(1)}, u32[]{:S(2)}, u32[]{:S(2)}) collective-permute-start(bf16[1,48,32,128]{3,2,1,0:T(8,128)(2,1)} %get-tuple-element.56), channel_id=1, source_target_pairs={{0,8},{4,12},{8,0},{12,4},{16,24},{20,28},{24,16},{28,20},{1,9},{5... | collective-permute-start | bytes 1179656 | tf_op jit(solution)/shard_map/ppermute | solution.py:294
  554.2 113.5 %copy-start.41 = (bf16[1,48,32,128]{3,2,1,0:T(8,128)(2,1)S(1)}, bf16[1,48,32,128]{3,2,1,0:T(8,128)(2,1)}, u32[]{:S(2)}) copy-start(bf16[1,48,32,128]{3,2,1,0:T(8,128)(2,1)} %get-tuple-element.45) | copy-start | bytes 1179652
  554.3 104.1 %copy-start.42 = (bf16[1,48,32,128]{3,2,1,0:T(8,128)(2,1)S(1)}, bf16[1,48,32,128]{3,2,1,0:T(8,128)(2,1)}, u32[]{:S(2)}) copy-start(bf16[1,48,32,128]{3,2,1,0:T(8,128)(2,1)} %get-tuple-element.44) | copy-start | bytes 1179652
  560.3 109.4 %copy-start.14 = (bf16[1,48,32,128]{3,2,1,0:T(8,128)(2,1)}, bf16[1,48,32,128]{3,2,1,0:T(8,128)(2,1)S(1)}, u32[]{:S(2)}) copy-start(bf16[1,48,32,128]{3,2,1,0:T(8,128)(2,1)S(1)} %collective-permute-done.55.refs_16_) | copy-start | bytes 1179652
  560.3 18.6 %collective-permute-start.44 = (bf16[1,48,32,128]{3,2,1,0:T(8,128)(2,1)}, bf16[1,48,32,128]{3,2,1,0:T(8,128)(2,1)S(1)}, u32[]{:S(2)}, u32[]{:S(2)}) collective-permute-start(bf16[1,48,32,128]{3,2,1,0:T(8,128)(2,1)} %get-tuple-element.57), channel_id=1, source_target_pairs={{0,12},{4,8},{8,4},{12,0},{16,28},{20,24},{24,20},{28,16},{1,13},{... | collective-permute-start | bytes 1179656 | tf_op jit(solution)/shard_map/ppermute | solution.py:294
  560.3 140.5 %copy-start.12 = (bf16[1,48,32,128]{3,2,1,0:T(8,128)(2,1)}, bf16[1,48,32,128]{3,2,1,0:T(8,128)(2,1)S(1)}, u32[]{:S(2)}) copy-start(bf16[1,48,32,128]{3,2,1,0:T(8,128)(2,1)S(1)} %collective-permute-done.28.refs_2_) | copy-start | bytes 1179652
  560.4 47.1 %collective-permute-start.45 = (bf16[1,48,32,128]{3,2,1,0:T(8,128)(2,1)}, bf16[1,48,32,128]{3,2,1,0:T(8,128)(2,1)S(1)}, u32[]{:S(2)}, u32[]{:S(2)}) collective-permute-start(bf16[1,48,32,128]{3,2,1,0:T(8,128)(2,1)} %get-tuple-element.58), channel_id=1, source_target_pairs={{0,16},{4,20},{8,24},{12,28},{16,0},{20,4},{24,8},{28,12},{1,17},{... | collective-permute-start | bytes 1179656 | tf_op jit(solution)/shard_map/ppermute | solution.py:294
  563.9 137.0 %copy-start.13 = (bf16[1,48,32,128]{3,2,1,0:T(8,128)(2,1)}, bf16[1,48,32,128]{3,2,1,0:T(8,128)(2,1)S(1)}, u32[]{:S(2)}) copy-start(bf16[1,48,32,128]{3,2,1,0:T(8,128)(2,1)S(1)} %collective-permute-done.29.refs_3_) | copy-start | bytes 1179652
  563.9 73.1 %collective-permute-start.46 = (bf16[1,48,32,128]{3,2,1,0:T(8,128)(2,1)}, bf16[1,48,32,128]{3,2,1,0:T(8,128)(2,1)S(1)}, u32[]{:S(2)}, u32[]{:S(2)}) collective-permute-start(bf16[1,48,32,128]{3,2,1,0:T(8,128)(2,1)} %get-tuple-element.59), channel_id=1, source_target_pairs={{0,20},{4,16},{8,28},{12,24},{16,4},{20,0},{24,12},{28,8},{1,21},{... | collective-permute-start | bytes 1179656 | tf_op jit(solution)/shard_map/ppermute | solution.py:294
  564.3 105.4 %copy-start.15 = (bf16[1,48,32,128]{3,2,1,0:T(8,128)(2,1)}, bf16[1,48,32,128]{3,2,1,0:T(8,128)(2,1)S(1)}, u32[]{:S(2)}) copy-start(bf16[1,48,32,128]{3,2,1,0:T(8,128)(2,1)S(1)} %collective-permute-done.42.refs_2_) | copy-start | bytes 1179652
  564.3 94.0 %collective-permute-start.47 = (bf16[1,48,32,128]{3,2,1,0:T(8,128)(2,1)}, bf16[1,48,32,128]{3,2,1,0:T(8,128)(2,1)S(1)}, u32[]{:S(2)}, u32[]{:S(2)}) collective-permute-start(bf16[1,48,32,128]{3,2,1,0:T(8,128)(2,1)} %get-tuple-element.60), channel_id=1, source_target_pairs={{0,24},{4,28},{8,16},{12,20},{16,8},{20,12},{24,0},{28,4},{1,25},{... | collective-permute-start | bytes 1179656 | tf_op jit(solution)/shard_map/ppermute | solution.py:294
  570.2 97.5 %collective-permute-start.48 = (bf16[1,48,32,128]{3,2,1,0:T(8,128)(2,1)}, bf16[1,48,32,128]{3,2,1,0:T(8,128)(2,1)S(1)}, u32[]{:S(2)}, u32[]{:S(2)}) collective-permute-start(bf16[1,48,32,128]{3,2,1,0:T(8,128)(2,1)} %get-tuple-element.61), channel_id=1, source_target_pairs={{0,28},{4,24},{8,20},{12,16},{16,12},{20,8},{24,4},{28,0},{1,29},{... | collective-permute-start | bytes 1179656 | tf_op jit(solution)/shard_map/ppermute | solution.py:294
  579.0 121.9 %collective-permute-start.30 = (bf16[1,48,32,128]{3,2,1,0:T(8,128)(2,1)}, bf16[1,48,32,128]{3,2,1,0:T(8,128)(2,1)S(1)}, u32[]{:S(2)}, u32[]{:S(2)}) collective-permute-start(bf16[1,48,32,128]{3,2,1,0:T(8,128)(2,1)} %get-tuple-element.41), channel_id=1, source_target_pairs={{0,12},{4,8},{8,4},{12,0},{16,28},{20,24},{24,20},{28,16},{1,13},{... | collective-permute-start | bytes 1179656 | tf_op jit(solution)/shard_map/ppermute | solution.py:294
  607.5 93.4 %collective-permute-start.31 = (bf16[1,48,32,128]{3,2,1,0:T(8,128)(2,1)}, bf16[1,48,32,128]{3,2,1,0:T(8,128)(2,1)S(1)}, u32[]{:S(2)}, u32[]{:S(2)}) collective-permute-start(bf16[1,48,32,128]{3,2,1,0:T(8,128)(2,1)} %get-tuple-element.42), channel_id=1, source_target_pairs={{0,16},{4,20},{8,24},{12,28},{16,0},{20,4},{24,8},{28,12},{1,17},{... | collective-permute-start | bytes 1179656 | tf_op jit(solution)/shard_map/ppermute | solution.py:294
  637.0 63.9 %collective-permute-start.32 = (bf16[1,48,32,128]{3,2,1,0:T(8,128)(2,1)S(1)}, bf16[1,48,32,128]{3,2,1,0:T(8,128)(2,1)S(1)}, u32[]{:S(2)}, u32[]{:S(2)}) collective-permute-start(bf16[1,48,32,128]{3,2,1,0:T(8,128)(2,1)S(1)} %copy-done.43), channel_id=1, source_target_pairs={{0,20},{4,16},{8,28},{12,24},{16,4},{20,0},{24,12},{28,8},{1,21},{... | collective-permute-start | bytes 1179656 | tf_op jit(solution)/shard_map/ppermute | solution.py:294
  658.3 42.6 %collective-permute-start.33 = (bf16[1,48,32,128]{3,2,1,0:T(8,128)(2,1)S(1)}, bf16[1,48,32,128]{3,2,1,0:T(8,128)(2,1)S(1)}, u32[]{:S(2)}, u32[]{:S(2)}) collective-permute-start(bf16[1,48,32,128]{3,2,1,0:T(8,128)(2,1)S(1)} %copy-done.42), channel_id=1, source_target_pairs={{0,24},{4,28},{8,16},{12,20},{16,8},{20,12},{24,0},{28,4},{1,25},{... | collective-permute-start | bytes 1179656 | tf_op jit(solution)/shard_map/ppermute | solution.py:294
  667.7 33.2 %collective-permute-start.34 = (bf16[1,48,32,128]{3,2,1,0:T(8,128)(2,1)S(1)}, bf16[1,48,32,128]{3,2,1,0:T(8,128)(2,1)S(1)}, u32[]{:S(2)}, u32[]{:S(2)}) collective-permute-start(bf16[1,48,32,128]{3,2,1,0:T(8,128)(2,1)S(1)} %copy-done.41), channel_id=1, source_target_pairs={{0,28},{4,24},{8,20},{12,16},{16,12},{20,8},{24,4},{28,0},{1,29},{... | collective-permute-start | bytes 1179656 | tf_op jit(solution)/shard_map/ppermute | solution.py:294
  (46 other events, 1381.2 us)
Sparse Core Ops, SparseCore 0:
  329.7 34.1 all-reduce.2
  366.8 33.4 all-reduce.4

commit v2 on v1

--- a/solution.py
+++ b/solution.py
@@ -33,7 +33,8 @@
     return jnp.where(offset < full.shape[1] - wave, full, 0.0)
 
 
-def synth_kernel(first, rb, pair, waves, coef, table, spread, out, work):
+def synth_kernel(first, rb, pair, waves, coef, table, spread, *outs_and_work):
+    *outs, work = outs_and_work
     block, inner = pl.program_id(0), pl.program_id(1)
     ns = spread.shape[0]
     fields = []
@@ -48,10 +49,14 @@
 
     @pl.when(inner == pl.num_programs(1) - 1)
     def _():
-        out[...] = work[...].reshape(ns, rb, lanes).astype(BF16)
-
-
-def synth(own_waves, coef, table, spread, first, count):
+        at = 0
+        for out in outs:
+            size = out.shape[0] * out.shape[1] * rb
+            out[...] = work[at : at + size, :].reshape(out.shape).astype(BF16)
+            at += size
+
+
+def synth(own_waves, coef, table, spread, first, count, shapes):
     parts, rows, members, levels, nwave = coef.shape
     lat = table.shape[2]
     ns = spread.shape[0]
@@ -73,14 +78,16 @@
                 pl.BlockSpec((pair, nwave, lat), lambda b, i, w: (base + b * inner + i, 0, 0)),
                 pl.BlockSpec((ns, lat), lambda b, i, w: (0, 0)),
             ],
-            out_specs=pl.BlockSpec((ns, rb, lanes), lambda b, i, w: (0, b, 0)),
+            out_specs=[
+                pl.BlockSpec((m, sq, rb, lanes), lambda b, i, w: (0, 0, b, 0)) for m, sq in shapes
+            ],
             scratch_shapes=[pltpu.VMEM((ns * rb, lanes), F32)],
         ),
-        out_shape=jax.ShapeDtypeStruct((ns, count, lanes), BF16),
+        out_shape=[jax.ShapeDtypeStruct((m, sq, count, lanes), BF16) for m, sq in shapes],
         compiler_params=pltpu.CompilerParams(vmem_limit_bytes=VMEM_LIMIT),
         cost_estimate=pl.CostEstimate(
-            flops=2 * count * lanes * lat * (nwave + ns),
-            bytes_accessed=count * (nwave * lat * 2 + lanes * nwave * 4 + lanes * ns * 2),
+            flops=int(0.1 * 2 * count * lanes * lat * (nwave + ns)),
+            bytes_accessed=int(0.1 * (count * (nwave * lat * 2 + lanes * nwave * 4 + lanes * ns * 2))),
             transcendentals=0,
         ),
     )(own_waves, coef, table, spread)
@@ -162,8 +169,8 @@
         input_output_aliases={n + 4: 0} if into else {},
         compiler_params=pltpu.CompilerParams(vmem_limit_bytes=VMEM_LIMIT),
         cost_estimate=pl.CostEstimate(
-            flops=2 * count * lanes * lat * (nwave + ns),
-            bytes_accessed=count * (nwave * lat * 2 + lanes * nwave * 8 + lanes * ns * 2),
+            flops=int(0.1 * 2 * count * lanes * lat * (nwave + ns)),
+            bytes_accessed=int(0.1 * (count * (nwave * lat * 2 + lanes * nwave * 8 + lanes * ns * 2))),
             transcendentals=0,
         ),
     )(own_waves, *received, coef, table, spread, *into)
@@ -208,8 +215,8 @@
         scratch_shapes=[pltpu.VMEM((sb * levels * members, kdim), BF16)],
         compiler_params=pltpu.CompilerParams(vmem_limit_bytes=VMEM_LIMIT),
         cost_estimate=pl.CostEstimate(
-            flops=2 * sq * levels * members * kdim * lon,
-            bytes_accessed=sq * levels * members * (lon + kdim) * 2 + kdim * lon * 2,
+            flops=int(0.1 * 2 * sq * levels * members * kdim * lon),
+            bytes_accessed=int(0.1 * (sq * levels * members * (lon + kdim) * 2 + kdim * lon * 2)),
             transcendentals=0,
         ),
     )(*received, perturb, fourier)
@@ -251,8 +258,8 @@
         out_shape=[jax.ShapeDtypeStruct((m, sq, rows, lanes), BF16) for m, rows in shapes],
         compiler_params=pltpu.CompilerParams(vmem_limit_bytes=VMEM_LIMIT),
         cost_estimate=pl.CostEstimate(
-            flops=2 * sq * levels * members * kdim * lon,
-            bytes_accessed=sq * levels * members * (lon + kdim) * 2 + kdim * lon * 2,
+            flops=int(0.1 * 2 * sq * levels * members * kdim * lon),
+            bytes_accessed=int(0.1 * (sq * levels * members * (lon + kdim) * 2 + kdim * lon * 2)),
             transcendentals=0,
         ),
     )(perturb, gradient, fourier)
@@ -277,9 +284,8 @@
     own_waves = lax.dynamic_slice_in_dim(wave_map, me * rows, rows)
 
     natural = jnp.arange(bands * lat_rows, dtype=jnp.int32)
-    spread = (lats_in_order.reshape(-1)[:, None] == natural[None, :]).astype(BF16)
     by_chunk = lats_in_order.reshape(bands, chunks, sq).transpose(1, 0, 2).reshape(-1)
-    gather = (by_chunk[:, None] == natural[None, :]).astype(BF16)
+    spread = (by_chunk[:, None] == natural[None, :]).astype(BF16)
 
     wave_order = waves_in_order.reshape(-1)
     columns = jnp.arange(lon, dtype=jnp.int32)
@@ -290,53 +296,81 @@
 
     perturb = perturb.transpose(0, 2, 1, 3)
 
-    def send(block, hop):
-        return lax.ppermute(block, "band", [(d, d ^ hop) for d in range(bands)])
-
-    hops = sorted(range(bands), reverse=True)
-
-    sent = [synth(own_waves, coef, table, spread, h * rh, rh) for h in range(halves)]
-    arrived = []
+    if pairwise:
+        far, near = list(range(bands // 2, bands)), [None, *range(1, bands // 2)]
+        hops = [hop for pair in zip(far, near) for hop in pair if hop is not None]
+        keys = [(h, hop) for h in range(halves) for hop in reversed(hops)]
+        pieces = bands
+    else:
+        keys, pieces = [(h, 0) for h in range(halves)], 1
+    deep = bands // pieces
+
+    def send(blocks, key):
+        if pairwise:
+            hop = key[1]
+            blocks[key] = lax.ppermute(blocks[key], "band", [(d, d ^ hop) for d in range(bands)])
+        else:
+            blocks[key] = lax.all_to_all(
+                blocks[key], "band", split_axis=0, concat_axis=0, tiled=True
+            )
+
+    def hold(blocks, these, *others):
+        these = list(these)
+        out = lax.optimization_barrier((*[blocks[key] for key in these], *others))
+        for key, block in zip(these, out):
+            blocks[key] = block
+        return out[len(these) :]
+
+    def by_wave(blocks):
+        return [blocks[h, p] for p in range(pieces) for h in range(halves)]
+
+    def grid(q, blocks):
+        return to_grid(by_wave(blocks), perturb, fourier, q * sq, sq, scale)
+
+    def adjoint(q, increment):
+        gradient = weight[q * sq : (q + 1) * sq] * increment
+        shapes = [(deep, rh) for _ in range(pieces) for _ in range(halves)]
+        outs = from_grid(perturb, gradient, fourier, q * sq, sq, shapes, scale)
+        return {(h, p): outs[p * halves + h] for p in range(pieces) for h in range(halves)}
+
+    per_half = len(keys) // halves
+    flight = 5
+    out_blocks = [{} for _ in range(chunks)]
+    for h in range(halves):
+        shapes = [(deep, sq)] * (chunks * pieces)
+        outs = synth(own_waves, coef, table, spread, h * rh, rh, shapes)
+        for q in range(chunks):
+            for p in range(pieces):
+                out_blocks[q][h, p] = outs[q * pieces + p]
+    if len(keys) > per_half + 2:
+        perturb, fourier = hold(out_blocks[0], keys[per_half + 2 :], perturb, fourier)
+
+    increments, flights = [], list(out_blocks)
+    sent = 0
     for q in range(chunks):
-        got = {}
-        for h in range(halves):
-            blocks = sent[h].reshape(bands, lat_rows, rh, -1)[:, q * sq : (q + 1) * sq]
-            if pairwise:
-                for hop in hops:
-                    block = blocks[hop : hop + 1]
-                    got[hop, h] = send(block, hop) if hop else block
-            else:
-                got[0, h] = lax.all_to_all(blocks, "band", split_axis=0, concat_axis=0, tiled=True)
-        arrived.append([got[key] for key in sorted(got)])
-
-    increments, returned = [], []
-    for q in range(chunks):
-        part = to_grid(arrived[q], perturb, fourier, q * sq, sq, scale)
-        if increments:
-            part, increments[-1] = lax.optimization_barrier((part, increments[-1]))
+        while sent <= q:
+            for key in keys:
+                send(flights[sent], key)
+            sent += 1
+        after = flights[sent] if sent < len(flights) else {}
+        part = grid(q, flights[q])
+        if after:
+            (part,) = hold(after, keys[9:], part)
         increment = lax.psum(part, "mem")
         increments.append(increment)
-        gradient = weight[q * sq : (q + 1) * sq] * increment
-        shapes = [(a.shape[0], a.shape[2]) for a in arrived[q]]
-        outs = from_grid(perturb, gradient, fourier, q * sq, sq, shapes, scale)
-        got = {}
-        for h in range(halves):
-            if pairwise:
-                for hop in hops:
-                    block = outs[hop * halves + h]
-                    got[h, hop] = send(block, hop) if hop else block
-            else:
-                got[h, 0] = lax.all_to_all(outs[h], "band", split_axis=0, concat_axis=0, tiled=True)
-        returned.append(got)
+        back = adjoint(q, increment)
+        if after:
+            back = dict(zip(back, hold(after, keys[12 :], *back.values())))
+        flights.append(back)
+    for blocks in flights[sent:]:
+        for key in keys:
+            send(blocks, key)
+    back_blocks = flights[chunks:]
 
     product = None
     for h in range(halves):
-        received = [
-            returned[q][h, hop]
-            for q in range(chunks)
-            for hop in range(bands if pairwise else 1)
-        ]
-        product = analyse(own_waves, received, coef, table, gather, h * rh, rh, product)
+        received = [back_blocks[q][h, p] for q in range(chunks) for p in range(pieces)]
+        product = analyse(own_waves, received, coef, table, spread, h * rh, rh, product)
     increment = jnp.concatenate(increments, axis=0) if chunks > 1 else increments[0]
     return (increment, product)
 

time: 742 us -> 654 us (0.88)
  waiting for transfers between devices: 397 us -> 323 us
  local copies, waits for them, and re-layouts: 36.3 us -> 23.8 us
    ppermute x56, waiting for transfers between devices: 344 us -> 270 us  [send(): lax.ppermute(blocks[key], 'band', [(d, d ^ hop) for d in range(bands)])]
    slice x2 -> x0, local copies, waits for them, and re-layouts: 10.6 us -> none  [body(): block = blocks[hop:hop + 1]]
    unnamed x105 -> x129, local copies, waits for them, and re-layouts: 23.3 us -> 21.5 us
  transfers between devices with their start and end apart: 58 -> 58, of which waited for: 28 -> 23; matrix products, arithmetic and copies ran while one was open for 6% -> 6% of each run, Pallas kernels for 14% -> 18%
where the time goes in v2:
time: 654 us; the launch traced here: 652 us
  waiting for transfers between devices  323 us (49%)
  Pallas kernels  177 us (27%)
  starting transfers between devices  90.1 us (14%)
  local copies, waits for them, and re-layouts  23.8 us (4%)
  other arithmetic  23.1 us (4%)
  between operations  14.8 us (2%)
    ppermute x56, waiting for transfers between devices, send(): lax.ppermute(blocks[key], 'band', [(d, d ^ hop) for d in range(bands)])  270 us
    ppermute x56, starting transfers between devices, send(): lax.ppermute(blocks[key], 'band', [(d, d ^ hop) for d in range(bands)])  90 us
    pallas_call x2, Pallas kernels, analyse(): pl.pallas_call(functools.partial(analyse_kernel, n, first, rb, pair), gri...  62 us
    pallas_call x2, Pallas kernels, synth(): pl.pallas_call(functools.partial(synth_kernel, first, rb, pair), grid_spe...  53.6 us
    psum x2, waiting for transfers between devices, body(): increment = lax.psum(part, 'mem')  52.5 us
    pallas_call x2, Pallas kernels, from_grid(): pl.pallas_call(functools.partial(adjoint_kernel, len(shapes), scale), gri...  30.8 us
    pallas_call x2, Pallas kernels, to_grid(): pl.pallas_call(functools.partial(grid_kernel, len(received), scale), grid...  30.5 us
    unnamed x129, local copies, waits for them, and re-layouts  21.5 us
  transfers between devices with their start and end apart: 58, of which 23 were waited for; matrix products, arithmetic and copies ran while one was open for 6% of the time, Pallas kernels for 18%

profile of v2, /device:TPU:8, one launch (start us, length us, event | category | flops | bytes accessed | tf_op | source)
XLA Modules:
  0.0 651.6 jit_solution(7193159592229408455)
XLA Ops:
  10.9 26.8 %shard_map.78 = (bf16[1,48,32,128]{3,2,1,0:T(8,128)(2,1)}, bf16[1,48,32,128]{3,2,1,0:T(8,128)(2,1)}, bf16[1,48,32,128]{3,2,1,0:T(8,128)(2,1)}, bf16[1,48,32,128]...) custom-call(s32[64]{0:T(128)} %dynamic_slice.3.waves.refs_0_, ...), custom_call_target="tpu_custom_call" | custom-call | flops 805306368 | bytes 3984588 | tf_op jit(solution)/shard_map/pallas_call | solution.py:68
  37.7 1.6 collective-permute-start
  39.7 1.5 collective-permute-start.4
  41.3 2.6 collective-permute-start.6
  45.4 26.7 %shard_map.77 = (bf16[1,48,32,128]{3,2,1,0:T(8,128)(2,1)}, bf16[1,48,32,128]{3,2,1,0:T(8,128)(2,1)}, bf16[1,48,32,128]{3,2,1,0:T(8,128)(2,1)}, bf16[1,48,32,128]...) custom-call(s32[64]{0:T(128)} %dynamic_slice.3.waves.refs_0_, ...), custom_call_target="tpu_custom_call" | custom-call | flops 805306368 | bytes 3984588 | tf_op jit(solution)/shard_map/pallas_call | solution.py:68
  72.1 1.6 collective-permute-start.10
  74.2 3.2 collective-permute-start.5
  77.4 2.7 collective-permute-start.13
  80.1 13.8 %multiply_convert_fusion.1 = (bf16[512,1536]{1,0:T(8,128)(2,1)S(1)}, bf16[512,1536]{1,0:T(8,128)(2,1)S(1)}) fusion(s32[512]{0:T(512)S(1)} %reshape.53, f32[512]{0:T(512)S(1)} %get-tuple-element.242, f32[512]{0:T(512)S(1)} %get-tuple-element.243), kind=kLoop, calls=%fused_computation.6 | loop fusion | flops 10223616 | bytes 3151872 | tf_op jit(solution)/shard_map/convert
  93.9 18.9 %copy.16 = bf16[96,32,2,1536]{3,1,2,0:T(8,128)(2,1)} copy(bf16[96,32,2,1536]{3,2,1,0:T(2,128)(2,1)} %param.7) | data formatting | bytes 37748736 | tf_op args[1]
  112.9 1.9 pad_maximum_fusion.refs_17_.fourier
  114.7 1.5 collective-permute-start.1
  116.4 4.8 collective-permute-done.12.refs_14_
  121.3 3.8 collective-permute-start.9
  125.0 29.9 %collective-permute-done.13.refs_15_ = bf16[1,48,32,128]{3,2,1,0:T(8,128)(2,1)S(1)} collective-permute-done((bf16[1,48,32,128]{3,2,1,0:T(8,128)(2,1)}, bf16[1,48,32,128]{3,2,1,0:T(8,128)(2,1)S(1)}, u32[]{:S(2)}, u32[]{:S(2)}) %collective-permute-start.13) | collective-permute-done | bytes 393248 | tf_op jit(solution)/shard_map/ppermute | solution.py:311
  155.0 3.3 collective-permute-start.11
  158.9 4.4 collective-permute-done.7.refs_9_
  164.7 7.4 %collective-permute-done.9.refs_11_ = bf16[1,48,32,128]{3,2,1,0:T(8,128)(2,1)S(1)} collective-permute-done((bf16[1,48,32,128]{3,2,1,0:T(8,128)(2,1)S(1)}, bf16[1,48,32,128]{3,2,1,0:T(8,128)(2,1)S(1)}, u32[]{:S(2)}, u32[]{:S(2)}) %collective-permute-start.9) | collective-permute-done | bytes 393248 | tf_op jit(solution)/shard_map/ppermute | solution.py:311
  172.1 4.7 collective-permute-start.20
  176.8 11.8 %collective-permute-done.11.refs_13_ = bf16[1,48,32,128]{3,2,1,0:T(8,128)(2,1)S(1)} collective-permute-done((bf16[1,48,32,128]{3,2,1,0:T(8,128)(2,1)S(1)}, bf16[1,48,32,128]{3,2,1,0:T(8,128)(2,1)S(1)}, u32[]{:S(2)}, u32[]{:S(2)}) %collective-permute-start.11) | collective-permute-done | bytes 393248 | tf_op jit(solution)/shard_map/ppermute | solution.py:311
  189.4 15.3 %shard_map.79 = f32[48,2,1536]{2,1,0:T(2,128)} custom-call(bf16[1,48,32,128]{3,2,1,0:T(8,128)(2,1)} %get-tuple-element.126.refs_0_, bf16[1,48,32,128]{3,2,1,0:T(8,128)(2,1)} %get-tuple-element.127.refs_1_, bf16[1,48,32,128]{3,2,1,0:T(8,128)(2,1)} %copy-done.17, bf16[1,48,32,128]{3,2,1,0:T(8,128)(2,1)} %copy-done.39, bf16[1,48,32,128]{3,2,1,0:T(8,128)(2,1)} %copy-done.20, ...), custom_call_target="tpu_custom_call" | custom-call | flops 966367616 | bytes 1887436 | tf_op jit(solution)/shard_map/pallas_call | solution.py:203
  204.8 2.5 collective-permute-start.24
  208.4 6.0 collective-permute-start.19
  214.4 24.9 %all-reduce.3.cloned.1.call-done = f32[48,2,1536]{2,1,0:T(2,128)} async-done(((f32[48,2,1536]{2,1,0:T(2,128)}), f32[48,2,1536]{2,1,0:T(2,128)}) %all-reduce.3.cloned.1.call-update) | async-done | bytes 589840 | tf_op jit(solution)/shard_map/psum | solution.py:359
  239.3 2.2 slice_multiply_fusion.1.gradient
  241.5 2.1 collective-permute-done.22.refs_10_
  244.1 12.8 %collective-permute-done.24.refs_12_ = bf16[1,48,32,128]{3,2,1,0:T(8,128)(2,1)S(1)} collective-permute-done((bf16[1,48,32,128]{3,2,1,0:T(8,128)(2,1)}, bf16[1,48,32,128]{3,2,1,0:T(8,128)(2,1)S(1)}, u32[]{:S(2)}, u32[]{:S(2)}) %collective-permute-start.24) | collective-permute-done | bytes 393248 | tf_op jit(solution)/shard_map/ppermute | solution.py:311
  256.9 17.9 %collective-permute-done.26.refs_14_ = bf16[1,48,32,128]{3,2,1,0:T(8,128)(2,1)} collective-permute-done((bf16[1,48,32,128]{3,2,1,0:T(8,128)(2,1)}, bf16[1,48,32,128]{3,2,1,0:T(8,128)(2,1)}, u32[]{:S(2)}, u32[]{:S(2)}) %collective-permute-start.26) | collective-permute-done | bytes 393248 | tf_op jit(solution)/shard_map/ppermute | solution.py:311
  275.7 15.4 %shard_map.80 = (bf16[1,48,32,128]{3,2,1,0:T(8,128)(2,1)}, bf16[1,48,32,128]{3,2,1,0:T(8,128)(2,1)}, bf16[1,48,32,128]{3,2,1,0:T(8,128)(2,1)}, bf16[1,48,32,128]...) custom-call(bf16[96,2,32,1536]{3,2,1,0:T(8,128)(2,1)} %bitcast.5, ...), custom_call_target="tpu_custom_call" | custom-call | flops 966367616 | bytes 1887436 | tf_op jit(solution)/shard_map/pallas_call | solution.py:249
  291.2 3.8 collective-permute-start.23
  295.1 1.5 collective-permute-start.34
  296.6 15.1 %collective-permute-done.25.refs_13_ = bf16[1,48,32,128]{3,2,1,0:T(8,128)(2,1)S(1)} collective-permute-done((bf16[1,48,32,128]{3,2,1,0:T(8,128)(2,1)}, bf16[1,48,32,128]{3,2,1,0:T(8,128)(2,1)S(1)}, u32[]{:S(2)}, u32[]{:S(2)}) %collective-permute-start.25) | collective-permute-done | bytes 393248 | tf_op jit(solution)/shard_map/ppermute | solution.py:311
  311.7 1.5 collective-permute-start.42
  313.2 10.5 %collective-permute-done.21.refs_9_ = bf16[1,48,32,128]{3,2,1,0:T(8,128)(2,1)S(1)} collective-permute-done((bf16[1,48,32,128]{3,2,1,0:T(8,128)(2,1)S(1)}, bf16[1,48,32,128]{3,2,1,0:T(8,128)(2,1)S(1)}, u32[]{:S(2)}, u32[]{:S(2)}) %collective-permute-start.21) | collective-permute-done | bytes 393248 | tf_op jit(solution)/shard_map/ppermute | solution.py:311
  323.7 8.4 %collective-permute-done.23.refs_11_ = bf16[1,48,32,128]{3,2,1,0:T(8,128)(2,1)S(1)} collective-permute-done((bf16[1,48,32,128]{3,2,1,0:T(8,128)(2,1)S(1)}, bf16[1,48,32,128]{3,2,1,0:T(8,128)(2,1)S(1)}, u32[]{:S(2)}, u32[]{:S(2)}) %collective-permute-start.23) | collective-permute-done | bytes 393248 | tf_op jit(solution)/shard_map/ppermute | solution.py:311
  332.9 15.3 %shard_map.81 = f32[48,2,1536]{2,1,0:T(2,128)} custom-call(bf16[1,48,32,128]{3,2,1,0:T(8,128)(2,1)} %get-tuple-element.173.refs_0_, bf16[1,48,32,128]{3,2,1,0:T(8,128)(2,1)} %get-tuple-element.174.refs_1_, bf16[1,48,32,128]{3,2,1,0:T(8,128)(2,1)} %copy-done.9, bf16[1,48,32,128]{3,2,1,0:T(8,128)(2,1)} %copy-done.33, bf16[1,48,32,128]{3,2,1,0:T(8,128)(2,1)} %copy-done.11, ...), custom_call_target="tpu_custom_call" | custom-call | flops 966367616 | bytes 1887436 | tf_op jit(solution)/shard_map/pallas_call | solution.py:203
  348.2 3.1 collective-permute-start.43
  351.4 3.2 collective-permute-start.45
  356.1 27.6 %all-reduce.5.cloned.1.call-done = f32[48,2,1536]{2,1,0:T(2,128)} async-done(((f32[48,2,1536]{2,1,0:T(2,128)}), f32[48,2,1536]{2,1,0:T(2,128)}) %all-reduce.5.cloned.1.call-update) | async-done | bytes 589840 | tf_op jit(solution)/shard_map/psum | solution.py:359
  383.7 2.2 slice_multiply_fusion.gradient
  386.0 15.4 %shard_map.82 = (bf16[1,48,32,128]{3,2,1,0:T(8,128)(2,1)}, bf16[1,48,32,128]{3,2,1,0:T(8,128)(2,1)}, bf16[1,48,32,128]{3,2,1,0:T(8,128)(2,1)}, bf16[1,48,32,128]...) custom-call(bf16[96,2,32,1536]{3,2,1,0:T(8,128)(2,1)} %bitcast.7, ...), custom_call_target="tpu_custom_call" | custom-call | flops 966367616 | bytes 1887436 | tf_op jit(solution)/shard_map/pallas_call | solution.py:249
  401.4 2.5 collective-permute-start.48
  404.5 2.6 collective-permute-start.29
  407.2 2.4 collective-permute-start.31
  409.6 33.0 %collective-permute-done.48.refs_8_ = bf16[1,48,32,128]{3,2,1,0:T(8,128)(2,1)S(1)} collective-permute-done((bf16[1,48,32,128]{3,2,1,0:T(8,128)(2,1)S(1)}, bf16[1,48,32,128]{3,2,1,0:T(8,128)(2,1)S(1)}, u32[]{:S(2)}, u32[]{:S(2)}) %collective-permute-start.48) | collective-permute-done | bytes 393248 | tf_op jit(solution)/shard_map/ppermute | solution.py:311
  442.9 12.8 %collective-permute-done.33.refs_7_ = bf16[1,48,32,128]{3,2,1,0:T(8,128)(2,1)S(1)} collective-permute-done((bf16[1,48,32,128]{3,2,1,0:T(8,128)(2,1)S(1)}, bf16[1,48,32,128]{3,2,1,0:T(8,128)(2,1)S(1)}, u32[]{:S(2)}, u32[]{:S(2)}) %collective-permute-start.33) | collective-permute-done | bytes 393248 | tf_op jit(solution)/shard_map/ppermute | solution.py:311
  456.0 7.9 %collective-permute-done.31.refs_5_ = bf16[1,48,32,128]{3,2,1,0:T(8,128)(2,1)S(1)} collective-permute-done((bf16[1,48,32,128]{3,2,1,0:T(8,128)(2,1)S(1)}, bf16[1,48,32,128]{3,2,1,0:T(8,128)(2,1)S(1)}, u32[]{:S(2)}, u32[]{:S(2)}) %collective-permute-start.31) | collective-permute-done | bytes 393248 | tf_op jit(solution)/shard_map/ppermute | solution.py:311
  463.8 1.7 collective-permute-start.50
  465.6 4.9 collective-permute-done.32.refs_6_
  470.5 3.5 collective-permute-start.51
  474.1 2.9 collective-permute-start.53
  478.4 7.7 %collective-permute-done.50.refs_11_ = bf16[1,48,32,128]{3,2,1,0:T(8,128)(2,1)S(1)} collective-permute-done((bf16[1,48,32,128]{3,2,1,0:T(8,128)(2,1)}, bf16[1,48,32,128]{3,2,1,0:T(8,128)(2,1)S(1)}, u32[]{:S(2)}, u32[]{:S(2)}) %collective-permute-start.50) | collective-permute-done | bytes 393248 | tf_op jit(solution)/shard_map/ppermute | solution.py:311
  486.1 2.3 collective-permute-start.55
  488.3 6.1 collective-permute-done.51.refs_12_
  494.4 3.3 collective-permute-start.37
  497.7 20.0 %collective-permute-done.52.refs_13_ = bf16[1,48,32,128]{3,2,1,0:T(8,128)(2,1)S(1)} collective-permute-done((bf16[1,48,32,128]{3,2,1,0:T(8,128)(2,1)}, bf16[1,48,32,128]{3,2,1,0:T(8,128)(2,1)S(1)}, u32[]{:S(2)}, u32[]{:S(2)}) %collective-permute-start.52) | collective-permute-done | bytes 393248 | tf_op jit(solution)/shard_map/ppermute | solution.py:311
  517.7 3.3 collective-permute-start.38
  521.0 26.2 %collective-permute-done.53.refs_14_ = bf16[1,48,32,128]{3,2,1,0:T(8,128)(2,1)S(1)} collective-permute-done((bf16[1,48,32,128]{3,2,1,0:T(8,128)(2,1)}, bf16[1,48,32,128]{3,2,1,0:T(8,128)(2,1)S(1)}, u32[]{:S(2)}, u32[]{:S(2)}) %collective-permute-start.53) | collective-permute-done | bytes 393248 | tf_op jit(solution)/shard_map/ppermute | solution.py:311
  547.2 4.2 collective-permute-start.39
  551.4 18.7 %collective-permute-done.54.refs_15_ = bf16[1,48,32,128]{3,2,1,0:T(8,128)(2,1)} collective-permute-done((bf16[1,48,32,128]{3,2,1,0:T(8,128)(2,1)}, bf16[1,48,32,128]{3,2,1,0:T(8,128)(2,1)}, u32[]{:S(2)}, u32[]{:S(2)}) %collective-permute-start.54) | collective-permute-done | bytes 393248 | tf_op jit(solution)/shard_map/ppermute | solution.py:311
  570.7 7.8 %collective-permute-done.55.refs_16_ = bf16[1,48,32,128]{3,2,1,0:T(8,128)(2,1)} collective-permute-done((bf16[1,48,32,128]{3,2,1,0:T(8,128)(2,1)}, bf16[1,48,32,128]{3,2,1,0:T(8,128)(2,1)}, u32[]{:S(2)}, u32[]{:S(2)}) %collective-permute-start.55) | collective-permute-done | bytes 393248 | tf_op jit(solution)/shard_map/ppermute | solution.py:311
  580.1 1.5 pad_maximum_fusion.1
  581.6 31.0 %shard_map.83.refs_20_ = f32[2,64,32,2,512]{4,3,2,1,0:T(2,128)} custom-call(s32[64]{0:T(128)} %dynamic_slice.3.waves.refs_0_, bf16[1,48,32,128]{3,2,1,0:T(8,128)(2,1)} %get-tuple-element.224.refs_1_, bf16[1,48,32,128]{3,2,1,0:T(8,128)(2,1)} %copy-done.5, bf16[1,48,32,128]{3,2,1,0:T(8,128)(2,1)} %copy-done.6, bf16[1,48,32,128]{3,2,1,0:T(8,128)(2,1)} %copy-done.7, ...), custom_call_target="tpu_custom_call" | custom-call | flops 805306368 | bytes 4823449 | tf_op jit(solution)/shard_map/pallas_call | solution.py:144
  613.7 31.0 %shard_map.84 = f32[2,64,32,2,512]{4,3,2,1,0:T(2,128)} custom-call(s32[64]{0:T(128)} %dynamic_slice.3.waves.refs_0_, bf16[1,48,32,128]{3,2,1,0:T(8,128)(2,1)} %get-tuple-element.190.refs_1_, bf16[1,48,32,128]{3,2,1,0:T(8,128)(2,1)} %copy-done.10, bf16[1,48,32,128]{3,2,1,0:T(8,128)(2,1)} %copy-done.12, ...), custom_call_target="tpu_custom_call", output_to_operand_aliasing={{}: (20, {})} | custom-call | flops 805306368 | bytes 4823449 | tf_op jit(solution)/shard_map/pallas_call | solution.py:144
  (209 shorter events, 19.9 us)
Async XLA Ops:
  7.2 232.2 %all-reduce.3.cloned.1.call-start = ((), (), s32[]{:S(2)}) async-start(), calls=%async_computation | async-start | bytes 1179648 | tf_op jit(solution)/shard_map/psum | solution.py:359
  37.7 34.4 %collective-permute-start = (bf16[1,48,32,128]{3,2,1,0:T(8,128)(2,1)}, bf16[1,48,32,128]{3,2,1,0:T(8,128)(2,1)S(1)}, u32[]{:S(2)}, u32[]{:S(2)}) collective-permute-start(bf16[1,48,32,128]{3,2,1,0:T(8,128)(2,1)} %get-tuple-element.128), channel_id=1, source_target_pairs={{0,4},{4,0},{8,12},{12,8},{16,20},{20,16},{24,28},{28,24},{1,5},{5... | collective-permute-start | bytes 1179656 | tf_op jit(solution)/shard_map/ppermute | solution.py:311
  39.3 34.5 %collective-permute-start.2 = (bf16[1,48,32,128]{3,2,1,0:T(8,128)(2,1)}, bf16[1,48,32,128]{3,2,1,0:T(8,128)(2,1)S(1)}, u32[]{:S(2)}, u32[]{:S(2)}) collective-permute-start(bf16[1,48,32,128]{3,2,1,0:T(8,128)(2,1)} %get-tuple-element.135), channel_id=1, source_target_pairs={{0,8},{4,12},{8,0},{12,4},{16,24},{20,28},{24,16},{28,20},{1,9},{5... | collective-permute-start | bytes 1179656 | tf_op jit(solution)/shard_map/ppermute | solution.py:311
  39.7 34.5 %collective-permute-start.4 = (bf16[1,48,32,128]{3,2,1,0:T(8,128)(2,1)}, bf16[1,48,32,128]{3,2,1,0:T(8,128)(2,1)S(1)}, u32[]{:S(2)}, u32[]{:S(2)}) collective-permute-start(bf16[1,48,32,128]{3,2,1,0:T(8,128)(2,1)} %get-tuple-element.137), channel_id=1, source_target_pairs={{0,12},{4,8},{8,4},{12,0},{16,28},{20,24},{24,20},{28,16},{1,13},{... | collective-permute-start | bytes 1179656 | tf_op jit(solution)/shard_map/ppermute | solution.py:311
  41.3 36.1 %collective-permute-start.6 = (bf16[1,48,32,128]{3,2,1,0:T(8,128)(2,1)}, bf16[1,48,32,128]{3,2,1,0:T(8,128)(2,1)S(1)}, u32[]{:S(2)}, u32[]{:S(2)}) collective-permute-start(bf16[1,48,32,128]{3,2,1,0:T(8,128)(2,1)} %get-tuple-element.139), channel_id=1, source_target_pairs={{0,16},{4,20},{8,24},{12,28},{16,0},{20,4},{24,8},{28,12},{1,17},{... | collective-permute-start | bytes 1179656 | tf_op jit(solution)/shard_map/ppermute | solution.py:311
  43.9 70.9 %collective-permute-start.8 = (bf16[1,48,32,128]{3,2,1,0:T(8,128)(2,1)}, bf16[1,48,32,128]{3,2,1,0:T(8,128)(2,1)S(1)}, u32[]{:S(2)}, u32[]{:S(2)}) collective-permute-start(bf16[1,48,32,128]{3,2,1,0:T(8,128)(2,1)} %get-tuple-element.141), channel_id=1, source_target_pairs={{0,20},{4,16},{8,28},{12,24},{16,4},{20,0},{24,12},{28,8},{1,21},{... | collective-permute-start | bytes 1179656 | tf_op jit(solution)/shard_map/ppermute | solution.py:311
  72.1 44.2 %collective-permute-start.10 = (bf16[1,48,32,128]{3,2,1,0:T(8,128)(2,1)}, bf16[1,48,32,128]{3,2,1,0:T(8,128)(2,1)S(1)}, u32[]{:S(2)}, u32[]{:S(2)}) collective-permute-start(bf16[1,48,32,128]{3,2,1,0:T(8,128)(2,1)} %get-tuple-element.143), channel_id=1, source_target_pairs={{0,24},{4,28},{8,16},{12,20},{16,8},{20,12},{24,0},{28,4},{1,25},{... | collective-permute-start | bytes 1179656 | tf_op jit(solution)/shard_map/ppermute | solution.py:311
  73.8 47.5 %collective-permute-start.12 = (bf16[1,48,32,128]{3,2,1,0:T(8,128)(2,1)}, bf16[1,48,32,128]{3,2,1,0:T(8,128)(2,1)S(1)}, u32[]{:S(2)}, u32[]{:S(2)}) collective-permute-start(bf16[1,48,32,128]{3,2,1,0:T(8,128)(2,1)} %get-tuple-element.145), channel_id=1, source_target_pairs={{0,28},{4,24},{8,20},{12,16},{16,12},{20,8},{24,4},{28,0},{1,29},{... | collective-permute-start | bytes 1179656 | tf_op jit(solution)/shard_map/ppermute | solution.py:311
  74.2 47.0 %collective-permute-start.5 = (bf16[1,48,32,128]{3,2,1,0:T(8,128)(2,1)}, bf16[1,48,32,128]{3,2,1,0:T(8,128)(2,1)S(1)}, u32[]{:S(2)}, u32[]{:S(2)}) collective-permute-start(bf16[1,48,32,128]{3,2,1,0:T(8,128)(2,1)} %get-tuple-element.138), channel_id=1, source_target_pairs={{0,12},{4,8},{8,4},{12,0},{16,28},{20,24},{24,20},{28,16},{1,13},{... | collective-permute-start | bytes 1179656 | tf_op jit(solution)/shard_map/ppermute | solution.py:311
  77.4 77.6 %collective-permute-start.13 = (bf16[1,48,32,128]{3,2,1,0:T(8,128)(2,1)}, bf16[1,48,32,128]{3,2,1,0:T(8,128)(2,1)S(1)}, u32[]{:S(2)}, u32[]{:S(2)}) collective-permute-start(bf16[1,48,32,128]{3,2,1,0:T(8,128)(2,1)} %get-tuple-element.146), channel_id=1, source_target_pairs={{0,28},{4,24},{8,20},{12,16},{16,12},{20,8},{24,4},{28,0},{1,29},{... | collective-permute-start | bytes 1179656 | tf_op jit(solution)/shard_map/ppermute | solution.py:311
  114.7 43.5 %collective-permute-start.1 = (bf16[1,48,32,128]{3,2,1,0:T(8,128)(2,1)S(1)}, bf16[1,48,32,128]{3,2,1,0:T(8,128)(2,1)S(1)}, u32[]{:S(2)}, u32[]{:S(2)}) collective-permute-start(bf16[1,48,32,128]{3,2,1,0:T(8,128)(2,1)S(1)} %copy-done.63), channel_id=1, source_target_pairs={{0,4},{4,0},{8,12},{12,8},{16,20},{20,16},{24,28},{28,24},{1,5},{5... | collective-permute-start | bytes 1179656 | tf_op jit(solution)/shard_map/ppermute | solution.py:311
  116.3 42.6 %collective-permute-start.3 = (bf16[1,48,32,128]{3,2,1,0:T(8,128)(2,1)S(1)}, bf16[1,48,32,128]{3,2,1,0:T(8,128)(2,1)S(1)}, u32[]{:S(2)}, u32[]{:S(2)}) collective-permute-start(bf16[1,48,32,128]{3,2,1,0:T(8,128)(2,1)S(1)} %copy-done.62), channel_id=1, source_target_pairs={{0,8},{4,12},{8,0},{12,4},{16,24},{20,28},{24,16},{28,20},{1,9},{5... | collective-permute-start | bytes 1179656 | tf_op jit(solution)/shard_map/ppermute | solution.py:311
  121.2 42.1 %collective-permute-start.7 = (bf16[1,48,32,128]{3,2,1,0:T(8,128)(2,1)S(1)}, bf16[1,48,32,128]{3,2,1,0:T(8,128)(2,1)S(1)}, u32[]{:S(2)}, u32[]{:S(2)}) collective-permute-start(bf16[1,48,32,128]{3,2,1,0:T(8,128)(2,1)S(1)} %copy-done.61), channel_id=1, source_target_pairs={{0,16},{4,20},{8,24},{12,28},{16,0},{20,4},{24,8},{28,12},{1,17},{... | collective-permute-start | bytes 1179656 | tf_op jit(solution)/shard_map/ppermute | solution.py:311
  121.3 50.8 %collective-permute-start.9 = (bf16[1,48,32,128]{3,2,1,0:T(8,128)(2,1)S(1)}, bf16[1,48,32,128]{3,2,1,0:T(8,128)(2,1)S(1)}, u32[]{:S(2)}, u32[]{:S(2)}) collective-permute-start(bf16[1,48,32,128]{3,2,1,0:T(8,128)(2,1)S(1)} %copy-done.60), channel_id=1, source_target_pairs={{0,20},{4,16},{8,28},{12,24},{16,4},{20,0},{24,12},{28,8},{1,21},{... | collective-permute-start | bytes 1179656 | tf_op jit(solution)/shard_map/ppermute | solution.py:311
  155.0 33.6 %collective-permute-start.11 = (bf16[1,48,32,128]{3,2,1,0:T(8,128)(2,1)S(1)}, bf16[1,48,32,128]{3,2,1,0:T(8,128)(2,1)S(1)}, u32[]{:S(2)}, u32[]{:S(2)}) collective-permute-start(bf16[1,48,32,128]{3,2,1,0:T(8,128)(2,1)S(1)} %copy-done.59), channel_id=1, source_target_pairs={{0,24},{4,28},{8,16},{12,20},{16,8},{20,12},{24,0},{28,4},{1,25},{... | collective-permute-start | bytes 1179656 | tf_op jit(solution)/shard_map/ppermute | solution.py:311
  158.3 46.6 %collective-permute-start.14 = (bf16[1,48,32,128]{3,2,1,0:T(8,128)(2,1)S(1)}, bf16[1,48,32,128]{3,2,1,0:T(8,128)(2,1)S(1)}, u32[]{:S(2)}, u32[]{:S(2)}) collective-permute-start(bf16[1,48,32,128]{3,2,1,0:T(8,128)(2,1)S(1)} %copy-done.54), channel_id=1, source_target_pairs={{0,4},{4,0},{8,12},{12,8},{16,20},{20,16},{24,28},{28,24},{1,5},{5... | collective-permute-start | bytes 1179656 | tf_op jit(solution)/shard_map/ppermute | solution.py:311
  158.9 48.5 %collective-permute-start.16 = (bf16[1,48,32,128]{3,2,1,0:T(8,128)(2,1)}, bf16[1,48,32,128]{3,2,1,0:T(8,128)(2,1)S(1)}, u32[]{:S(2)}, u32[]{:S(2)}) collective-permute-start(bf16[1,48,32,128]{3,2,1,0:T(8,128)(2,1)} %get-tuple-element.177), channel_id=1, source_target_pairs={{0,8},{4,12},{8,0},{12,4},{16,24},{20,28},{24,16},{28,20},{1,9},{5... | collective-permute-start | bytes 1179656 | tf_op jit(solution)/shard_map/ppermute | solution.py:311
  163.3 45.1 %collective-permute-start.18 = (bf16[1,48,32,128]{3,2,1,0:T(8,128)(2,1)}, bf16[1,48,32,128]{3,2,1,0:T(8,128)(2,1)S(1)}, u32[]{:S(2)}, u32[]{:S(2)}) collective-permute-start(bf16[1,48,32,128]{3,2,1,0:T(8,128)(2,1)} %get-tuple-element.179), channel_id=1, source_target_pairs={{0,12},{4,8},{8,4},{12,0},{16,28},{20,24},{24,20},{28,16},{1,13},{... | collective-permute-start | bytes 1179656 | tf_op jit(solution)/shard_map/ppermute | solution.py:311
  172.1 42.4 %collective-permute-start.20 = (bf16[1,48,32,128]{3,2,1,0:T(8,128)(2,1)}, bf16[1,48,32,128]{3,2,1,0:T(8,128)(2,1)S(1)}, u32[]{:S(2)}, u32[]{:S(2)}) collective-permute-start(bf16[1,48,32,128]{3,2,1,0:T(8,128)(2,1)} %get-tuple-element.181), channel_id=1, source_target_pairs={{0,16},{4,20},{8,24},{12,28},{16,0},{20,4},{24,8},{28,12},{1,17},{... | collective-permute-start | bytes 1179656 | tf_op jit(solution)/shard_map/ppermute | solution.py:311
  204.7 179.0 %all-reduce.5.cloned.1.call-start = ((), (), s32[]{:S(2)}) async-start(), calls=%async_computation.1 | async-start | bytes 1179648 | tf_op jit(solution)/shard_map/psum | solution.py:359
  204.7 38.9 %collective-permute-start.22 = (bf16[1,48,32,128]{3,2,1,0:T(8,128)(2,1)}, bf16[1,48,32,128]{3,2,1,0:T(8,128)(2,1)S(1)}, u32[]{:S(2)}, u32[]{:S(2)}) collective-permute-start(bf16[1,48,32,128]{3,2,1,0:T(8,128)(2,1)} %get-tuple-element.183), channel_id=1, source_target_pairs={{0,20},{4,16},{8,28},{12,24},{16,4},{20,0},{24,12},{28,8},{1,21},{... | collective-permute-start | bytes 1179656 | tf_op jit(solution)/shard_map/ppermute | solution.py:311
  204.8 52.1 %collective-permute-start.24 = (bf16[1,48,32,128]{3,2,1,0:T(8,128)(2,1)}, bf16[1,48,32,128]{3,2,1,0:T(8,128)(2,1)S(1)}, u32[]{:S(2)}, u32[]{:S(2)}) collective-permute-start(bf16[1,48,32,128]{3,2,1,0:T(8,128)(2,1)} %get-tuple-element.185), channel_id=1, source_target_pairs={{0,24},{4,28},{8,16},{12,20},{16,8},{20,12},{24,0},{28,4},{1,25},{... | collective-permute-start | bytes 1179656 | tf_op jit(solution)/shard_map/ppermute | solution.py:311
  207.4 67.4 %collective-permute-start.26 = (bf16[1,48,32,128]{3,2,1,0:T(8,128)(2,1)}, bf16[1,48,32,128]{3,2,1,0:T(8,128)(2,1)}, u32[]{:S(2)}, u32[]{:S(2)}) collective-permute-start(bf16[1,48,32,128]{3,2,1,0:T(8,128)(2,1)} %get-tuple-element.187), channel_id=1, source_target_pairs={{0,28},{4,24},{8,20},{12,16},{16,12},{20,8},{24,4},{28,0},{1,29},{... | collective-permute-start | bytes 1179656 | tf_op jit(solution)/shard_map/ppermute | solution.py:311
  208.4 82.7 %collective-permute-start.19 = (bf16[1,48,32,128]{3,2,1,0:T(8,128)(2,1)}, bf16[1,48,32,128]{3,2,1,0:T(8,128)(2,1)}, u32[]{:S(2)}, u32[]{:S(2)}) collective-permute-start(bf16[1,48,32,128]{3,2,1,0:T(8,128)(2,1)} %get-tuple-element.180), channel_id=1, source_target_pairs={{0,12},{4,8},{8,4},{12,0},{16,28},{20,24},{24,20},{28,16},{1,13},{... | collective-permute-start | bytes 1179656 | tf_op jit(solution)/shard_map/ppermute | solution.py:311
  214.4 76.8 %collective-permute-start.27 = (bf16[1,48,32,128]{3,2,1,0:T(8,128)(2,1)}, bf16[1,48,32,128]{3,2,1,0:T(8,128)(2,1)}, u32[]{:S(2)}, u32[]{:S(2)}) collective-permute-start(bf16[1,48,32,128]{3,2,1,0:T(8,128)(2,1)} %get-tuple-element.188), channel_id=1, source_target_pairs={{0,28},{4,24},{8,20},{12,16},{16,12},{20,8},{24,4},{28,0},{1,29},{... | collective-permute-start | bytes 1179656 | tf_op jit(solution)/shard_map/ppermute | solution.py:311
  243.6 51.4 %collective-permute-start.15 = (bf16[1,48,32,128]{3,2,1,0:T(8,128)(2,1)}, bf16[1,48,32,128]{3,2,1,0:T(8,128)(2,1)S(1)}, u32[]{:S(2)}, u32[]{:S(2)}) collective-permute-start(bf16[1,48,32,128]{3,2,1,0:T(8,128)(2,1)} %get-tuple-element.176), channel_id=1, source_target_pairs={{0,4},{4,0},{8,12},{12,8},{16,20},{20,16},{24,28},{28,24},{1,5},{5... | collective-permute-start | bytes 1179656 | tf_op jit(solution)/shard_map/ppermute | solution.py:311
  256.9 38.1 %collective-permute-start.17 = (bf16[1,48,32,128]{3,2,1,0:T(8,128)(2,1)}, bf16[1,48,32,128]{3,2,1,0:T(8,128)(2,1)S(1)}, u32[]{:S(2)}, u32[]{:S(2)}) collective-permute-start(bf16[1,48,32,128]{3,2,1,0:T(8,128)(2,1)} %get-tuple-element.178), channel_id=1, source_target_pairs={{0,8},{4,12},{8,0},{12,4},{16,24},{20,28},{24,16},{28,20},{1,9},{5... | collective-permute-start | bytes 1179656 | tf_op jit(solution)/shard_map/ppermute | solution.py:311
  274.8 36.9 %collective-permute-start.25 = (bf16[1,48,32,128]{3,2,1,0:T(8,128)(2,1)}, bf16[1,48,32,128]{3,2,1,0:T(8,128)(2,1)S(1)}, u32[]{:S(2)}, u32[]{:S(2)}) collective-permute-start(bf16[1,48,32,128]{3,2,1,0:T(8,128)(2,1)} %get-tuple-element.186), channel_id=1, source_target_pairs={{0,24},{4,28},{8,16},{12,20},{16,8},{20,12},{24,0},{28,4},{1,25},{... | collective-permute-start | bytes 1179656 | tf_op jit(solution)/shard_map/ppermute | solution.py:311
  291.1 32.6 %collective-permute-start.21 = (bf16[1,48,32,128]{3,2,1,0:T(8,128)(2,1)S(1)}, bf16[1,48,32,128]{3,2,1,0:T(8,128)(2,1)S(1)}, u32[]{:S(2)}, u32[]{:S(2)}) collective-permute-start(bf16[1,48,32,128]{3,2,1,0:T(8,128)(2,1)S(1)} %copy-done.51), channel_id=1, source_target_pairs={{0,16},{4,20},{8,24},{12,28},{16,0},{20,4},{24,8},{28,12},{1,17},{... | collective-permute-start | bytes 1179656 | tf_op jit(solution)/shard_map/ppermute | solution.py:311
  291.2 40.9 %collective-permute-start.23 = (bf16[1,48,32,128]{3,2,1,0:T(8,128)(2,1)S(1)}, bf16[1,48,32,128]{3,2,1,0:T(8,128)(2,1)S(1)}, u32[]{:S(2)}, u32[]{:S(2)}) collective-permute-start(bf16[1,48,32,128]{3,2,1,0:T(8,128)(2,1)S(1)} %copy-done.50), channel_id=1, source_target_pairs={{0,20},{4,16},{8,28},{12,24},{16,4},{20,0},{24,12},{28,8},{1,21},{... | collective-permute-start | bytes 1179656 | tf_op jit(solution)/shard_map/ppermute | solution.py:311
  295.0 56.3 %collective-permute-start.30 = (bf16[1,48,32,128]{3,2,1,0:T(8,128)(2,1)}, bf16[1,48,32,128]{3,2,1,0:T(8,128)(2,1)S(1)}, u32[]{:S(2)}, u32[]{:S(2)}) collective-permute-start(bf16[1,48,32,128]{3,2,1,0:T(8,128)(2,1)} %get-tuple-element.193), channel_id=1, source_target_pairs={{0,12},{4,8},{8,4},{12,0},{16,28},{20,24},{24,20},{28,16},{1,13},{... | collective-permute-start | bytes 1179656 | tf_op jit(solution)/shard_map/ppermute | solution.py:311
  295.1 59.5 %collective-permute-start.34 = (bf16[1,48,32,128]{3,2,1,0:T(8,128)(2,1)}, bf16[1,48,32,128]{3,2,1,0:T(8,128)(2,1)S(1)}, u32[]{:S(2)}, u32[]{:S(2)}) collective-permute-start(bf16[1,48,32,128]{3,2,1,0:T(8,128)(2,1)} %get-tuple-element.215), channel_id=1, source_target_pairs={{0,28},{4,24},{8,20},{12,16},{16,12},{20,8},{24,4},{28,0},{1,29},{... | collective-permute-start | bytes 1179656 | tf_op jit(solution)/shard_map/ppermute | solution.py:311
  311.7 43.5 %collective-permute-start.42 = (bf16[1,48,32,128]{3,2,1,0:T(8,128)(2,1)}, bf16[1,48,32,128]{3,2,1,0:T(8,128)(2,1)S(1)}, u32[]{:S(2)}, u32[]{:S(2)}) collective-permute-start(bf16[1,48,32,128]{3,2,1,0:T(8,128)(2,1)} %get-tuple-element.225), channel_id=1, source_target_pairs={{0,4},{4,0},{8,12},{12,8},{16,20},{20,16},{24,28},{28,24},{1,5},{5... | collective-permute-start | bytes 1179656 | tf_op jit(solution)/shard_map/ppermute | solution.py:311
  348.2 53.2 %collective-permute-start.43 = (bf16[1,48,32,128]{3,2,1,0:T(8,128)(2,1)}, bf16[1,48,32,128]{3,2,1,0:T(8,128)(2,1)S(1)}, u32[]{:S(2)}, u32[]{:S(2)}) collective-permute-start(bf16[1,48,32,128]{3,2,1,0:T(8,128)(2,1)} %get-tuple-element.226), channel_id=1, source_target_pairs={{0,8},{4,12},{8,0},{12,4},{16,24},{20,28},{24,16},{28,20},{1,9},{5... | collective-permute-start | bytes 1179656 | tf_op jit(solution)/shard_map/ppermute | solution.py:311
  351.3 52.6 %collective-permute-start.44 = (bf16[1,48,32,128]{3,2,1,0:T(8,128)(2,1)}, bf16[1,48,32,128]{3,2,1,0:T(8,128)(2,1)S(1)}, u32[]{:S(2)}, u32[]{:S(2)}) collective-permute-start(bf16[1,48,32,128]{3,2,1,0:T(8,128)(2,1)} %get-tuple-element.227), channel_id=1, source_target_pairs={{0,12},{4,8},{8,4},{12,0},{16,28},{20,24},{24,20},{28,16},{1,13},{... | collective-permute-start | bytes 1179656 | tf_op jit(solution)/shard_map/ppermute | solution.py:311
  351.4 53.1 %collective-permute-start.45 = (bf16[1,48,32,128]{3,2,1,0:T(8,128)(2,1)}, bf16[1,48,32,128]{3,2,1,0:T(8,128)(2,1)S(1)}, u32[]{:S(2)}, u32[]{:S(2)}) collective-permute-start(bf16[1,48,32,128]{3,2,1,0:T(8,128)(2,1)} %get-tuple-element.228), channel_id=1, source_target_pairs={{0,16},{4,20},{8,24},{12,28},{16,0},{20,4},{24,8},{28,12},{1,17},{... | collective-permute-start | bytes 1179656 | tf_op jit(solution)/shard_map/ppermute | solution.py:311
  354.6 52.6 %collective-permute-start.46 = (bf16[1,48,32,128]{3,2,1,0:T(8,128)(2,1)}, bf16[1,48,32,128]{3,2,1,0:T(8,128)(2,1)}, u32[]{:S(2)}, u32[]{:S(2)}) collective-permute-start(bf16[1,48,32,128]{3,2,1,0:T(8,128)(2,1)} %get-tuple-element.229), channel_id=1, source_target_pairs={{0,20},{4,16},{8,28},{12,24},{16,4},{20,0},{24,12},{28,8},{1,21},{... | collective-permute-start | bytes 1179656 | tf_op jit(solution)/shard_map/ppermute | solution.py:311
  355.2 51.9 %collective-permute-start.47 = (bf16[1,48,32,128]{3,2,1,0:T(8,128)(2,1)}, bf16[1,48,32,128]{3,2,1,0:T(8,128)(2,1)}, u32[]{:S(2)}, u32[]{:S(2)}) collective-permute-start(bf16[1,48,32,128]{3,2,1,0:T(8,128)(2,1)} %get-tuple-element.230), channel_id=1, source_target_pairs={{0,24},{4,28},{8,16},{12,20},{16,8},{20,12},{24,0},{28,4},{1,25},{... | collective-permute-start | bytes 1179656 | tf_op jit(solution)/shard_map/ppermute | solution.py:311
  385.9 194.1 %copy-start = (f32[48,2,1536]{2,1,0:T(2,128)S(1)}, f32[48,2,1536]{2,1,0:T(2,128)}, u32[]{:S(2)}) copy-start(f32[48,2,1536]{2,1,0:T(2,128)} %all-reduce.3.cloned.1.call-done) | copy-start | bytes 1769476
  385.9 194.1 %copy-start.1 = (f32[48,2,1536]{2,1,0:T(2,128)S(1)}, f32[48,2,1536]{2,1,0:T(2,128)}, u32[]{:S(2)}) copy-start(f32[48,2,1536]{2,1,0:T(2,128)} %all-reduce.5.cloned.1.call-done) | copy-start | bytes 1769476
  401.4 180.2 %copy-start.6 = (bf16[1,48,32,128]{3,2,1,0:T(8,128)(2,1)}, bf16[1,48,32,128]{3,2,1,0:T(8,128)(2,1)S(1)}, u32[]{:S(2)}) copy-start(bf16[1,48,32,128]{3,2,1,0:T(8,128)(2,1)S(1)} %collective-permute-done.43.refs_3_) | copy-start | bytes 1179652
  401.4 41.2 %collective-permute-start.48 = (bf16[1,48,32,128]{3,2,1,0:T(8,128)(2,1)S(1)}, bf16[1,48,32,128]{3,2,1,0:T(8,128)(2,1)S(1)}, u32[]{:S(2)}, u32[]{:S(2)}) collective-permute-start(bf16[1,48,32,128]{3,2,1,0:T(8,128)(2,1)S(1)} %copy-done.58), channel_id=1, source_target_pairs={{0,28},{4,24},{8,20},{12,16},{16,12},{20,8},{24,4},{28,0},{1,29},{... | collective-permute-start | bytes 1179656 | tf_op jit(solution)/shard_map/ppermute | solution.py:311
  403.9 177.7 %copy-start.7 = (bf16[1,48,32,128]{3,2,1,0:T(8,128)(2,1)}, bf16[1,48,32,128]{3,2,1,0:T(8,128)(2,1)S(1)}, u32[]{:S(2)}) copy-start(bf16[1,48,32,128]{3,2,1,0:T(8,128)(2,1)S(1)} %collective-permute-done.44.refs_4_) | copy-start | bytes 1179652
  403.9 38.8 %collective-permute-start.28 = (bf16[1,48,32,128]{3,2,1,0:T(8,128)(2,1)S(1)}, bf16[1,48,32,128]{3,2,1,0:T(8,128)(2,1)S(1)}, u32[]{:S(2)}, u32[]{:S(2)}) collective-permute-start(bf16[1,48,32,128]{3,2,1,0:T(8,128)(2,1)S(1)} %copy-done.57), channel_id=1, source_target_pairs={{0,4},{4,0},{8,12},{12,8},{16,20},{20,16},{24,28},{28,24},{1,5},{5... | collective-permute-start | bytes 1179656 | tf_op jit(solution)/shard_map/ppermute | solution.py:311
  404.5 177.1 %copy-start.8 = (bf16[1,48,32,128]{3,2,1,0:T(8,128)(2,1)}, bf16[1,48,32,128]{3,2,1,0:T(8,128)(2,1)S(1)}, u32[]{:S(2)}) copy-start(bf16[1,48,32,128]{3,2,1,0:T(8,128)(2,1)S(1)} %collective-permute-done.45.refs_5_) | copy-start | bytes 1179652
  404.5 38.3 %collective-permute-start.29 = (bf16[1,48,32,128]{3,2,1,0:T(8,128)(2,1)S(1)}, bf16[1,48,32,128]{3,2,1,0:T(8,128)(2,1)S(1)}, u32[]{:S(2)}, u32[]{:S(2)}) collective-permute-start(bf16[1,48,32,128]{3,2,1,0:T(8,128)(2,1)S(1)} %copy-done.56), channel_id=1, source_target_pairs={{0,8},{4,12},{8,0},{12,4},{16,24},{20,28},{24,16},{28,20},{1,9},{5... | collective-permute-start | bytes 1179656 | tf_op jit(solution)/shard_map/ppermute | solution.py:311
  407.2 48.5 %collective-permute-start.33 = (bf16[1,48,32,128]{3,2,1,0:T(8,128)(2,1)S(1)}, bf16[1,48,32,128]{3,2,1,0:T(8,128)(2,1)S(1)}, u32[]{:S(2)}, u32[]{:S(2)}) collective-permute-start(bf16[1,48,32,128]{3,2,1,0:T(8,128)(2,1)S(1)} %copy-done.55), channel_id=1, source_target_pairs={{0,24},{4,28},{8,16},{12,20},{16,8},{20,12},{24,0},{28,4},{1,25},{... | collective-permute-start | bytes 1179656 | tf_op jit(solution)/shard_map/ppermute | solution.py:311
  407.2 56.7 %collective-permute-start.31 = (bf16[1,48,32,128]{3,2,1,0:T(8,128)(2,1)S(1)}, bf16[1,48,32,128]{3,2,1,0:T(8,128)(2,1)S(1)}, u32[]{:S(2)}, u32[]{:S(2)}) collective-permute-start(bf16[1,48,32,128]{3,2,1,0:T(8,128)(2,1)S(1)} %copy-done.53), channel_id=1, source_target_pairs={{0,16},{4,20},{8,24},{12,28},{16,0},{20,4},{24,8},{28,12},{1,17},{... | collective-permute-start | bytes 1179656 | tf_op jit(solution)/shard_map/ppermute | solution.py:311
  442.7 27.8 %collective-permute-start.32 = (bf16[1,48,32,128]{3,2,1,0:T(8,128)(2,1)S(1)}, bf16[1,48,32,128]{3,2,1,0:T(8,128)(2,1)S(1)}, u32[]{:S(2)}, u32[]{:S(2)}) collective-permute-start(bf16[1,48,32,128]{3,2,1,0:T(8,128)(2,1)S(1)} %copy-done.52), channel_id=1, source_target_pairs={{0,20},{4,16},{8,28},{12,24},{16,4},{20,0},{24,12},{28,8},{1,21},{... | collective-permute-start | bytes 1179656 | tf_op jit(solution)/shard_map/ppermute | solution.py:311
  442.7 170.0 %copy-start.10 = (bf16[1,48,32,128]{3,2,1,0:T(8,128)(2,1)}, bf16[1,48,32,128]{3,2,1,0:T(8,128)(2,1)S(1)}, u32[]{:S(2)}) copy-start(bf16[1,48,32,128]{3,2,1,0:T(8,128)(2,1)S(1)} %collective-permute-done.28.refs_2_) | copy-start | bytes 1179652
  442.7 31.3 %collective-permute-start.35 = (bf16[1,48,32,128]{3,2,1,0:T(8,128)(2,1)}, bf16[1,48,32,128]{3,2,1,0:T(8,128)(2,1)S(1)}, u32[]{:S(2)}, u32[]{:S(2)}) collective-permute-start(bf16[1,48,32,128]{3,2,1,0:T(8,128)(2,1)} %get-tuple-element.217), channel_id=1, source_target_pairs={{0,4},{4,0},{8,12},{12,8},{16,20},{20,16},{24,28},{28,24},{1,5},{5... | collective-permute-start | bytes 1179656 | tf_op jit(solution)/shard_map/ppermute | solution.py:311
  442.8 31.3 %collective-permute-start.36 = (bf16[1,48,32,128]{3,2,1,0:T(8,128)(2,1)}, bf16[1,48,32,128]{3,2,1,0:T(8,128)(2,1)S(1)}, u32[]{:S(2)}, u32[]{:S(2)}) collective-permute-start(bf16[1,48,32,128]{3,2,1,0:T(8,128)(2,1)} %get-tuple-element.218), channel_id=1, source_target_pairs={{0,8},{4,12},{8,0},{12,4},{16,24},{20,28},{24,16},{28,20},{1,9},{5... | collective-permute-start | bytes 1179656 | tf_op jit(solution)/shard_map/ppermute | solution.py:311
  455.7 21.3 %collective-permute-start.49 = (bf16[1,48,32,128]{3,2,1,0:T(8,128)(2,1)}, bf16[1,48,32,128]{3,2,1,0:T(8,128)(2,1)S(1)}, u32[]{:S(2)}, u32[]{:S(2)}) collective-permute-start(bf16[1,48,32,128]{3,2,1,0:T(8,128)(2,1)} %get-tuple-element.233), channel_id=1, source_target_pairs={{0,4},{4,0},{8,12},{12,8},{16,20},{20,16},{24,28},{28,24},{1,5},{5... | collective-permute-start | bytes 1179656 | tf_op jit(solution)/shard_map/ppermute | solution.py:311
  463.8 22.2 %collective-permute-start.50 = (bf16[1,48,32,128]{3,2,1,0:T(8,128)(2,1)}, bf16[1,48,32,128]{3,2,1,0:T(8,128)(2,1)S(1)}, u32[]{:S(2)}, u32[]{:S(2)}) collective-permute-start(bf16[1,48,32,128]{3,2,1,0:T(8,128)(2,1)} %get-tuple-element.234), channel_id=1, source_target_pairs={{0,8},{4,12},{8,0},{12,4},{16,24},{20,28},{24,16},{28,20},{1,9},{5... | collective-permute-start | bytes 1179656 | tf_op jit(solution)/shard_map/ppermute | solution.py:311
  470.5 23.9 %collective-permute-start.51 = (bf16[1,48,32,128]{3,2,1,0:T(8,128)(2,1)}, bf16[1,48,32,128]{3,2,1,0:T(8,128)(2,1)S(1)}, u32[]{:S(2)}, u32[]{:S(2)}) collective-permute-start(bf16[1,48,32,128]{3,2,1,0:T(8,128)(2,1)} %get-tuple-element.235), channel_id=1, source_target_pairs={{0,12},{4,8},{8,4},{12,0},{16,28},{20,24},{24,20},{28,16},{1,13},{... | collective-permute-start | bytes 1179656 | tf_op jit(solution)/shard_map/ppermute | solution.py:311
  474.0 43.7 %collective-permute-start.52 = (bf16[1,48,32,128]{3,2,1,0:T(8,128)(2,1)}, bf16[1,48,32,128]{3,2,1,0:T(8,128)(2,1)S(1)}, u32[]{:S(2)}, u32[]{:S(2)}) collective-permute-start(bf16[1,48,32,128]{3,2,1,0:T(8,128)(2,1)} %get-tuple-element.236), channel_id=1, source_target_pairs={{0,16},{4,20},{8,24},{12,28},{16,0},{20,4},{24,8},{28,12},{1,17},{... | collective-permute-start | bytes 1179656 | tf_op jit(solution)/shard_map/ppermute | solution.py:311
  474.1 73.1 %collective-permute-start.53 = (bf16[1,48,32,128]{3,2,1,0:T(8,128)(2,1)}, bf16[1,48,32,128]{3,2,1,0:T(8,128)(2,1)S(1)}, u32[]{:S(2)}, u32[]{:S(2)}) collective-permute-start(bf16[1,48,32,128]{3,2,1,0:T(8,128)(2,1)} %get-tuple-element.237), channel_id=1, source_target_pairs={{0,20},{4,16},{8,28},{12,24},{16,4},{20,0},{24,12},{28,8},{1,21},{... | collective-permute-start | bytes 1179656 | tf_op jit(solution)/shard_map/ppermute | solution.py:311
  476.9 93.1 %collective-permute-start.54 = (bf16[1,48,32,128]{3,2,1,0:T(8,128)(2,1)}, bf16[1,48,32,128]{3,2,1,0:T(8,128)(2,1)}, u32[]{:S(2)}, u32[]{:S(2)}) collective-permute-start(bf16[1,48,32,128]{3,2,1,0:T(8,128)(2,1)} %get-tuple-element.238), channel_id=1, source_target_pairs={{0,24},{4,28},{8,16},{12,20},{16,8},{20,12},{24,0},{28,4},{1,25},{... | collective-permute-start | bytes 1179656 | tf_op jit(solution)/shard_map/ppermute | solution.py:311
  486.1 92.5 %collective-permute-start.55 = (bf16[1,48,32,128]{3,2,1,0:T(8,128)(2,1)}, bf16[1,48,32,128]{3,2,1,0:T(8,128)(2,1)}, u32[]{:S(2)}, u32[]{:S(2)}) collective-permute-start(bf16[1,48,32,128]{3,2,1,0:T(8,128)(2,1)} %get-tuple-element.239), channel_id=1, source_target_pairs={{0,28},{4,24},{8,20},{12,16},{16,12},{20,8},{24,4},{28,0},{1,29},{... | collective-permute-start | bytes 1179656 | tf_op jit(solution)/shard_map/ppermute | solution.py:311
  494.4 118.4 %collective-permute-start.37 = (bf16[1,48,32,128]{3,2,1,0:T(8,128)(2,1)}, bf16[1,48,32,128]{3,2,1,0:T(8,128)(2,1)S(1)}, u32[]{:S(2)}, u32[]{:S(2)}) collective-permute-start(bf16[1,48,32,128]{3,2,1,0:T(8,128)(2,1)} %get-tuple-element.219), channel_id=1, source_target_pairs={{0,12},{4,8},{8,4},{12,0},{16,28},{20,24},{24,20},{28,16},{1,13},{... | collective-permute-start | bytes 1179656 | tf_op jit(solution)/shard_map/ppermute | solution.py:311
  517.7 95.1 %collective-permute-start.38 = (bf16[1,48,32,128]{3,2,1,0:T(8,128)(2,1)}, bf16[1,48,32,128]{3,2,1,0:T(8,128)(2,1)S(1)}, u32[]{:S(2)}, u32[]{:S(2)}) collective-permute-start(bf16[1,48,32,128]{3,2,1,0:T(8,128)(2,1)} %get-tuple-element.220), channel_id=1, source_target_pairs={{0,16},{4,20},{8,24},{12,28},{16,0},{20,4},{24,8},{28,12},{1,17},{... | collective-permute-start | bytes 1179656 | tf_op jit(solution)/shard_map/ppermute | solution.py:311
  547.2 65.6 %collective-permute-start.39 = (bf16[1,48,32,128]{3,2,1,0:T(8,128)(2,1)}, bf16[1,48,32,128]{3,2,1,0:T(8,128)(2,1)}, u32[]{:S(2)}, u32[]{:S(2)}) collective-permute-start(bf16[1,48,32,128]{3,2,1,0:T(8,128)(2,1)} %get-tuple-element.221), channel_id=1, source_target_pairs={{0,20},{4,16},{8,28},{12,24},{16,4},{20,0},{24,12},{28,8},{1,21},{... | collective-permute-start | bytes 1179656 | tf_op jit(solution)/shard_map/ppermute | solution.py:311
  570.0 42.7 %collective-permute-start.40 = (bf16[1,48,32,128]{3,2,1,0:T(8,128)(2,1)}, bf16[1,48,32,128]{3,2,1,0:T(8,128)(2,1)}, u32[]{:S(2)}, u32[]{:S(2)}) collective-permute-start(bf16[1,48,32,128]{3,2,1,0:T(8,128)(2,1)} %get-tuple-element.222), channel_id=1, source_target_pairs={{0,24},{4,28},{8,16},{12,20},{16,8},{20,12},{24,0},{28,4},{1,25},{... | collective-permute-start | bytes 1179656 | tf_op jit(solution)/shard_map/ppermute | solution.py:311
  578.6 34.2 %collective-permute-start.41 = (bf16[1,48,32,128]{3,2,1,0:T(8,128)(2,1)}, bf16[1,48,32,128]{3,2,1,0:T(8,128)(2,1)}, u32[]{:S(2)}, u32[]{:S(2)}) collective-permute-start(bf16[1,48,32,128]{3,2,1,0:T(8,128)(2,1)} %get-tuple-element.223), channel_id=1, source_target_pairs={{0,28},{4,24},{8,20},{12,16},{16,12},{20,8},{24,4},{28,0},{1,29},{... | collective-permute-start | bytes 1179656 | tf_op jit(solution)/shard_map/ppermute | solution.py:311
  (58 other events, 3095.2 us)
Sparse Core Ops, SparseCore 0:
  204.8 34.4 all-reduce.2
  348.3 35.3 all-reduce.4

commit v3 on v2

--- a/solution.py
+++ b/solution.py
@@ -62,7 +62,7 @@
     ns = spread.shape[0]
     lanes = parts * members * levels
     rb = 16 if count % 16 == 0 else count
-    pair = 2 if rb % 2 == 0 else 1
+    pair = 8 if rb % 8 == 0 else 1
     inner = rb // pair
     base = first // pair
     return pl.pallas_call(
@@ -136,7 +136,7 @@
     ns = spread.shape[0]
     lanes = parts * members * levels
     rb = 16 if count % 16 == 0 else count
-    pair = 2 if rb % 2 == 0 else 1
+    pair = 8 if rb % 8 == 0 else 1
     inner = rb // pair
     base = first // pair
     n = len(received)

time: 654 us -> 638 us (0.976)
  Pallas kernels: 177 us -> 155 us
  waiting for transfers between devices: 323 us -> 334 us
    pallas_call x2, Pallas kernels: 53.6 us -> 40 us  [synth(): pl.pallas_call(functools.partial(synth_kernel, first, rb, pair), grid_spe...]
    ppermute x56, waiting for transfers between devices: 270 us -> 281 us  [send(): lax.ppermute(blocks[key], 'band', [(d, d ^ hop) for d in range(bands)])]
    pallas_call x2, Pallas kernels: 62 us -> 53.4 us  [analyse(): pl.pallas_call(functools.partial(analyse_kernel, n, first, rb, pair), gri...]
  transfers between devices with their start and end apart: 58 -> 58, of which waited for: 23 -> 25; matrix products, arithmetic and copies ran while one was open for 6% -> 6% of each run, Pallas kernels for 18% -> 17%
where the time goes in v3:
time: 638 us; the launch traced here: 637 us
  waiting for transfers between devices  334 us (52%)
  Pallas kernels  155 us (24%)
  starting transfers between devices  87.8 us (14%)
  other arithmetic  23.1 us (4%)
  local copies, waits for them, and re-layouts  23 us (4%)
  between operations  14.8 us (2%)
    ppermute x56, waiting for transfers between devices, send(): lax.ppermute(blocks[key], 'band', [(d, d ^ hop) for d in range(bands)])  281 us
    ppermute x56, starting transfers between devices, send(): lax.ppermute(blocks[key], 'band', [(d, d ^ hop) for d in range(bands)])  87.5 us
    pallas_call x2, Pallas kernels, analyse(): pl.pallas_call(functools.partial(analyse_kernel, n, first, rb, pair), gri...  53.4 us
    psum x2, waiting for transfers between devices, body(): increment = lax.psum(part, 'mem')  52.3 us
    pallas_call x2, Pallas kernels, synth(): pl.pallas_call(functools.partial(synth_kernel, first, rb, pair), grid_spe...  40 us
    pallas_call x2, Pallas kernels, from_grid(): pl.pallas_call(functools.partial(adjoint_kernel, len(shapes), scale), gri...  30.6 us
    pallas_call x2, Pallas kernels, to_grid(): pl.pallas_call(functools.partial(grid_kernel, len(received), scale), grid...  30.6 us
    unnamed x129, local copies, waits for them, and re-layouts  20.6 us
  transfers between devices with their start and end apart: 58, of which 25 were waited for; matrix products, arithmetic and copies ran while one was open for 6% of the time, Pallas kernels for 17%

profile of v3, /device:TPU:8, one launch (start us, length us, event | category | flops | bytes accessed | tf_op | source)
XLA Modules:
  0.0 637.1 jit_solution(2678333202640647431)
XLA Ops:
  10.9 20.1 %shard_map.78 = (bf16[1,48,32,128]{3,2,1,0:T(8,128)(2,1)}, bf16[1,48,32,128]{3,2,1,0:T(8,128)(2,1)}, bf16[1,48,32,128]{3,2,1,0:T(8,128)(2,1)}, bf16[1,48,32,128]...) custom-call(s32[64]{0:T(128)} %dynamic_slice.3.waves.refs_0_, ...), custom_call_target="tpu_custom_call" | custom-call | flops 805306368 | bytes 3984588 | tf_op jit(solution)/shard_map/pallas_call | solution.py:68
  30.9 1.6 collective-permute-start
  32.9 1.6 collective-permute-start.4
  34.5 2.6 collective-permute-start.6
  38.6 20.0 %shard_map.77 = (bf16[1,48,32,128]{3,2,1,0:T(8,128)(2,1)}, bf16[1,48,32,128]{3,2,1,0:T(8,128)(2,1)}, bf16[1,48,32,128]{3,2,1,0:T(8,128)(2,1)}, bf16[1,48,32,128]...) custom-call(s32[64]{0:T(128)} %dynamic_slice.3.waves.refs_0_, ...), custom_call_target="tpu_custom_call" | custom-call | flops 805306368 | bytes 3984588 | tf_op jit(solution)/shard_map/pallas_call | solution.py:68
  58.6 1.6 collective-permute-start.10
  60.7 5.8 collective-permute-done.4.refs_6_
  66.4 3.3 collective-permute-start.5
  69.7 13.8 %multiply_convert_fusion.1 = (bf16[512,1536]{1,0:T(8,128)(2,1)S(1)}, bf16[512,1536]{1,0:T(8,128)(2,1)S(1)}) fusion(s32[512]{0:T(512)S(1)} %reshape.53, f32[512]{0:T(512)S(1)} %get-tuple-element.242, f32[512]{0:T(512)S(1)} %get-tuple-element.243), kind=kLoop, calls=%fused_computation.6 | loop fusion | flops 10223616 | bytes 3151872 | tf_op jit(solution)/shard_map/convert
  83.6 18.9 %copy.16 = bf16[96,32,2,1536]{3,1,2,0:T(8,128)(2,1)} copy(bf16[96,32,2,1536]{3,2,1,0:T(2,128)(2,1)} %param.7) | data formatting | bytes 37748736 | tf_op args[1]
  102.5 1.9 pad_maximum_fusion.refs_17_.fourier
  104.4 1.9 collective-permute-start.1
  106.4 8.1 %collective-permute-done.12.refs_14_ = bf16[1,48,32,128]{3,2,1,0:T(8,128)(2,1)S(1)} collective-permute-done((bf16[1,48,32,128]{3,2,1,0:T(8,128)(2,1)}, bf16[1,48,32,128]{3,2,1,0:T(8,128)(2,1)S(1)}, u32[]{:S(2)}, u32[]{:S(2)}) %collective-permute-start.12) | collective-permute-done | bytes 393248 | tf_op jit(solution)/shard_map/ppermute | solution.py:311
  114.5 3.8 collective-permute-start.9
  118.3 29.7 %collective-permute-done.13.refs_15_ = bf16[1,48,32,128]{3,2,1,0:T(8,128)(2,1)S(1)} collective-permute-done((bf16[1,48,32,128]{3,2,1,0:T(8,128)(2,1)}, bf16[1,48,32,128]{3,2,1,0:T(8,128)(2,1)S(1)}, u32[]{:S(2)}, u32[]{:S(2)}) %collective-permute-start.13) | collective-permute-done | bytes 393248 | tf_op jit(solution)/shard_map/ppermute | solution.py:311
  147.9 3.6 collective-permute-start.11
  151.7 4.9 collective-permute-done.7.refs_9_
  157.9 7.4 %collective-permute-done.9.refs_11_ = bf16[1,48,32,128]{3,2,1,0:T(8,128)(2,1)S(1)} collective-permute-done((bf16[1,48,32,128]{3,2,1,0:T(8,128)(2,1)S(1)}, bf16[1,48,32,128]{3,2,1,0:T(8,128)(2,1)S(1)}, u32[]{:S(2)}, u32[]{:S(2)}) %collective-permute-start.9) | collective-permute-done | bytes 393248 | tf_op jit(solution)/shard_map/ppermute | solution.py:311
  165.3 4.7 collective-permute-start.20
  170.0 11.8 %collective-permute-done.11.refs_13_ = bf16[1,48,32,128]{3,2,1,0:T(8,128)(2,1)S(1)} collective-permute-done((bf16[1,48,32,128]{3,2,1,0:T(8,128)(2,1)S(1)}, bf16[1,48,32,128]{3,2,1,0:T(8,128)(2,1)S(1)}, u32[]{:S(2)}, u32[]{:S(2)}) %collective-permute-start.11) | collective-permute-done | bytes 393248 | tf_op jit(solution)/shard_map/ppermute | solution.py:311
  182.6 15.3 %shard_map.79 = f32[48,2,1536]{2,1,0:T(2,128)} custom-call(bf16[1,48,32,128]{3,2,1,0:T(8,128)(2,1)} %get-tuple-element.126.refs_0_, bf16[1,48,32,128]{3,2,1,0:T(8,128)(2,1)} %get-tuple-element.127.refs_1_, bf16[1,48,32,128]{3,2,1,0:T(8,128)(2,1)} %copy-done.17, bf16[1,48,32,128]{3,2,1,0:T(8,128)(2,1)} %copy-done.39, bf16[1,48,32,128]{3,2,1,0:T(8,128)(2,1)} %copy-done.20, ...), custom_call_target="tpu_custom_call" | custom-call | flops 966367616 | bytes 1887436 | tf_op jit(solution)/shard_map/pallas_call | solution.py:203
  198.3 2.6 collective-permute-start.24
  201.8 6.0 collective-permute-start.19
  207.8 24.7 %all-reduce.3.cloned.1.call-done = f32[48,2,1536]{2,1,0:T(2,128)} async-done(((f32[48,2,1536]{2,1,0:T(2,128)}), f32[48,2,1536]{2,1,0:T(2,128)}) %all-reduce.3.cloned.1.call-update) | async-done | bytes 589840 | tf_op jit(solution)/shard_map/psum | solution.py:359
  232.6 2.2 slice_multiply_fusion.1.gradient
  234.8 2.3 collective-permute-done.22.refs_10_
  237.6 12.8 %collective-permute-done.24.refs_12_ = bf16[1,48,32,128]{3,2,1,0:T(8,128)(2,1)S(1)} collective-permute-done((bf16[1,48,32,128]{3,2,1,0:T(8,128)(2,1)}, bf16[1,48,32,128]{3,2,1,0:T(8,128)(2,1)S(1)}, u32[]{:S(2)}, u32[]{:S(2)}) %collective-permute-start.24) | collective-permute-done | bytes 393248 | tf_op jit(solution)/shard_map/ppermute | solution.py:311
  250.4 17.9 %collective-permute-done.26.refs_14_ = bf16[1,48,32,128]{3,2,1,0:T(8,128)(2,1)} collective-permute-done((bf16[1,48,32,128]{3,2,1,0:T(8,128)(2,1)}, bf16[1,48,32,128]{3,2,1,0:T(8,128)(2,1)}, u32[]{:S(2)}, u32[]{:S(2)}) %collective-permute-start.26) | collective-permute-done | bytes 393248 | tf_op jit(solution)/shard_map/ppermute | solution.py:311
  269.1 15.2 %shard_map.80 = (bf16[1,48,32,128]{3,2,1,0:T(8,128)(2,1)}, bf16[1,48,32,128]{3,2,1,0:T(8,128)(2,1)}, bf16[1,48,32,128]{3,2,1,0:T(8,128)(2,1)}, bf16[1,48,32,128]...) custom-call(bf16[96,2,32,1536]{3,2,1,0:T(8,128)(2,1)} %bitcast.5, ...), custom_call_target="tpu_custom_call" | custom-call | flops 966367616 | bytes 1887436 | tf_op jit(solution)/shard_map/pallas_call | solution.py:249
  284.5 3.8 collective-permute-start.23
  288.3 1.5 collective-permute-start.34
  289.9 15.2 %collective-permute-done.25.refs_13_ = bf16[1,48,32,128]{3,2,1,0:T(8,128)(2,1)S(1)} collective-permute-done((bf16[1,48,32,128]{3,2,1,0:T(8,128)(2,1)}, bf16[1,48,32,128]{3,2,1,0:T(8,128)(2,1)S(1)}, u32[]{:S(2)}, u32[]{:S(2)}) %collective-permute-start.25) | collective-permute-done | bytes 393248 | tf_op jit(solution)/shard_map/ppermute | solution.py:311
  306.6 10.5 %collective-permute-done.21.refs_9_ = bf16[1,48,32,128]{3,2,1,0:T(8,128)(2,1)S(1)} collective-permute-done((bf16[1,48,32,128]{3,2,1,0:T(8,128)(2,1)S(1)}, bf16[1,48,32,128]{3,2,1,0:T(8,128)(2,1)S(1)}, u32[]{:S(2)}, u32[]{:S(2)}) %collective-permute-start.21) | collective-permute-done | bytes 393248 | tf_op jit(solution)/shard_map/ppermute | solution.py:311
  317.1 8.4 %collective-permute-done.23.refs_11_ = bf16[1,48,32,128]{3,2,1,0:T(8,128)(2,1)S(1)} collective-permute-done((bf16[1,48,32,128]{3,2,1,0:T(8,128)(2,1)S(1)}, bf16[1,48,32,128]{3,2,1,0:T(8,128)(2,1)S(1)}, u32[]{:S(2)}, u32[]{:S(2)}) %collective-permute-start.23) | collective-permute-done | bytes 393248 | tf_op jit(solution)/shard_map/ppermute | solution.py:311
  326.3 15.3 %shard_map.81 = f32[48,2,1536]{2,1,0:T(2,128)} custom-call(bf16[1,48,32,128]{3,2,1,0:T(8,128)(2,1)} %get-tuple-element.173.refs_0_, bf16[1,48,32,128]{3,2,1,0:T(8,128)(2,1)} %get-tuple-element.174.refs_1_, bf16[1,48,32,128]{3,2,1,0:T(8,128)(2,1)} %copy-done.9, bf16[1,48,32,128]{3,2,1,0:T(8,128)(2,1)} %copy-done.33, bf16[1,48,32,128]{3,2,1,0:T(8,128)(2,1)} %copy-done.11, ...), custom_call_target="tpu_custom_call" | custom-call | flops 966367616 | bytes 1887436 | tf_op jit(solution)/shard_map/pallas_call | solution.py:203
  341.6 3.1 collective-permute-start.43
  344.8 3.2 collective-permute-start.45
  349.5 27.6 %all-reduce.5.cloned.1.call-done = f32[48,2,1536]{2,1,0:T(2,128)} async-done(((f32[48,2,1536]{2,1,0:T(2,128)}), f32[48,2,1536]{2,1,0:T(2,128)}) %all-reduce.5.cloned.1.call-update) | async-done | bytes 589840 | tf_op jit(solution)/shard_map/psum | solution.py:359
  377.1 2.2 slice_multiply_fusion.gradient
  379.4 15.4 %shard_map.82 = (bf16[1,48,32,128]{3,2,1,0:T(8,128)(2,1)}, bf16[1,48,32,128]{3,2,1,0:T(8,128)(2,1)}, bf16[1,48,32,128]{3,2,1,0:T(8,128)(2,1)}, bf16[1,48,32,128]...) custom-call(bf16[96,2,32,1536]{3,2,1,0:T(8,128)(2,1)} %bitcast.7, ...), custom_call_target="tpu_custom_call" | custom-call | flops 966367616 | bytes 1887436 | tf_op jit(solution)/shard_map/pallas_call | solution.py:249
  394.8 2.5 collective-permute-start.48
  397.9 2.6 collective-permute-start.29
  400.6 2.4 collective-permute-start.31
  403.0 33.0 %collective-permute-done.48.refs_8_ = bf16[1,48,32,128]{3,2,1,0:T(8,128)(2,1)S(1)} collective-permute-done((bf16[1,48,32,128]{3,2,1,0:T(8,128)(2,1)S(1)}, bf16[1,48,32,128]{3,2,1,0:T(8,128)(2,1)S(1)}, u32[]{:S(2)}, u32[]{:S(2)}) %collective-permute-start.48) | collective-permute-done | bytes 393248 | tf_op jit(solution)/shard_map/ppermute | solution.py:311
  436.3 12.8 %collective-permute-done.33.refs_7_ = bf16[1,48,32,128]{3,2,1,0:T(8,128)(2,1)S(1)} collective-permute-done((bf16[1,48,32,128]{3,2,1,0:T(8,128)(2,1)S(1)}, bf16[1,48,32,128]{3,2,1,0:T(8,128)(2,1)S(1)}, u32[]{:S(2)}, u32[]{:S(2)}) %collective-permute-start.33) | collective-permute-done | bytes 393248 | tf_op jit(solution)/shard_map/ppermute | solution.py:311
  449.4 7.9 %collective-permute-done.31.refs_5_ = bf16[1,48,32,128]{3,2,1,0:T(8,128)(2,1)S(1)} collective-permute-done((bf16[1,48,32,128]{3,2,1,0:T(8,128)(2,1)S(1)}, bf16[1,48,32,128]{3,2,1,0:T(8,128)(2,1)S(1)}, u32[]{:S(2)}, u32[]{:S(2)}) %collective-permute-start.31) | collective-permute-done | bytes 393248 | tf_op jit(solution)/shard_map/ppermute | solution.py:311
  457.2 1.7 collective-permute-start.50
  459.0 4.9 collective-permute-done.32.refs_6_
  463.9 3.5 collective-permute-start.51
  467.5 2.9 collective-permute-start.53
  471.8 7.7 %collective-permute-done.50.refs_11_ = bf16[1,48,32,128]{3,2,1,0:T(8,128)(2,1)S(1)} collective-permute-done((bf16[1,48,32,128]{3,2,1,0:T(8,128)(2,1)}, bf16[1,48,32,128]{3,2,1,0:T(8,128)(2,1)S(1)}, u32[]{:S(2)}, u32[]{:S(2)}) %collective-permute-start.50) | collective-permute-done | bytes 393248 | tf_op jit(solution)/shard_map/ppermute | solution.py:311
  479.4 2.3 collective-permute-start.55
  481.7 6.0 collective-permute-done.51.refs_12_
  487.8 3.3 collective-permute-start.37
  491.0 20.1 %collective-permute-done.52.refs_13_ = bf16[1,48,32,128]{3,2,1,0:T(8,128)(2,1)S(1)} collective-permute-done((bf16[1,48,32,128]{3,2,1,0:T(8,128)(2,1)}, bf16[1,48,32,128]{3,2,1,0:T(8,128)(2,1)S(1)}, u32[]{:S(2)}, u32[]{:S(2)}) %collective-permute-start.52) | collective-permute-done | bytes 393248 | tf_op jit(solution)/shard_map/ppermute | solution.py:311
  511.1 3.3 collective-permute-start.38
  514.4 26.2 %collective-permute-done.53.refs_14_ = bf16[1,48,32,128]{3,2,1,0:T(8,128)(2,1)S(1)} collective-permute-done((bf16[1,48,32,128]{3,2,1,0:T(8,128)(2,1)}, bf16[1,48,32,128]{3,2,1,0:T(8,128)(2,1)S(1)}, u32[]{:S(2)}, u32[]{:S(2)}) %collective-permute-start.53) | collective-permute-done | bytes 393248 | tf_op jit(solution)/shard_map/ppermute | solution.py:311
  540.6 4.2 collective-permute-start.39
  544.8 18.7 %collective-permute-done.54.refs_15_ = bf16[1,48,32,128]{3,2,1,0:T(8,128)(2,1)} collective-permute-done((bf16[1,48,32,128]{3,2,1,0:T(8,128)(2,1)}, bf16[1,48,32,128]{3,2,1,0:T(8,128)(2,1)}, u32[]{:S(2)}, u32[]{:S(2)}) %collective-permute-start.54) | collective-permute-done | bytes 393248 | tf_op jit(solution)/shard_map/ppermute | solution.py:311
  564.1 7.8 %collective-permute-done.55.refs_16_ = bf16[1,48,32,128]{3,2,1,0:T(8,128)(2,1)} collective-permute-done((bf16[1,48,32,128]{3,2,1,0:T(8,128)(2,1)}, bf16[1,48,32,128]{3,2,1,0:T(8,128)(2,1)}, u32[]{:S(2)}, u32[]{:S(2)}) %collective-permute-start.55) | collective-permute-done | bytes 393248 | tf_op jit(solution)/shard_map/ppermute | solution.py:311
  573.5 1.5 pad_maximum_fusion.1
  575.0 26.8 %shard_map.83.refs_20_ = f32[2,64,32,2,512]{4,3,2,1,0:T(2,128)} custom-call(s32[64]{0:T(128)} %dynamic_slice.3.waves.refs_0_, bf16[1,48,32,128]{3,2,1,0:T(8,128)(2,1)} %get-tuple-element.224.refs_1_, bf16[1,48,32,128]{3,2,1,0:T(8,128)(2,1)} %copy-done.5, bf16[1,48,32,128]{3,2,1,0:T(8,128)(2,1)} %copy-done.6, bf16[1,48,32,128]{3,2,1,0:T(8,128)(2,1)} %copy-done.7, ...), custom_call_target="tpu_custom_call" | custom-call | flops 805306368 | bytes 4823449 | tf_op jit(solution)/shard_map/pallas_call | solution.py:144
  602.0 1.7 collective-permute-done.41.refs_16_
  603.7 26.6 %shard_map.84 = f32[2,64,32,2,512]{4,3,2,1,0:T(2,128)} custom-call(s32[64]{0:T(128)} %dynamic_slice.3.waves.refs_0_, bf16[1,48,32,128]{3,2,1,0:T(8,128)(2,1)} %get-tuple-element.190.refs_1_, bf16[1,48,32,128]{3,2,1,0:T(8,128)(2,1)} %copy-done.10, bf16[1,48,32,128]{3,2,1,0:T(8,128)(2,1)} %copy-done.12, ...), custom_call_target="tpu_custom_call", output_to_operand_aliasing={{}: (20, {})} | custom-call | flops 805306368 | bytes 4823449 | tf_op jit(solution)/shard_map/pallas_call | solution.py:144
  (209 shorter events, 20.1 us)
Async XLA Ops:
  7.2 225.4 %all-reduce.3.cloned.1.call-start = ((), (), s32[]{:S(2)}) async-start(), calls=%async_computation | async-start | bytes 1179648 | tf_op jit(solution)/shard_map/psum | solution.py:359
  30.9 27.6 %collective-permute-start = (bf16[1,48,32,128]{3,2,1,0:T(8,128)(2,1)}, bf16[1,48,32,128]{3,2,1,0:T(8,128)(2,1)S(1)}, u32[]{:S(2)}, u32[]{:S(2)}) collective-permute-start(bf16[1,48,32,128]{3,2,1,0:T(8,128)(2,1)} %get-tuple-element.128), channel_id=1, source_target_pairs={{0,4},{4,0},{8,12},{12,8},{16,20},{20,16},{24,28},{28,24},{1,5},{5... | collective-permute-start | bytes 1179656 | tf_op jit(solution)/shard_map/ppermute | solution.py:311
  32.5 27.7 %collective-permute-start.2 = (bf16[1,48,32,128]{3,2,1,0:T(8,128)(2,1)}, bf16[1,48,32,128]{3,2,1,0:T(8,128)(2,1)S(1)}, u32[]{:S(2)}, u32[]{:S(2)}) collective-permute-start(bf16[1,48,32,128]{3,2,1,0:T(8,128)(2,1)} %get-tuple-element.135), channel_id=1, source_target_pairs={{0,8},{4,12},{8,0},{12,4},{16,24},{20,28},{24,16},{28,20},{1,9},{5... | collective-permute-start | bytes 1179656 | tf_op jit(solution)/shard_map/ppermute | solution.py:311
  32.9 33.5 %collective-permute-start.4 = (bf16[1,48,32,128]{3,2,1,0:T(8,128)(2,1)}, bf16[1,48,32,128]{3,2,1,0:T(8,128)(2,1)S(1)}, u32[]{:S(2)}, u32[]{:S(2)}) collective-permute-start(bf16[1,48,32,128]{3,2,1,0:T(8,128)(2,1)} %get-tuple-element.137), channel_id=1, source_target_pairs={{0,12},{4,8},{8,4},{12,0},{16,28},{20,24},{24,20},{28,16},{1,13},{... | collective-permute-start | bytes 1179656 | tf_op jit(solution)/shard_map/ppermute | solution.py:311
  34.5 35.2 %collective-permute-start.6 = (bf16[1,48,32,128]{3,2,1,0:T(8,128)(2,1)}, bf16[1,48,32,128]{3,2,1,0:T(8,128)(2,1)S(1)}, u32[]{:S(2)}, u32[]{:S(2)}) collective-permute-start(bf16[1,48,32,128]{3,2,1,0:T(8,128)(2,1)} %get-tuple-element.139), channel_id=1, source_target_pairs={{0,16},{4,20},{8,24},{12,28},{16,0},{20,4},{24,8},{28,12},{1,17},{... | collective-permute-start | bytes 1179656 | tf_op jit(solution)/shard_map/ppermute | solution.py:311
  37.1 67.3 %collective-permute-start.8 = (bf16[1,48,32,128]{3,2,1,0:T(8,128)(2,1)}, bf16[1,48,32,128]{3,2,1,0:T(8,128)(2,1)S(1)}, u32[]{:S(2)}, u32[]{:S(2)}) collective-permute-start(bf16[1,48,32,128]{3,2,1,0:T(8,128)(2,1)} %get-tuple-element.141), channel_id=1, source_target_pairs={{0,20},{4,16},{8,28},{12,24},{16,4},{20,0},{24,12},{28,8},{1,21},{... | collective-permute-start | bytes 1179656 | tf_op jit(solution)/shard_map/ppermute | solution.py:311
  58.6 47.7 %collective-permute-start.10 = (bf16[1,48,32,128]{3,2,1,0:T(8,128)(2,1)}, bf16[1,48,32,128]{3,2,1,0:T(8,128)(2,1)S(1)}, u32[]{:S(2)}, u32[]{:S(2)}) collective-permute-start(bf16[1,48,32,128]{3,2,1,0:T(8,128)(2,1)} %get-tuple-element.143), channel_id=1, source_target_pairs={{0,24},{4,28},{8,16},{12,20},{16,8},{20,12},{24,0},{28,4},{1,25},{... | collective-permute-start | bytes 1179656 | tf_op jit(solution)/shard_map/ppermute | solution.py:311
  60.2 54.2 %collective-permute-start.12 = (bf16[1,48,32,128]{3,2,1,0:T(8,128)(2,1)}, bf16[1,48,32,128]{3,2,1,0:T(8,128)(2,1)S(1)}, u32[]{:S(2)}, u32[]{:S(2)}) collective-permute-start(bf16[1,48,32,128]{3,2,1,0:T(8,128)(2,1)} %get-tuple-element.145), channel_id=1, source_target_pairs={{0,28},{4,24},{8,20},{12,16},{16,12},{20,8},{24,4},{28,0},{1,29},{... | collective-permute-start | bytes 1179656 | tf_op jit(solution)/shard_map/ppermute | solution.py:311
  66.4 48.0 %collective-permute-start.5 = (bf16[1,48,32,128]{3,2,1,0:T(8,128)(2,1)}, bf16[1,48,32,128]{3,2,1,0:T(8,128)(2,1)S(1)}, u32[]{:S(2)}, u32[]{:S(2)}) collective-permute-start(bf16[1,48,32,128]{3,2,1,0:T(8,128)(2,1)} %get-tuple-element.138), channel_id=1, source_target_pairs={{0,12},{4,8},{8,4},{12,0},{16,28},{20,24},{24,20},{28,16},{1,13},{... | collective-permute-start | bytes 1179656 | tf_op jit(solution)/shard_map/ppermute | solution.py:311
  69.7 78.2 %collective-permute-start.13 = (bf16[1,48,32,128]{3,2,1,0:T(8,128)(2,1)}, bf16[1,48,32,128]{3,2,1,0:T(8,128)(2,1)S(1)}, u32[]{:S(2)}, u32[]{:S(2)}) collective-permute-start(bf16[1,48,32,128]{3,2,1,0:T(8,128)(2,1)} %get-tuple-element.146), channel_id=1, source_target_pairs={{0,28},{4,24},{8,20},{12,16},{16,12},{20,8},{24,4},{28,0},{1,29},{... | collective-permute-start | bytes 1179656 | tf_op jit(solution)/shard_map/ppermute | solution.py:311
  104.4 47.1 %collective-permute-start.1 = (bf16[1,48,32,128]{3,2,1,0:T(8,128)(2,1)S(1)}, bf16[1,48,32,128]{3,2,1,0:T(8,128)(2,1)S(1)}, u32[]{:S(2)}, u32[]{:S(2)}) collective-permute-start(bf16[1,48,32,128]{3,2,1,0:T(8,128)(2,1)S(1)} %copy-done.63), channel_id=1, source_target_pairs={{0,4},{4,0},{8,12},{12,8},{16,20},{20,16},{24,28},{28,24},{1,5},{5... | collective-permute-start | bytes 1179656 | tf_op jit(solution)/shard_map/ppermute | solution.py:311
  106.3 45.3 %collective-permute-start.3 = (bf16[1,48,32,128]{3,2,1,0:T(8,128)(2,1)S(1)}, bf16[1,48,32,128]{3,2,1,0:T(8,128)(2,1)S(1)}, u32[]{:S(2)}, u32[]{:S(2)}) collective-permute-start(bf16[1,48,32,128]{3,2,1,0:T(8,128)(2,1)S(1)} %copy-done.62), channel_id=1, source_target_pairs={{0,8},{4,12},{8,0},{12,4},{16,24},{20,28},{24,16},{28,20},{1,9},{5... | collective-permute-start | bytes 1179656 | tf_op jit(solution)/shard_map/ppermute | solution.py:311
  114.5 42.1 %collective-permute-start.7 = (bf16[1,48,32,128]{3,2,1,0:T(8,128)(2,1)S(1)}, bf16[1,48,32,128]{3,2,1,0:T(8,128)(2,1)S(1)}, u32[]{:S(2)}, u32[]{:S(2)}) collective-permute-start(bf16[1,48,32,128]{3,2,1,0:T(8,128)(2,1)S(1)} %copy-done.61), channel_id=1, source_target_pairs={{0,16},{4,20},{8,24},{12,28},{16,0},{20,4},{24,8},{28,12},{1,17},{... | collective-permute-start | bytes 1179656 | tf_op jit(solution)/shard_map/ppermute | solution.py:311
  114.5 50.8 %collective-permute-start.9 = (bf16[1,48,32,128]{3,2,1,0:T(8,128)(2,1)S(1)}, bf16[1,48,32,128]{3,2,1,0:T(8,128)(2,1)S(1)}, u32[]{:S(2)}, u32[]{:S(2)}) collective-permute-start(bf16[1,48,32,128]{3,2,1,0:T(8,128)(2,1)S(1)} %copy-done.60), channel_id=1, source_target_pairs={{0,20},{4,16},{8,28},{12,24},{16,4},{20,0},{24,12},{28,8},{1,21},{... | collective-permute-start | bytes 1179656 | tf_op jit(solution)/shard_map/ppermute | solution.py:311
  147.9 33.9 %collective-permute-start.11 = (bf16[1,48,32,128]{3,2,1,0:T(8,128)(2,1)S(1)}, bf16[1,48,32,128]{3,2,1,0:T(8,128)(2,1)S(1)}, u32[]{:S(2)}, u32[]{:S(2)}) collective-permute-start(bf16[1,48,32,128]{3,2,1,0:T(8,128)(2,1)S(1)} %copy-done.59), channel_id=1, source_target_pairs={{0,24},{4,28},{8,16},{12,20},{16,8},{20,12},{24,0},{28,4},{1,25},{... | collective-permute-start | bytes 1179656 | tf_op jit(solution)/shard_map/ppermute | solution.py:311
  151.5 46.8 %collective-permute-start.14 = (bf16[1,48,32,128]{3,2,1,0:T(8,128)(2,1)S(1)}, bf16[1,48,32,128]{3,2,1,0:T(8,128)(2,1)S(1)}, u32[]{:S(2)}, u32[]{:S(2)}) collective-permute-start(bf16[1,48,32,128]{3,2,1,0:T(8,128)(2,1)S(1)} %copy-done.54), channel_id=1, source_target_pairs={{0,4},{4,0},{8,12},{12,8},{16,20},{20,16},{24,28},{28,24},{1,5},{5... | collective-permute-start | bytes 1179656 | tf_op jit(solution)/shard_map/ppermute | solution.py:311
  151.6 49.2 %collective-permute-start.16 = (bf16[1,48,32,128]{3,2,1,0:T(8,128)(2,1)}, bf16[1,48,32,128]{3,2,1,0:T(8,128)(2,1)S(1)}, u32[]{:S(2)}, u32[]{:S(2)}) collective-permute-start(bf16[1,48,32,128]{3,2,1,0:T(8,128)(2,1)} %get-tuple-element.177), channel_id=1, source_target_pairs={{0,8},{4,12},{8,0},{12,4},{16,24},{20,28},{24,16},{28,20},{1,9},{5... | collective-permute-start | bytes 1179656 | tf_op jit(solution)/shard_map/ppermute | solution.py:311
  156.6 45.2 %collective-permute-start.18 = (bf16[1,48,32,128]{3,2,1,0:T(8,128)(2,1)}, bf16[1,48,32,128]{3,2,1,0:T(8,128)(2,1)S(1)}, u32[]{:S(2)}, u32[]{:S(2)}) collective-permute-start(bf16[1,48,32,128]{3,2,1,0:T(8,128)(2,1)} %get-tuple-element.179), channel_id=1, source_target_pairs={{0,12},{4,8},{8,4},{12,0},{16,28},{20,24},{24,20},{28,16},{1,13},{... | collective-permute-start | bytes 1179656 | tf_op jit(solution)/shard_map/ppermute | solution.py:311
  165.3 42.5 %collective-permute-start.20 = (bf16[1,48,32,128]{3,2,1,0:T(8,128)(2,1)}, bf16[1,48,32,128]{3,2,1,0:T(8,128)(2,1)S(1)}, u32[]{:S(2)}, u32[]{:S(2)}) collective-permute-start(bf16[1,48,32,128]{3,2,1,0:T(8,128)(2,1)} %get-tuple-element.181), channel_id=1, source_target_pairs={{0,16},{4,20},{8,24},{12,28},{16,0},{20,4},{24,8},{28,12},{1,17},{... | collective-permute-start | bytes 1179656 | tf_op jit(solution)/shard_map/ppermute | solution.py:311
  197.9 179.2 %all-reduce.5.cloned.1.call-start = ((), (), s32[]{:S(2)}) async-start(), calls=%async_computation.1 | async-start | bytes 1179648 | tf_op jit(solution)/shard_map/psum | solution.py:359
  198.2 38.8 %collective-permute-start.22 = (bf16[1,48,32,128]{3,2,1,0:T(8,128)(2,1)}, bf16[1,48,32,128]{3,2,1,0:T(8,128)(2,1)S(1)}, u32[]{:S(2)}, u32[]{:S(2)}) collective-permute-start(bf16[1,48,32,128]{3,2,1,0:T(8,128)(2,1)} %get-tuple-element.183), channel_id=1, source_target_pairs={{0,20},{4,16},{8,28},{12,24},{16,4},{20,0},{24,12},{28,8},{1,21},{... | collective-permute-start | bytes 1179656 | tf_op jit(solution)/shard_map/ppermute | solution.py:311
  198.3 52.1 %collective-permute-start.24 = (bf16[1,48,32,128]{3,2,1,0:T(8,128)(2,1)}, bf16[1,48,32,128]{3,2,1,0:T(8,128)(2,1)S(1)}, u32[]{:S(2)}, u32[]{:S(2)}) collective-permute-start(bf16[1,48,32,128]{3,2,1,0:T(8,128)(2,1)} %get-tuple-element.185), channel_id=1, source_target_pairs={{0,24},{4,28},{8,16},{12,20},{16,8},{20,12},{24,0},{28,4},{1,25},{... | collective-permute-start | bytes 1179656 | tf_op jit(solution)/shard_map/ppermute | solution.py:311
  200.8 67.4 %collective-permute-start.26 = (bf16[1,48,32,128]{3,2,1,0:T(8,128)(2,1)}, bf16[1,48,32,128]{3,2,1,0:T(8,128)(2,1)}, u32[]{:S(2)}, u32[]{:S(2)}) collective-permute-start(bf16[1,48,32,128]{3,2,1,0:T(8,128)(2,1)} %get-tuple-element.187), channel_id=1, source_target_pairs={{0,28},{4,24},{8,20},{12,16},{16,12},{20,8},{24,4},{28,0},{1,29},{... | collective-permute-start | bytes 1179656 | tf_op jit(solution)/shard_map/ppermute | solution.py:311
  201.8 82.6 %collective-permute-start.19 = (bf16[1,48,32,128]{3,2,1,0:T(8,128)(2,1)}, bf16[1,48,32,128]{3,2,1,0:T(8,128)(2,1)}, u32[]{:S(2)}, u32[]{:S(2)}) collective-permute-start(bf16[1,48,32,128]{3,2,1,0:T(8,128)(2,1)} %get-tuple-element.180), channel_id=1, source_target_pairs={{0,12},{4,8},{8,4},{12,0},{16,28},{20,24},{24,20},{28,16},{1,13},{... | collective-permute-start | bytes 1179656 | tf_op jit(solution)/shard_map/ppermute | solution.py:311
  207.8 76.7 %collective-permute-start.27 = (bf16[1,48,32,128]{3,2,1,0:T(8,128)(2,1)}, bf16[1,48,32,128]{3,2,1,0:T(8,128)(2,1)}, u32[]{:S(2)}, u32[]{:S(2)}) collective-permute-start(bf16[1,48,32,128]{3,2,1,0:T(8,128)(2,1)} %get-tuple-element.188), channel_id=1, source_target_pairs={{0,28},{4,24},{8,20},{12,16},{16,12},{20,8},{24,4},{28,0},{1,29},{... | collective-permute-start | bytes 1179656 | tf_op jit(solution)/shard_map/ppermute | solution.py:311
  237.0 51.3 %collective-permute-start.15 = (bf16[1,48,32,128]{3,2,1,0:T(8,128)(2,1)}, bf16[1,48,32,128]{3,2,1,0:T(8,128)(2,1)S(1)}, u32[]{:S(2)}, u32[]{:S(2)}) collective-permute-start(bf16[1,48,32,128]{3,2,1,0:T(8,128)(2,1)} %get-tuple-element.176), channel_id=1, source_target_pairs={{0,4},{4,0},{8,12},{12,8},{16,20},{20,16},{24,28},{28,24},{1,5},{5... | collective-permute-start | bytes 1179656 | tf_op jit(solution)/shard_map/ppermute | solution.py:311
  250.3 38.0 %collective-permute-start.17 = (bf16[1,48,32,128]{3,2,1,0:T(8,128)(2,1)}, bf16[1,48,32,128]{3,2,1,0:T(8,128)(2,1)S(1)}, u32[]{:S(2)}, u32[]{:S(2)}) collective-permute-start(bf16[1,48,32,128]{3,2,1,0:T(8,128)(2,1)} %get-tuple-element.178), channel_id=1, source_target_pairs={{0,8},{4,12},{8,0},{12,4},{16,24},{20,28},{24,16},{28,20},{1,9},{5... | collective-permute-start | bytes 1179656 | tf_op jit(solution)/shard_map/ppermute | solution.py:311
  268.2 36.9 %collective-permute-start.25 = (bf16[1,48,32,128]{3,2,1,0:T(8,128)(2,1)}, bf16[1,48,32,128]{3,2,1,0:T(8,128)(2,1)S(1)}, u32[]{:S(2)}, u32[]{:S(2)}) collective-permute-start(bf16[1,48,32,128]{3,2,1,0:T(8,128)(2,1)} %get-tuple-element.186), channel_id=1, source_target_pairs={{0,24},{4,28},{8,16},{12,20},{16,8},{20,12},{24,0},{28,4},{1,25},{... | collective-permute-start | bytes 1179656 | tf_op jit(solution)/shard_map/ppermute | solution.py:311
  284.4 32.7 %collective-permute-start.21 = (bf16[1,48,32,128]{3,2,1,0:T(8,128)(2,1)S(1)}, bf16[1,48,32,128]{3,2,1,0:T(8,128)(2,1)S(1)}, u32[]{:S(2)}, u32[]{:S(2)}) collective-permute-start(bf16[1,48,32,128]{3,2,1,0:T(8,128)(2,1)S(1)} %copy-done.51), channel_id=1, source_target_pairs={{0,16},{4,20},{8,24},{12,28},{16,0},{20,4},{24,8},{28,12},{1,17},{... | collective-permute-start | bytes 1179656 | tf_op jit(solution)/shard_map/ppermute | solution.py:311
  284.5 41.0 %collective-permute-start.23 = (bf16[1,48,32,128]{3,2,1,0:T(8,128)(2,1)S(1)}, bf16[1,48,32,128]{3,2,1,0:T(8,128)(2,1)S(1)}, u32[]{:S(2)}, u32[]{:S(2)}) collective-permute-start(bf16[1,48,32,128]{3,2,1,0:T(8,128)(2,1)S(1)} %copy-done.50), channel_id=1, source_target_pairs={{0,20},{4,16},{8,28},{12,24},{16,4},{20,0},{24,12},{28,8},{1,21},{... | collective-permute-start | bytes 1179656 | tf_op jit(solution)/shard_map/ppermute | solution.py:311
  288.3 56.5 %collective-permute-start.30 = (bf16[1,48,32,128]{3,2,1,0:T(8,128)(2,1)}, bf16[1,48,32,128]{3,2,1,0:T(8,128)(2,1)S(1)}, u32[]{:S(2)}, u32[]{:S(2)}) collective-permute-start(bf16[1,48,32,128]{3,2,1,0:T(8,128)(2,1)} %get-tuple-element.193), channel_id=1, source_target_pairs={{0,12},{4,8},{8,4},{12,0},{16,28},{20,24},{24,20},{28,16},{1,13},{... | collective-permute-start | bytes 1179656 | tf_op jit(solution)/shard_map/ppermute | solution.py:311
  288.3 59.7 %collective-permute-start.34 = (bf16[1,48,32,128]{3,2,1,0:T(8,128)(2,1)}, bf16[1,48,32,128]{3,2,1,0:T(8,128)(2,1)S(1)}, u32[]{:S(2)}, u32[]{:S(2)}) collective-permute-start(bf16[1,48,32,128]{3,2,1,0:T(8,128)(2,1)} %get-tuple-element.215), channel_id=1, source_target_pairs={{0,28},{4,24},{8,20},{12,16},{16,12},{20,8},{24,4},{28,0},{1,29},{... | collective-permute-start | bytes 1179656 | tf_op jit(solution)/shard_map/ppermute | solution.py:311
  305.1 43.5 %collective-permute-start.42 = (bf16[1,48,32,128]{3,2,1,0:T(8,128)(2,1)}, bf16[1,48,32,128]{3,2,1,0:T(8,128)(2,1)S(1)}, u32[]{:S(2)}, u32[]{:S(2)}) collective-permute-start(bf16[1,48,32,128]{3,2,1,0:T(8,128)(2,1)} %get-tuple-element.225), channel_id=1, source_target_pairs={{0,4},{4,0},{8,12},{12,8},{16,20},{20,16},{24,28},{28,24},{1,5},{5... | collective-permute-start | bytes 1179656 | tf_op jit(solution)/shard_map/ppermute | solution.py:311
  341.6 53.2 %collective-permute-start.43 = (bf16[1,48,32,128]{3,2,1,0:T(8,128)(2,1)}, bf16[1,48,32,128]{3,2,1,0:T(8,128)(2,1)S(1)}, u32[]{:S(2)}, u32[]{:S(2)}) collective-permute-start(bf16[1,48,32,128]{3,2,1,0:T(8,128)(2,1)} %get-tuple-element.226), channel_id=1, source_target_pairs={{0,8},{4,12},{8,0},{12,4},{16,24},{20,28},{24,16},{28,20},{1,9},{5... | collective-permute-start | bytes 1179656 | tf_op jit(solution)/shard_map/ppermute | solution.py:311
  344.7 52.6 %collective-permute-start.44 = (bf16[1,48,32,128]{3,2,1,0:T(8,128)(2,1)}, bf16[1,48,32,128]{3,2,1,0:T(8,128)(2,1)S(1)}, u32[]{:S(2)}, u32[]{:S(2)}) collective-permute-start(bf16[1,48,32,128]{3,2,1,0:T(8,128)(2,1)} %get-tuple-element.227), channel_id=1, source_target_pairs={{0,12},{4,8},{8,4},{12,0},{16,28},{20,24},{24,20},{28,16},{1,13},{... | collective-permute-start | bytes 1179656 | tf_op jit(solution)/shard_map/ppermute | solution.py:311
  344.8 53.1 %collective-permute-start.45 = (bf16[1,48,32,128]{3,2,1,0:T(8,128)(2,1)}, bf16[1,48,32,128]{3,2,1,0:T(8,128)(2,1)S(1)}, u32[]{:S(2)}, u32[]{:S(2)}) collective-permute-start(bf16[1,48,32,128]{3,2,1,0:T(8,128)(2,1)} %get-tuple-element.228), channel_id=1, source_target_pairs={{0,16},{4,20},{8,24},{12,28},{16,0},{20,4},{24,8},{28,12},{1,17},{... | collective-permute-start | bytes 1179656 | tf_op jit(solution)/shard_map/ppermute | solution.py:311
  348.0 52.5 %collective-permute-start.46 = (bf16[1,48,32,128]{3,2,1,0:T(8,128)(2,1)}, bf16[1,48,32,128]{3,2,1,0:T(8,128)(2,1)}, u32[]{:S(2)}, u32[]{:S(2)}) collective-permute-start(bf16[1,48,32,128]{3,2,1,0:T(8,128)(2,1)} %get-tuple-element.229), channel_id=1, source_target_pairs={{0,20},{4,16},{8,28},{12,24},{16,4},{20,0},{24,12},{28,8},{1,21},{... | collective-permute-start | bytes 1179656 | tf_op jit(solution)/shard_map/ppermute | solution.py:311
  348.6 51.9 %collective-permute-start.47 = (bf16[1,48,32,128]{3,2,1,0:T(8,128)(2,1)}, bf16[1,48,32,128]{3,2,1,0:T(8,128)(2,1)}, u32[]{:S(2)}, u32[]{:S(2)}) collective-permute-start(bf16[1,48,32,128]{3,2,1,0:T(8,128)(2,1)} %get-tuple-element.230), channel_id=1, source_target_pairs={{0,24},{4,28},{8,16},{12,20},{16,8},{20,12},{24,0},{28,4},{1,25},{... | collective-permute-start | bytes 1179656 | tf_op jit(solution)/shard_map/ppermute | solution.py:311
  379.3 194.1 %copy-start = (f32[48,2,1536]{2,1,0:T(2,128)S(1)}, f32[48,2,1536]{2,1,0:T(2,128)}, u32[]{:S(2)}) copy-start(f32[48,2,1536]{2,1,0:T(2,128)} %all-reduce.3.cloned.1.call-done) | copy-start | bytes 1769476
  379.3 194.1 %copy-start.1 = (f32[48,2,1536]{2,1,0:T(2,128)S(1)}, f32[48,2,1536]{2,1,0:T(2,128)}, u32[]{:S(2)}) copy-start(f32[48,2,1536]{2,1,0:T(2,128)} %all-reduce.5.cloned.1.call-done) | copy-start | bytes 1769476
  394.8 180.2 %copy-start.6 = (bf16[1,48,32,128]{3,2,1,0:T(8,128)(2,1)}, bf16[1,48,32,128]{3,2,1,0:T(8,128)(2,1)S(1)}, u32[]{:S(2)}) copy-start(bf16[1,48,32,128]{3,2,1,0:T(8,128)(2,1)S(1)} %collective-permute-done.43.refs_3_) | copy-start | bytes 1179652
  394.8 41.2 %collective-permute-start.48 = (bf16[1,48,32,128]{3,2,1,0:T(8,128)(2,1)S(1)}, bf16[1,48,32,128]{3,2,1,0:T(8,128)(2,1)S(1)}, u32[]{:S(2)}, u32[]{:S(2)}) collective-permute-start(bf16[1,48,32,128]{3,2,1,0:T(8,128)(2,1)S(1)} %copy-done.58), channel_id=1, source_target_pairs={{0,28},{4,24},{8,20},{12,16},{16,12},{20,8},{24,4},{28,0},{1,29},{... | collective-permute-start | bytes 1179656 | tf_op jit(solution)/shard_map/ppermute | solution.py:311
  397.3 177.7 %copy-start.7 = (bf16[1,48,32,128]{3,2,1,0:T(8,128)(2,1)}, bf16[1,48,32,128]{3,2,1,0:T(8,128)(2,1)S(1)}, u32[]{:S(2)}) copy-start(bf16[1,48,32,128]{3,2,1,0:T(8,128)(2,1)S(1)} %collective-permute-done.44.refs_4_) | copy-start | bytes 1179652
  397.3 38.8 %collective-permute-start.28 = (bf16[1,48,32,128]{3,2,1,0:T(8,128)(2,1)S(1)}, bf16[1,48,32,128]{3,2,1,0:T(8,128)(2,1)S(1)}, u32[]{:S(2)}, u32[]{:S(2)}) collective-permute-start(bf16[1,48,32,128]{3,2,1,0:T(8,128)(2,1)S(1)} %copy-done.57), channel_id=1, source_target_pairs={{0,4},{4,0},{8,12},{12,8},{16,20},{20,16},{24,28},{28,24},{1,5},{5... | collective-permute-start | bytes 1179656 | tf_op jit(solution)/shard_map/ppermute | solution.py:311
  397.9 177.1 %copy-start.8 = (bf16[1,48,32,128]{3,2,1,0:T(8,128)(2,1)}, bf16[1,48,32,128]{3,2,1,0:T(8,128)(2,1)S(1)}, u32[]{:S(2)}) copy-start(bf16[1,48,32,128]{3,2,1,0:T(8,128)(2,1)S(1)} %collective-permute-done.45.refs_5_) | copy-start | bytes 1179652
  397.9 38.3 %collective-permute-start.29 = (bf16[1,48,32,128]{3,2,1,0:T(8,128)(2,1)S(1)}, bf16[1,48,32,128]{3,2,1,0:T(8,128)(2,1)S(1)}, u32[]{:S(2)}, u32[]{:S(2)}) collective-permute-start(bf16[1,48,32,128]{3,2,1,0:T(8,128)(2,1)S(1)} %copy-done.56), channel_id=1, source_target_pairs={{0,8},{4,12},{8,0},{12,4},{16,24},{20,28},{24,16},{28,20},{1,9},{5... | collective-permute-start | bytes 1179656 | tf_op jit(solution)/shard_map/ppermute | solution.py:311
  400.5 48.5 %collective-permute-start.33 = (bf16[1,48,32,128]{3,2,1,0:T(8,128)(2,1)S(1)}, bf16[1,48,32,128]{3,2,1,0:T(8,128)(2,1)S(1)}, u32[]{:S(2)}, u32[]{:S(2)}) collective-permute-start(bf16[1,48,32,128]{3,2,1,0:T(8,128)(2,1)S(1)} %copy-done.55), channel_id=1, source_target_pairs={{0,24},{4,28},{8,16},{12,20},{16,8},{20,12},{24,0},{28,4},{1,25},{... | collective-permute-start | bytes 1179656 | tf_op jit(solution)/shard_map/ppermute | solution.py:311
  400.6 56.7 %collective-permute-start.31 = (bf16[1,48,32,128]{3,2,1,0:T(8,128)(2,1)S(1)}, bf16[1,48,32,128]{3,2,1,0:T(8,128)(2,1)S(1)}, u32[]{:S(2)}, u32[]{:S(2)}) collective-permute-start(bf16[1,48,32,128]{3,2,1,0:T(8,128)(2,1)S(1)} %copy-done.53), channel_id=1, source_target_pairs={{0,16},{4,20},{8,24},{12,28},{16,0},{20,4},{24,8},{28,12},{1,17},{... | collective-permute-start | bytes 1179656 | tf_op jit(solution)/shard_map/ppermute | solution.py:311
  436.1 27.8 %collective-permute-start.32 = (bf16[1,48,32,128]{3,2,1,0:T(8,128)(2,1)S(1)}, bf16[1,48,32,128]{3,2,1,0:T(8,128)(2,1)S(1)}, u32[]{:S(2)}, u32[]{:S(2)}) collective-permute-start(bf16[1,48,32,128]{3,2,1,0:T(8,128)(2,1)S(1)} %copy-done.52), channel_id=1, source_target_pairs={{0,20},{4,16},{8,28},{12,24},{16,4},{20,0},{24,12},{28,8},{1,21},{... | collective-permute-start | bytes 1179656 | tf_op jit(solution)/shard_map/ppermute | solution.py:311
  436.1 165.8 %copy-start.10 = (bf16[1,48,32,128]{3,2,1,0:T(8,128)(2,1)}, bf16[1,48,32,128]{3,2,1,0:T(8,128)(2,1)S(1)}, u32[]{:S(2)}) copy-start(bf16[1,48,32,128]{3,2,1,0:T(8,128)(2,1)S(1)} %collective-permute-done.28.refs_2_) | copy-start | bytes 1179652
  436.1 31.3 %collective-permute-start.35 = (bf16[1,48,32,128]{3,2,1,0:T(8,128)(2,1)}, bf16[1,48,32,128]{3,2,1,0:T(8,128)(2,1)S(1)}, u32[]{:S(2)}, u32[]{:S(2)}) collective-permute-start(bf16[1,48,32,128]{3,2,1,0:T(8,128)(2,1)} %get-tuple-element.217), channel_id=1, source_target_pairs={{0,4},{4,0},{8,12},{12,8},{16,20},{20,16},{24,28},{28,24},{1,5},{5... | collective-permute-start | bytes 1179656 | tf_op jit(solution)/shard_map/ppermute | solution.py:311
  436.2 31.3 %collective-permute-start.36 = (bf16[1,48,32,128]{3,2,1,0:T(8,128)(2,1)}, bf16[1,48,32,128]{3,2,1,0:T(8,128)(2,1)S(1)}, u32[]{:S(2)}, u32[]{:S(2)}) collective-permute-start(bf16[1,48,32,128]{3,2,1,0:T(8,128)(2,1)} %get-tuple-element.218), channel_id=1, source_target_pairs={{0,8},{4,12},{8,0},{12,4},{16,24},{20,28},{24,16},{28,20},{1,9},{5... | collective-permute-start | bytes 1179656 | tf_op jit(solution)/shard_map/ppermute | solution.py:311
  449.1 21.3 %collective-permute-start.49 = (bf16[1,48,32,128]{3,2,1,0:T(8,128)(2,1)}, bf16[1,48,32,128]{3,2,1,0:T(8,128)(2,1)S(1)}, u32[]{:S(2)}, u32[]{:S(2)}) collective-permute-start(bf16[1,48,32,128]{3,2,1,0:T(8,128)(2,1)} %get-tuple-element.233), channel_id=1, source_target_pairs={{0,4},{4,0},{8,12},{12,8},{16,20},{20,16},{24,28},{28,24},{1,5},{5... | collective-permute-start | bytes 1179656 | tf_op jit(solution)/shard_map/ppermute | solution.py:311
  457.2 22.2 %collective-permute-start.50 = (bf16[1,48,32,128]{3,2,1,0:T(8,128)(2,1)}, bf16[1,48,32,128]{3,2,1,0:T(8,128)(2,1)S(1)}, u32[]{:S(2)}, u32[]{:S(2)}) collective-permute-start(bf16[1,48,32,128]{3,2,1,0:T(8,128)(2,1)} %get-tuple-element.234), channel_id=1, source_target_pairs={{0,8},{4,12},{8,0},{12,4},{16,24},{20,28},{24,16},{28,20},{1,9},{5... | collective-permute-start | bytes 1179656 | tf_op jit(solution)/shard_map/ppermute | solution.py:311
  463.9 23.9 %collective-permute-start.51 = (bf16[1,48,32,128]{3,2,1,0:T(8,128)(2,1)}, bf16[1,48,32,128]{3,2,1,0:T(8,128)(2,1)S(1)}, u32[]{:S(2)}, u32[]{:S(2)}) collective-permute-start(bf16[1,48,32,128]{3,2,1,0:T(8,128)(2,1)} %get-tuple-element.235), channel_id=1, source_target_pairs={{0,12},{4,8},{8,4},{12,0},{16,28},{20,24},{24,20},{28,16},{1,13},{... | collective-permute-start | bytes 1179656 | tf_op jit(solution)/shard_map/ppermute | solution.py:311
  467.3 43.7 %collective-permute-start.52 = (bf16[1,48,32,128]{3,2,1,0:T(8,128)(2,1)}, bf16[1,48,32,128]{3,2,1,0:T(8,128)(2,1)S(1)}, u32[]{:S(2)}, u32[]{:S(2)}) collective-permute-start(bf16[1,48,32,128]{3,2,1,0:T(8,128)(2,1)} %get-tuple-element.236), channel_id=1, source_target_pairs={{0,16},{4,20},{8,24},{12,28},{16,0},{20,4},{24,8},{28,12},{1,17},{... | collective-permute-start | bytes 1179656 | tf_op jit(solution)/shard_map/ppermute | solution.py:311
  467.5 73.1 %collective-permute-start.53 = (bf16[1,48,32,128]{3,2,1,0:T(8,128)(2,1)}, bf16[1,48,32,128]{3,2,1,0:T(8,128)(2,1)S(1)}, u32[]{:S(2)}, u32[]{:S(2)}) collective-permute-start(bf16[1,48,32,128]{3,2,1,0:T(8,128)(2,1)} %get-tuple-element.237), channel_id=1, source_target_pairs={{0,20},{4,16},{8,28},{12,24},{16,4},{20,0},{24,12},{28,8},{1,21},{... | collective-permute-start | bytes 1179656 | tf_op jit(solution)/shard_map/ppermute | solution.py:311
  470.3 93.1 %collective-permute-start.54 = (bf16[1,48,32,128]{3,2,1,0:T(8,128)(2,1)}, bf16[1,48,32,128]{3,2,1,0:T(8,128)(2,1)}, u32[]{:S(2)}, u32[]{:S(2)}) collective-permute-start(bf16[1,48,32,128]{3,2,1,0:T(8,128)(2,1)} %get-tuple-element.238), channel_id=1, source_target_pairs={{0,24},{4,28},{8,16},{12,20},{16,8},{20,12},{24,0},{28,4},{1,25},{... | collective-permute-start | bytes 1179656 | tf_op jit(solution)/shard_map/ppermute | solution.py:311
  479.4 92.5 %collective-permute-start.55 = (bf16[1,48,32,128]{3,2,1,0:T(8,128)(2,1)}, bf16[1,48,32,128]{3,2,1,0:T(8,128)(2,1)}, u32[]{:S(2)}, u32[]{:S(2)}) collective-permute-start(bf16[1,48,32,128]{3,2,1,0:T(8,128)(2,1)} %get-tuple-element.239), channel_id=1, source_target_pairs={{0,28},{4,24},{8,20},{12,16},{16,12},{20,8},{24,4},{28,0},{1,29},{... | collective-permute-start | bytes 1179656 | tf_op jit(solution)/shard_map/ppermute | solution.py:311
  487.8 114.2 %collective-permute-start.37 = (bf16[1,48,32,128]{3,2,1,0:T(8,128)(2,1)}, bf16[1,48,32,128]{3,2,1,0:T(8,128)(2,1)S(1)}, u32[]{:S(2)}, u32[]{:S(2)}) collective-permute-start(bf16[1,48,32,128]{3,2,1,0:T(8,128)(2,1)} %get-tuple-element.219), channel_id=1, source_target_pairs={{0,12},{4,8},{8,4},{12,0},{16,28},{20,24},{24,20},{28,16},{1,13},{... | collective-permute-start | bytes 1179656 | tf_op jit(solution)/shard_map/ppermute | solution.py:311
  511.1 90.9 %collective-permute-start.38 = (bf16[1,48,32,128]{3,2,1,0:T(8,128)(2,1)}, bf16[1,48,32,128]{3,2,1,0:T(8,128)(2,1)S(1)}, u32[]{:S(2)}, u32[]{:S(2)}) collective-permute-start(bf16[1,48,32,128]{3,2,1,0:T(8,128)(2,1)} %get-tuple-element.220), channel_id=1, source_target_pairs={{0,16},{4,20},{8,24},{12,28},{16,0},{20,4},{24,8},{28,12},{1,17},{... | collective-permute-start | bytes 1179656 | tf_op jit(solution)/shard_map/ppermute | solution.py:311
  540.6 61.4 %collective-permute-start.39 = (bf16[1,48,32,128]{3,2,1,0:T(8,128)(2,1)}, bf16[1,48,32,128]{3,2,1,0:T(8,128)(2,1)}, u32[]{:S(2)}, u32[]{:S(2)}) collective-permute-start(bf16[1,48,32,128]{3,2,1,0:T(8,128)(2,1)} %get-tuple-element.221), channel_id=1, source_target_pairs={{0,20},{4,16},{8,28},{12,24},{16,4},{20,0},{24,12},{28,8},{1,21},{... | collective-permute-start | bytes 1179656 | tf_op jit(solution)/shard_map/ppermute | solution.py:311
  563.4 38.6 %collective-permute-start.40 = (bf16[1,48,32,128]{3,2,1,0:T(8,128)(2,1)}, bf16[1,48,32,128]{3,2,1,0:T(8,128)(2,1)}, u32[]{:S(2)}, u32[]{:S(2)}) collective-permute-start(bf16[1,48,32,128]{3,2,1,0:T(8,128)(2,1)} %get-tuple-element.222), channel_id=1, source_target_pairs={{0,24},{4,28},{8,16},{12,20},{16,8},{20,12},{24,0},{28,4},{1,25},{... | collective-permute-start | bytes 1179656 | tf_op jit(solution)/shard_map/ppermute | solution.py:311
  572.0 31.7 %collective-permute-start.41 = (bf16[1,48,32,128]{3,2,1,0:T(8,128)(2,1)}, bf16[1,48,32,128]{3,2,1,0:T(8,128)(2,1)}, u32[]{:S(2)}, u32[]{:S(2)}) collective-permute-start(bf16[1,48,32,128]{3,2,1,0:T(8,128)(2,1)} %get-tuple-element.223), channel_id=1, source_target_pairs={{0,28},{4,24},{8,20},{12,16},{16,12},{20,8},{24,4},{28,0},{1,29},{... | collective-permute-start | bytes 1179656 | tf_op jit(solution)/shard_map/ppermute | solution.py:311
  (58 other events, 3087.9 us)
Sparse Core Ops, SparseCore 0:
  198.1 34.4 all-reduce.2
  341.8 35.3 all-reduce.4
